TPU v7x, 128 devices: a whole 4x4x4 slice. The times are simulated.
128 devices in a mesh: row: 8 (over z, y_lo), col: 16 (over y_hi, x, core).
Axes of the slice: x: 4, y: 4 (y_hi: 2, y_lo: 2; y = y_hi * 2 + y_lo), z: 4, core: 2. Of those that a mesh axis runs over, the one named last changes fastest.
Arguments:
- tiles: bfloat16 [8, 16, 128, 128, 128], P('row', 'col'), may hold values from -2 to 2
- tile_src: int32 [8, 16, 128], P('row', 'col'), may hold values from 0 to 127
- tile_out: int32 [8, 16, 128], P('row', 'col'), may hold values from 0 to 255, as said below
- basis0: bfloat16 [262144, 256], P(('row', 'col')), may hold values from -40 to 40
Outputs:
- ortho_basis: float32 [262144, 256], P(('row', 'col'))
- gram_factor: float32 [256, 256], replicated
Inputs may be any that keep to these rules, and one draw needn't show every extreme that they name: `tile_out`: tile t of a device writes into a block owned by col index t // 8 of the same row: its value lies in (t // 8) * 16 to that plus 16 - 1.
All inputs are finite; a program needn't handle non-finite values.
Results may differ from a plain program's by a relative error of at most 0.0032.
Values may be sent and summed in bfloat16 or wider, within the bound.
No kernel may reach another device: no remote copies, remote signals or barrier semaphores. Data moves between devices by JAX's collectives and lax.ppermute only.
A program may use at most 192 MiB of HBM per device.

v0:
```python
import jax
import jax.numpy as jnp
from jax import lax
from jax.sharding import PartitionSpec as P

BLOCK = 128
BASIS = 256
BLOCKS_DEV = 16
PER_PEER = 8
ROWS_DEV = 2048


def local(tiles, tile_src, tile_out, basis0):
    row_width = lax.axis_size("row")
    col_width = lax.axis_size("col")
    item_count = ROWS_DEV * row_width * col_width
    tiles_here = tiles[0, 0]
    source_index = tile_src[0, 0]
    local_block = tile_out[0, 0] % BLOCKS_DEV
    picker = (
        local_block.reshape(col_width, PER_PEER)[:, :, None]
        == jnp.arange(BLOCKS_DEV, dtype=jnp.int32)[None, None, :]
    ).astype(jnp.bfloat16)
    column = lax.all_gather(basis0, "row", axis=0, tiled=True).reshape(-1, BLOCK, BASIS)
    sources = jnp.take(column, source_index, axis=0)
    products = jnp.einsum(
        "tij,tjk->tik", tiles_here, sources, preferred_element_type=jnp.float32
    ).astype(jnp.bfloat16)
    products = products.reshape(col_width, PER_PEER, BLOCK, BASIS)
    placed = jnp.einsum("pqb,pqik->pbik", picker, products, preferred_element_type=jnp.float32)
    summed = lax.psum_scatter(
        placed.reshape(ROWS_DEV * lax.axis_size("col"), BASIS),
        "col",
        scatter_dimension=0,
        tiled=True,
    )
    local_gram = lax.dot_general(
        summed, summed, (((0,), (0,)), ((), ())), precision=lax.Precision.HIGHEST
    )
    gram_total = lax.psum(local_gram, ("row", "col")) / item_count
    factor = jnp.linalg.cholesky(gram_total)
    orthonormal = lax.linalg.triangular_solve(
        factor, summed, left_side=False, lower=True, transpose_a=True
    )
    return (orthonormal, factor)


def solution(mesh):
    in_specs = (
        P("row", "col", None, None, None),
        P("row", "col", None),
        P("row", "col", None),
        P(("row", "col"), None),
    )
    out_specs = (P(("row", "col"), None), P())
    return jax.shard_map(local, mesh=mesh, in_specs=in_specs, out_specs=out_specs, check_vma=False)
```

profile of v0, /device:TPU:1, one launch (start us, length us, event | category | flops | bytes accessed | tf_op | source)
XLA Modules:
  0.0 734.1 jit_solution(14449603054402610528)
XLA Ops:
  7.2 0.7 all-gather.2.cloned.1.call-update
  7.9 0.5 broadcast.166
  8.5 1.3 reduce.15
  9.9 0.7 fusion.22
  10.5 0.7 compare_and_fusion
  11.2 170.0 %all-gather.2.cloned.1.call-done = bf16[16384,256]{1,0:T(8,128)(2,1)} async-done(((bf16[2048,256]{1,0:T(8,128)(2,1)}), bf16[16384,256]{1,0:T(8,128)(2,1)}) %all-gather.2.cloned.1.call-update) | async-done | bytes 8388624 | tf_op jit(solution)/shard_map/all_gather | solution.py:24
  181.2 9.9 %gather_fusion = bf16[128,128,256]{2,1,0:T(8,128)(2,1)} fusion(bf16[128,128,256]{2,1,0:T(8,128)(2,1)} %bitcast.55, s32[1024]{0:T(1024)S(1)} %pad_clamp_fusion), kind=kCustom, calls=%fused_computation | custom fusion | bytes 16777728 | tf_op jit(solution)/shard_map/jit(_take)/gather | solution.py:25
  191.2 11.8 %fusion.3 = bf16[128,256,128]{2,1,0:T(8,128)(2,1)} fusion(bf16[128,128,256]{2,1,0:T(8,128)(2,1)} %gather_fusion, pred[128]{0:T(512)(128)(4,1)S(1)} %compare_and_fusion, bf16[1,1,128,128,128]{4,3,2,1,0:T(8,128)(2,1)} %param.4), kind=kOutput, calls=%fused_computation.6 | convolution fusion | flops 1082130432 | bytes 20971648 | tf_op jit(solution)/shard_map/tij,tjk->tik/dot_general | solution.py:26
  202.9 12.6 %copy.11 = bf16[16,8,128,256]{3,1,2,0:T(8,128)(2,1)} copy(bf16[16,8,128,256]{2,3,1,0:T(8,128)(2,1)} %bitcast.54) | data formatting | bytes 16777216 | tf_op jit(solution)/shard_map/reshape | solution.py:29
  215.6 15.0 %fusion.18 = f32[16,16,128,256]{3,1,2,0:T(8,128)} fusion(bf16[16,8,128,256]{3,1,2,0:T(8,128)(2,1)} %copy.11, s32[16,8]{1,0:T(8,128)S(1)} %add_select_fusion), kind=kOutput, calls=%fused_computation.34 | convolution fusion | flops 134219776 | bytes 41943552 | tf_op jit(solution)/shard_map/pqb,pqik->pbik/dot_general | solution.py:30
  230.5 31.7 %copy.12 = f32[16,16,128,256]{3,2,1,0:T(8,128)} copy(f32[16,16,128,256]{3,1,2,0:T(8,128)} %fusion.18) | data formatting | bytes 67108864 | tf_op jit(solution)/shard_map/pqb,pqik->pbik/dot_general | solution.py:30
  262.5 246.0 %reduce-scatter.2.cloned.1.call-done = f32[2048,256]{1,0:T(8,128)} async-done(((f32[32768,256]{1,0:T(8,128)}), f32[2048,256]{1,0:T(8,128)}) %reduce-scatter.2.cloned.1.call-update) | async-done | bytes 2097168 | tf_op jit(solution)/shard_map/reduce_scatter | solution.py:31
  508.5 6.5 fusion.25
  515.1 144.1 %all-reduce.3.cloned.1.call-done = f32[256,256]{0,1:T(8,128)} async-done(((f32[256,256]{0,1:T(8,128)}), f32[256,256]{0,1:T(8,128)}) %all-reduce.3.cloned.1.call-update) | async-done | bytes 262160 | tf_op jit(solution)/shard_map/psum | solution.py:40
  659.2 1.0 broadcast_multiply_fusion
  660.3 1.0 fusion.10
  661.3 11.7 %cholesky.50 = f32[128,128]{1,0:T(8,128)S(1)} custom-call(f32[128,128]{1,0:T(8,128)S(1)} %cholesky.118), custom_call_target="Cholesky" | custom-call | tf_op jit(solution)/shard_map/jit(cholesky)/cholesky | solution.py:41
  673.1 9.8 %custom-call.14 = f32[1,128,128]{1,2,0:T(8,128)S(1)} custom-call(f32[1,128,128]{2,1,0:T(8,128)S(1)} %get-tuple-element.29), custom_call_target="InvertDiagBlocksLowerTriangular" | custom-call | tf_op jit(solution)/shard_map/jit(cholesky)/cholesky | solution.py:41
  683.1 0.3 convolution_subtract_fusion.1
  683.4 11.9 %cholesky.105 = f32[128,128]{1,0:T(8,128)S(1)} custom-call(f32[128,128]{1,0:T(8,128)S(1)} %convolution_subtract_fusion.1), custom_call_target="Cholesky" | custom-call | tf_op jit(solution)/shard_map/jit(cholesky)/cholesky | solution.py:41
  695.3 0.7 compare_reduce_fusion
  697.3 0.7 fusion.11
  698.1 3.9 while.1
  698.1 0.6 fusion.34
  698.7 1.3 bitcast_dynamic-update-slice_fusion.2
  700.0 0.6 fusion.34
  700.6 1.3 bitcast_dynamic-update-slice_fusion.2
  701.9 19.7 %custom-call.15 = f32[2,128,128]{1,2,0:T(8,128)S(1)} custom-call(f32[2,128,128]{2,1,0:T(8,128)S(1)} %get-tuple-element.9), custom_call_target="InvertDiagBlocksLowerTriangular" | custom-call | tf_op jit(solution)/shard_map/triangular_solve | solution.py:42
  721.6 1.1 fusion.8
  722.7 1.8 convolution_subtract_fusion
  724.6 1.1 fusion.12
  725.8 1.8 copy.15
  (22 shorter events, 1.1 us)
Async XLA Ops:
  7.2 174.0 %all-gather.2.cloned.1.call-start = ((), (), s32[]{:S(2)}) async-start(), calls=%async_computation.1 | async-start | bytes 9437184 | tf_op jit(solution)/shard_map/all_gather | solution.py:24
  7.9 500.6 %reduce-scatter.2.cloned.1.call-start = ((), (), s32[]{:S(2)}) async-start(), calls=%async_computation.2 | async-start | bytes 35651584 | tf_op jit(solution)/shard_map/reduce_scatter | solution.py:31
  262.3 396.9 %all-reduce.3.cloned.1.call-start = ((), (), s32[]{:S(2)}) async-start(), calls=%async_computation.3 | async-start | bytes 524288 | tf_op jit(solution)/shard_map/psum | solution.py:40
  508.5 213.1 %copy-start = (f32[2048,256]{1,0:T(8,128)S(1)}, f32[2048,256]{1,0:T(8,128)}, u32[]{:S(2)}) copy-start(f32[2048,256]{1,0:T(8,128)} %reduce-scatter.2.cloned.1.call-done) | copy-start | bytes 6291460
Sparse Core Ops, SparseCore 0:
  9.6 171.5 all-gather.1
  262.4 246.0 reduce-scatter.1
  515.2 143.9 all-reduce.2
where the time goes:
time: 735 us; the launch traced here: 734 us
  waiting for transfers between devices  561 us (76%)
  local copies, waits for them, and re-layouts  60.7 us (8%)
  other arithmetic  59.3 us (8%)
  matrix products  37.8 us (5%)
  between operations  15.1 us (2%)
    reduce_scatter x1, waiting for transfers between devices, local(): lax.psum_scatter(placed.reshape(ROWS_DEV * lax.axis_size('col'), BASIS),...  246 us
    all_gather x1, waiting for transfers between devices, local(): lax.all_gather(basis0, 'row', axis=0, tiled=True).reshape(-1, BLOCK, BASIS)  170 us
    psum x1, waiting for transfers between devices, local(): gram_total = lax.psum(local_gram, ('row', 'col')) / item_count  144 us
    another operation x6, other arithmetic, local(): factor = jnp.linalg.cholesky(gram_total)  34.2 us
    dot_general x1, local copies, waits for them, and re-layouts, local(): jnp.einsum('pqb,pqik->pbik', picker, products, preferred_element_type=jnp...  31.7 us
    another operation x4, other arithmetic, local(): lax.linalg.triangular_solve(factor, summed, left_side=False, lower=True,...  20.6 us
    dot_general x1, matrix products, local(): jnp.einsum('pqb,pqik->pbik', picker, products, preferred_element_type=jnp...  15 us
  transfers between devices with their start and end apart: 3, of which 3 were waited for; matrix products, arithmetic and copies ran while one was open for 0% of the time, Pallas kernels for 0%

commit v1 on v0

v1 whole, which is shorter than its diff:
```python
import jax
import jax.numpy as jnp
from jax import lax
from jax.experimental import pallas as pl
from jax.experimental.pallas import tpu as pltpu
from jax.sharding import PartitionSpec as P

BLOCK = 128
BASIS = 256
BLOCKS_DEV = 16
PER_PEER = 8
TILE_DEV = 128
ROWS_DEV = 2048
N_ROW = 8
N_COL = 16
ITEMS = 262144
BOTH = ("row", "col")


def device(z, y, x, core):
    z, y, x = z % 4, y % 4, x % 4
    return (z * 2 + y % 2) * N_COL + (y // 2 * 4 + x) * 2 + core


def shifted(value, dz=0, dy=0, dx=0, dcore=0):
    pairs = [
        (device(z, y, x, c), device(z + dz, y + dy, x + dx, (c + dcore) % 2))
        for z in range(4)
        for y in range(4)
        for x in range(4)
        for c in range(2)
    ]
    return lax.ppermute(value, BOTH, pairs)


def row_shifted(value, dz, flip):
    pairs = [(z * 2 + y, (z + dz) % 4 * 2 + (y ^ flip)) for z in range(4) for y in range(2)]
    return lax.ppermute(value, "row", pairs)


def gather_column(own):
    half = ROWS_DEV // 2
    below = row_shifted(own, 1, 0)
    above = row_shifted(own, -1, 0)
    beside = row_shifted(own, 0, 1)
    across_a = row_shifted(below[:half], 1, 0)
    across_b = row_shifted(above[half:], -1, 0)
    beside_above = row_shifted(above, 0, 1)
    beside_below = row_shifted(beside, 1, 0)
    beside_across = row_shifted(beside_above, -1, 0)
    return own, above, across_a, across_b, below, beside, beside_above, beside_across, beside_below


def product_kernel(src, tiles, *refs):
    parts, out, column, sems = refs[:9], refs[9], refs[10], refs[11]

    @pl.when(pl.program_id(0) == 0)
    def _():
        start = 0
        copies = []
        for i, part in enumerate(parts):
            rows = part.shape[0]
            copies.append(pltpu.make_async_copy(part, column.at[pl.ds(start, rows)], sems.at[i]))
            start += rows
        for copy in copies:
            copy.start()
        for copy in copies:
            copy.wait()

    for q in range(PER_PEER):
        place = src[pl.program_id(0) * PER_PEER + q]
        source = column[pl.ds(pl.multiple_of(place * BLOCK, BLOCK), BLOCK), :]
        product = jnp.dot(tiles[q], source, preferred_element_type=jnp.float32)
        out[pl.ds(q * BLOCK, BLOCK), :] = product.astype(jnp.bfloat16)


def make_products(src, tiles, parts):
    return pl.pallas_call(
        product_kernel,
        out_shape=jax.ShapeDtypeStruct((TILE_DEV * BLOCK, BASIS), jnp.bfloat16),
        grid_spec=pltpu.PrefetchScalarGridSpec(
            num_scalar_prefetch=1,
            grid=(N_COL,),
            in_specs=[pl.BlockSpec((PER_PEER, BLOCK, BLOCK), lambda p, src: (p, 0, 0))]
            + [pl.BlockSpec(memory_space=pl.ANY)] * 9,
            out_specs=pl.BlockSpec((PER_PEER * BLOCK, BASIS), lambda p, src: (p, 0)),
            scratch_shapes=[
                pltpu.VMEM((N_ROW * ROWS_DEV, BASIS), jnp.bfloat16),
                pltpu.SemaphoreType.DMA((9,)),
            ],
        ),
        compiler_params=pltpu.CompilerParams(vmem_limit_bytes=40 * 1024 * 1024),
        name="products",
    )(src, tiles, *parts)


def sum_kernel(place, products, summed, gram):
    p = pl.program_id(0)

    @pl.when(p == 0)
    def _():
        summed[...] = jnp.zeros_like(summed)

    for q in range(PER_PEER):
        rows = pl.ds(pl.multiple_of(place[p * PER_PEER + q] * BLOCK, BLOCK), BLOCK)
        summed[rows, :] += products[pl.ds(q * BLOCK, BLOCK), :].astype(jnp.float32)

    @pl.when(p == N_COL - 1)
    def _():
        def contract(a, b):
            return lax.dot_general(
                a,
                b,
                (((0,), (0,)), ((), ())),
                precision=lax.Precision.HIGHEST,
                preferred_element_type=jnp.float32,
            )

        left, right = summed[:, :BLOCK], summed[:, BLOCK:]
        gram[0:BLOCK, :] = contract(left, left)
        gram[BLOCK : 2 * BLOCK, :] = contract(left, right)
        gram[2 * BLOCK :, :] = contract(right, right)


def sum_and_gram(place, products):
    return pl.pallas_call(
        sum_kernel,
        out_shape=(
            jax.ShapeDtypeStruct((ROWS_DEV, BASIS), jnp.float32),
            jax.ShapeDtypeStruct((3 * BLOCK, BLOCK), jnp.float32),
        ),
        grid_spec=pltpu.PrefetchScalarGridSpec(
            num_scalar_prefetch=1,
            grid=(N_COL,),
            in_specs=[pl.BlockSpec((PER_PEER * BLOCK, BASIS), lambda p, place: (p, 0))],
            out_specs=(
                pl.BlockSpec((ROWS_DEV, BASIS), lambda p, place: (0, 0)),
                pl.BlockSpec((3 * BLOCK, BLOCK), lambda p, place: (0, 0)),
            ),
        ),
        compiler_params=pltpu.CompilerParams(vmem_limit_bytes=40 * 1024 * 1024),
        name="sum_and_gram",
    )(place, products)


def reduce_everywhere(gram):
    col = lax.axis_index("col")
    core, x = col % 2, col // 2 % 4
    rows = gram.shape[0] // 8

    def pick(parts, i):
        return lax.dynamic_index_in_dim(parts, i % parts.shape[0], 0, keepdims=False)

    halves = gram.reshape(2, 4 * rows, -1)
    part = pick(halves, core) + shifted(pick(halves, 1 - core), dcore=1)
    part = part.reshape(4, rows, -1)
    part = pick(part, x) + sum(shifted(pick(part, x + d), dx=d) for d in (1, 2, 3))
    part = part + sum(shifted(part, dy=d) for d in (1, 2, 3))
    part = part + sum(shifted(part, dz=d) for d in (1, 2, 3))
    parts = jnp.stack([part] + [shifted(part, dx=-d) for d in (1, 2, 3)])
    mine = jnp.concatenate([pick(parts, k - x) for k in range(4)])
    other = shifted(mine, dcore=1)
    return jnp.where(core == 0, jnp.concatenate([mine, other]), jnp.concatenate([other, mine]))


def local(tiles, tile_src, tile_out, basis0):
    row = lax.axis_index("row")
    places = lax.all_gather(tile_out[0, 0].reshape(N_COL, PER_PEER), "col", axis=0)
    place = lax.dynamic_index_in_dim(places, lax.axis_index("col"), 1, keepdims=False)
    place = (place % BLOCKS_DEV).reshape(-1)
    src = tile_src[0, 0]
    group = src // BLOCKS_DEV
    distance = (group // 2 - row // 2) % 4 + 4 * ((group + row) % 2)
    src = distance * BLOCKS_DEV + src % BLOCKS_DEV

    parts = gather_column(basis0)
    products = make_products(src, tiles[0, 0], parts)
    products = lax.all_to_all(
        products.reshape(N_COL, PER_PEER * BLOCK, BASIS), "col", 0, 0, tiled=True
    )
    summed, gram = sum_and_gram(place, products.reshape(-1, BASIS))
    gram = reduce_everywhere(gram) / ITEMS
    upper = gram[BLOCK : 2 * BLOCK]
    gram_total = jnp.concatenate(
        [
            jnp.concatenate([gram[:BLOCK], upper], axis=1),
            jnp.concatenate([upper.T, gram[2 * BLOCK :]], axis=1),
        ]
    )
    factor = jnp.linalg.cholesky(gram_total)
    orthonormal = lax.linalg.triangular_solve(
        factor, summed, left_side=False, lower=True, transpose_a=True
    )
    return (orthonormal, factor)


def solution(mesh):
    in_specs = (
        P("row", "col", None, None, None),
        P("row", "col", None),
        P("row", "col", None),
        P(("row", "col"), None),
    )
    out_specs = (P(("row", "col"), None), P())
    return jax.shard_map(local, mesh=mesh, in_specs=in_specs, out_specs=out_specs, check_vma=False)
```

time: 735 us -> 353 us (0.48)
  waiting for transfers between devices: 561 us -> 85.3 us
  blocking collectives: 0 us -> 125 us
  local copies, waits for them, and re-layouts: 60.7 us -> 11.8 us
  starting transfers between devices: 0.3 us -> 41.8 us
  matrix products: 37.8 us -> 4.46 us
  Pallas kernels: 0 us -> 25.4 us
  between operations: 15.1 us -> 2.26 us
    reduce_scatter x1 -> x0, waiting for transfers between devices: 246 us -> none  [local(): lax.psum_scatter(placed.reshape(ROWS_DEV * lax.axis_size('col'), BASIS),...]
    all_gather x1 -> x0, waiting for transfers between devices: 170 us -> none  [local(): lax.all_gather(basis0, 'row', axis=0, tiled=True).reshape(-1, BLOCK, BASIS)]
    psum x1 -> x0, waiting for transfers between devices: 144 us -> none  [local(): gram_total = lax.psum(local_gram, ('row', 'col')) / item_count]
    all_gather x0 -> x1, blocking collectives: none -> 125 us  [local(): lax.all_gather(tile_out[0, 0].reshape(N_COL, PER_PEER), 'col', axis=0)]
    ppermute x0 -> x22, waiting for transfers between devices: none -> 85.3 us  [the longest x8 71.6 us: row_shifted(): return lax.ppermute(value, 'row', pairs)]
    dot_general x3 -> x0, matrix products: 33.3 us -> none  [the longest x1 15 us: local(): jnp.einsum('pqb,pqik->pbik', picker, products, preferred_element_type=jnp...]
    ppermute x0 -> x22, starting transfers between devices: none -> 32.7 us  [the longest x14 19 us: shifted(): return lax.ppermute(value, BOTH, pairs)]
    dot_general x1 -> x0, local copies, waits for them, and re-layouts: 31.7 us -> none  [local(): jnp.einsum('pqb,pqik->pbik', picker, products, preferred_element_type=jnp...]
  transfers between devices with their start and end apart: 3 -> 23, of which waited for: 3 -> 16; matrix products, arithmetic and copies ran while one was open for 0% -> 1% of each run, Pallas kernels for 0% -> 0%
where the time goes in v1:
time: 353 us; the launch traced here: 352 us
  blocking collectives  125 us (35%)
  waiting for transfers between devices  85.3 us (24%)
  other arithmetic  55.5 us (16%)
  starting transfers between devices  41.8 us (12%)
  Pallas kernels  25.4 us (7%)
  local copies, waits for them, and re-layouts  11.8 us (3%)
  matrix products  4.46 us (1%)
    all_gather x1, blocking collectives, local(): lax.all_gather(tile_out[0, 0].reshape(N_COL, PER_PEER), 'col', axis=0)  125 us
    ppermute x8, waiting for transfers between devices, row_shifted(): return lax.ppermute(value, 'row', pairs)  71.6 us
    another operation x6, other arithmetic, local(): factor = jnp.linalg.cholesky(gram_total)  33.9 us
    another operation x4, other arithmetic, local(): lax.linalg.triangular_solve(factor, summed, left_side=False, lower=True,...  20.6 us
    ppermute x14, starting transfers between devices, shifted(): return lax.ppermute(value, BOTH, pairs)  19 us
    ppermute x8, starting transfers between devices, row_shifted(): return lax.ppermute(value, 'row', pairs)  13.8 us
    ppermute x14, waiting for transfers between devices, shifted(): return lax.ppermute(value, BOTH, pairs)  13.7 us
    pallas_call x1, Pallas kernels, sum_and_gram(): pl.pallas_call(sum_kernel, out_shape=(jax.ShapeDtypeStruct((ROWS_DEV, BAS...  13.1 us
  transfers between devices with their start and end apart: 23, of which 16 were waited for; matrix products, arithmetic and copies ran while one was open for 1% of the time, Pallas kernels for 0%

profile of v1, /device:TPU:1, one launch (start us, length us, event | category | flops | bytes accessed | tf_op | source)
XLA Modules:
  0.0 352.1 jit_solution(5720611292809427713)
XLA Ops:
  0.6 4.7 %collective-permute-start = (bf16[2048,256]{1,0:T(8,128)(2,1)}, bf16[2048,256]{1,0:T(8,128)(2,1)S(1)}, u32[]{:S(2)}, u32[]{:S(2)}) collective-permute-start(bf16[2048,256]{1,0:T(8,128)(2,1)} %refs_0_.1), channel_id=1, source_target_pairs={{0,96},{16,112},{32,0},{48,16},{64,32},{80,48},{96,64},{112,80},{1... | collective-permute-start | bytes 3145736 | tf_op jit(solution)/shard_map/ppermute | solution.py:38
  5.3 1.3 collective-permute-start.4
  6.6 20.8 %collective-permute-done.refs_1_ = bf16[2048,256]{1,0:T(8,128)(2,1)S(1)} collective-permute-done((bf16[2048,256]{1,0:T(8,128)(2,1)}, bf16[2048,256]{1,0:T(8,128)(2,1)S(1)}, u32[]{:S(2)}, u32[]{:S(2)}) %collective-permute-start) | collective-permute-done | bytes 1048608 | tf_op jit(solution)/shard_map/ppermute | solution.py:38
  27.4 1.3 collective-permute-start.5
  30.5 21.3 %collective-permute-done.5.refs_6_ = bf16[2048,256]{1,0:T(8,128)(2,1)} collective-permute-done((bf16[2048,256]{1,0:T(8,128)(2,1)S(1)}, bf16[2048,256]{1,0:T(8,128)(2,1)}, u32[]{:S(2)}, u32[]{:S(2)}) %collective-permute-start.5) | collective-permute-done | bytes 1048608 | tf_op jit(solution)/shard_map/ppermute | solution.py:38
  51.7 2.2 collective-permute-start.6
  55.6 2.7 collective-permute-start.3
  58.3 29.4 %collective-permute-done.2.refs_2_ = bf16[1024,256]{1,0:T(8,128)(2,1)} collective-permute-done((bf16[1024,256]{1,0:T(8,128)(2,1)}, bf16[1024,256]{1,0:T(8,128)(2,1)}, u32[]{:S(2)}, u32[]{:S(2)}) %collective-permute-start.2) | collective-permute-done | bytes 524320 | tf_op jit(solution)/shard_map/ppermute | solution.py:38
  87.8 2.2 copy-done
  89.9 12.4 %products.1 = bf16[16384,256]{1,0:T(8,128)(2,1)} custom-call(s32[128]{0:T(128)S(1)} %fusion.10.src, bf16[128,128,128]{2,1,0:T(8,128)(2,1)S(1)} %bitcast.71, bf16[2048,256]{1,0:T(8,128)(2,1)S(1)} %copy-done.1, bf16[2048,256]{1,0:T(8,128)(2,1)S(1)} %collective-permute-done.refs_1_, bf16[1024,256]{1,0:T(8,128)(2,1)} %collective-permute-done.2.refs_2_, ...), custom_call_target="tpu_custom_call" | custom-call | tf_op jit(solution)/shard_map/products/pallas_call | solution.py:78
  102.3 9.1 %all-to-all-start = ((bf16[16,1024,256]{2,1,0:T(8,128)(2,1)}), bf16[16,1024,256]{2,1,0:T(8,128)(2,1)}, u32[]{:S(2)}, u32[]{:S(2)}) async-start(bf16[16,1024,256]{2,1,0:T(8,128)(2,1)} %bitcast.74), calls=%async_computation | async-start | bytes 16777216 | tf_op jit(solution)/shard_map/all_to_all | solution.py:178
  112.8 125.5 %all_gather.3 = s32[16,16,8]{1,2,0:T(8,128)S(1)} all-gather(s32[1,16,8]{1,2,0:T(8,128)S(1)} %copy.19), channel_id=1, replica_groups=mesh['row'=8,'col'=16] {'col'}, dimensions={0}, use_global_device_ids=true | all-gather | bytes 8704 | tf_op jit(solution)/shard_map/all_gather | solution.py:168
  238.8 13.1 %sum_and_gram.1 = (f32[2048,256]{1,0:T(8,128)S(1)}, f32[384,128]{1,0:T(8,128)S(1)}) custom-call(s32[128]{0:T(128)S(1)} %and_select_fusion.5.place, bf16[16384,256]{1,0:T(8,128)(2,1)} %bitcast.3.products), custom_call_target="tpu_custom_call" | custom-call | tf_op jit(solution)/shard_map/sum_and_gram/pallas_call | solution.py:126
  253.4 1.5 collective-permute-start.9
  257.3 1.7 collective-permute-done.10
  259.0 1.7 collective-permute-start.14
  260.8 2.2 collective-permute-start.13
  262.9 1.7 collective-permute-done.12
  265.0 3.0 collective-permute-start.17
  269.2 2.6 collective-permute-done.15
  272.2 2.5 collective-permute-start.19
  274.9 1.5 collective-permute-done.20
  278.0 6.2 %collective-permute-start.21 = (f32[192,128]{0,1:T(8,128)S(1)}, f32[192,128]{0,1:T(8,128)S(1)}, u32[]{:S(2)}, u32[]{:S(2)}) collective-permute-start(f32[192,128]{0,1:T(8,128)S(1)} %pad_maximum_fusion.1), channel_id=1, source_target_pairs={{0,1},{1,0},{2,3},{3,2},{4,5},{5,4},{6,7},{7,6},{16,17},{17,16},{1... | collective-permute-start | bytes 294920 | tf_op jit(solution)/shard_map/ppermute | solution.py:33
  285.9 11.7 %cholesky.50 = f32[128,128]{1,0:T(8,128)S(1)} custom-call(f32[128,128]{1,0:T(8,128)S(1)} %cholesky.118), custom_call_target="Cholesky" | custom-call | tf_op jit(solution)/shard_map/jit(cholesky)/cholesky | solution.py:190
  297.7 9.8 %custom-call.14 = f32[1,128,128]{1,2,0:T(8,128)S(1)} custom-call(f32[1,128,128]{2,1,0:T(8,128)S(1)} %get-tuple-element.48), custom_call_target="InvertDiagBlocksLowerTriangular" | custom-call | tf_op jit(solution)/shard_map/jit(cholesky)/cholesky | solution.py:190
  308.0 11.7 %cholesky.105 = f32[128,128]{1,0:T(8,128)S(1)} custom-call(f32[128,128]{1,0:T(8,128)S(1)} %convolution_subtract_fusion.1), custom_call_target="Cholesky" | custom-call | tf_op jit(solution)/shard_map/jit(cholesky)/cholesky | solution.py:190
  322.5 3.9 %while.1 = (s32[]{:T(128)}, f32[256,256]{1,0:T(8,128)S(1)}, s32[2,2]{1,0:T(2,128)S(1)}, f32[2,128,128]{2,1,0:T(8,128)S(1)}, s32[]{:T(128)}) while((s32[]{:T(128)}, f32[256,256]{1,0:T(8,128)S(1)}, s32[2,2]{1,0:T(2,128)S(1)}, f32[2,128,128]{2,1,0:T(8,128)S(1)}, s32[]{:T(128)}) %tuple.40), condition=%wide.while_cond, body=%wide.while_body.sunk | while | flops 2 | bytes 131189 | solution.py:191
  323.1 1.4 bitcast_dynamic-update-slice_fusion.2
  325.1 1.4 bitcast_dynamic-update-slice_fusion.2
  326.4 19.7 %custom-call.15 = f32[2,128,128]{1,2,0:T(8,128)S(1)} custom-call(f32[2,128,128]{2,1,0:T(8,128)S(1)} %get-tuple-element.13), custom_call_target="InvertDiagBlocksLowerTriangular" | custom-call | tf_op jit(solution)/shard_map/triangular_solve | solution.py:191
  347.2 1.8 convolution_subtract_fusion
  350.3 1.8 copy.26
  (83 shorter events, 20.1 us)
Async XLA Ops:
  0.6 87.1 %copy-start.1 = (bf16[2048,256]{1,0:T(8,128)(2,1)S(1)}, bf16[2048,256]{1,0:T(8,128)(2,1)}, u32[]{:S(2)}) copy-start(bf16[2048,256]{1,0:T(8,128)(2,1)} %refs_0_.1) | copy-start | bytes 3145732
  0.6 57.7 %copy-start.2 = (s32[1,1,128]{2,1,0:T(1,128)S(1)}, s32[1,1,128]{2,1,0:T(1,128)}, u32[]{:S(2)}) copy-start(s32[1,1,128]{2,1,0:T(1,128)} %param.5) | copy-start | bytes 1540
  0.6 26.8 %collective-permute-start = (bf16[2048,256]{1,0:T(8,128)(2,1)}, bf16[2048,256]{1,0:T(8,128)(2,1)S(1)}, u32[]{:S(2)}, u32[]{:S(2)}) collective-permute-start(bf16[2048,256]{1,0:T(8,128)(2,1)} %refs_0_.1), channel_id=1, source_target_pairs={{0,96},{16,112},{32,0},{48,16},{64,32},{80,48},{96,64},{112,80},{1... | collective-permute-start | bytes 3145736 | tf_op jit(solution)/shard_map/ppermute | solution.py:38
  5.3 24.0 %collective-permute-start.4 = (bf16[2048,256]{1,0:T(8,128)(2,1)}, bf16[2048,256]{1,0:T(8,128)(2,1)}, u32[]{:S(2)}, u32[]{:S(2)}) collective-permute-start(bf16[2048,256]{1,0:T(8,128)(2,1)} %refs_0_.1), channel_id=1, source_target_pairs={{0,16},{16,0},{32,48},{48,32},{64,80},{80,64},{96,112},{112,96},{1... | collective-permute-start | bytes 3145736 | tf_op jit(solution)/shard_map/ppermute | solution.py:38
  27.4 24.3 %collective-permute-start.5 = (bf16[2048,256]{1,0:T(8,128)(2,1)S(1)}, bf16[2048,256]{1,0:T(8,128)(2,1)}, u32[]{:S(2)}, u32[]{:S(2)}) collective-permute-start(bf16[2048,256]{1,0:T(8,128)(2,1)S(1)} %collective-permute-done.refs_1_), channel_id=1, source_target_pairs={{0,16},{16,0},{32,48},{48,32},{64,80},{80,64},{96,112},{112,96},{1... | collective-permute-start | bytes 3145736 | tf_op jit(solution)/shard_map/ppermute | solution.py:38
  28.7 25.2 %collective-permute-start.1 = (bf16[2048,256]{1,0:T(8,128)(2,1)}, bf16[2048,256]{1,0:T(8,128)(2,1)S(1)}, u32[]{:S(2)}, u32[]{:S(2)}) collective-permute-start(bf16[2048,256]{1,0:T(8,128)(2,1)} %refs_0_.1), channel_id=1, source_target_pairs={{0,32},{16,48},{32,64},{48,80},{64,96},{80,112},{96,0},{112,16},{1... | collective-permute-start | bytes 3145736 | tf_op jit(solution)/shard_map/ppermute | solution.py:38
  29.3 58.4 %collective-permute-start.7 = (bf16[2048,256]{1,0:T(8,128)(2,1)}, bf16[2048,256]{1,0:T(8,128)(2,1)}, u32[]{:S(2)}, u32[]{:S(2)}) collective-permute-start(bf16[2048,256]{1,0:T(8,128)(2,1)} %collective-permute-done.4.refs_5_), channel_id=1, source_target_pairs={{0,32},{16,48},{32,64},{48,80},{64,96},{80,112},{96,0},{112,16},{1... | collective-permute-start | bytes 3145736 | tf_op jit(solution)/shard_map/ppermute | solution.py:38
  51.7 36.0 %collective-permute-start.6 = (bf16[2048,256]{1,0:T(8,128)(2,1)}, bf16[2048,256]{1,0:T(8,128)(2,1)}, u32[]{:S(2)}, u32[]{:S(2)}) collective-permute-start(bf16[2048,256]{1,0:T(8,128)(2,1)} %collective-permute-done.5.refs_6_), channel_id=1, source_target_pairs={{0,96},{16,112},{32,0},{48,16},{64,32},{80,48},{96,64},{112,80},{1... | collective-permute-start | bytes 3145736 | tf_op jit(solution)/shard_map/ppermute | solution.py:38
  54.8 32.9 %collective-permute-start.2 = (bf16[1024,256]{1,0:T(8,128)(2,1)}, bf16[1024,256]{1,0:T(8,128)(2,1)}, u32[]{:S(2)}, u32[]{:S(2)}) collective-permute-start(bf16[1024,256]{1,0:T(8,128)(2,1)} %slice.73), channel_id=1, source_target_pairs={{0,32},{16,48},{32,64},{48,80},{64,96},{80,112},{96,0},{112,16},{1... | collective-permute-start | bytes 1572872 | tf_op jit(solution)/shard_map/ppermute | solution.py:38
  55.6 32.1 %collective-permute-start.3 = (bf16[1024,256]{1,0:T(8,128)(2,1)}, bf16[1024,256]{1,0:T(8,128)(2,1)}, u32[]{:S(2)}, u32[]{:S(2)}) collective-permute-start(bf16[1024,256]{1,0:T(8,128)(2,1)} %slice.74), channel_id=1, source_target_pairs={{0,96},{16,112},{32,0},{48,16},{64,32},{80,48},{96,64},{112,80},{1... | collective-permute-start | bytes 1572872 | tf_op jit(solution)/shard_map/ppermute | solution.py:38
  87.7 2.2 copy-start
  102.3 9.7 %copy-start.3 = (s32[1,1,128]{2,1,0:T(1,128)S(1)}, s32[1,1,128]{2,1,0:T(1,128)}, u32[]{:S(2)}) copy-start(s32[1,1,128]{2,1,0:T(1,128)} %param.6) | copy-start | bytes 1540
  102.3 136.4 %all-to-all-start = ((bf16[16,1024,256]{2,1,0:T(8,128)(2,1)}), bf16[16,1024,256]{2,1,0:T(8,128)(2,1)}, u32[]{:S(2)}, u32[]{:S(2)}) async-start(bf16[16,1024,256]{2,1,0:T(8,128)(2,1)} %bitcast.74), calls=%async_computation | async-start | bytes 16777216 | tf_op jit(solution)/shard_map/all_to_all | solution.py:178
  251.9 1.4 collective-permute-start.8
  253.3 2.7 collective-permute-start.11
  253.4 4.0 %collective-permute-start.9 = (f32[48,128]{1,0:T(8,128)S(1)}, f32[48,128]{1,0:T(8,128)S(1)}, u32[]{:S(2)}, u32[]{:S(2)}) collective-permute-start(f32[48,128]{1,0:T(8,128)S(1)} %get-tuple-element.44), channel_id=1, source_target_pairs={{0,2},{1,3},{2,4},{3,5},{4,6},{5,7},{6,0},{7,1},{16,18},{17,19},{1... | collective-permute-start | bytes 73736 | tf_op jit(solution)/shard_map/ppermute | solution.py:33
  254.8 4.2 %collective-permute-start.10 = (f32[48,128]{1,0:T(8,128)S(1)}, f32[48,128]{1,0:T(8,128)S(1)}, u32[]{:S(2)}, u32[]{:S(2)}) collective-permute-start(f32[48,128]{1,0:T(8,128)S(1)} %get-tuple-element.42), channel_id=1, source_target_pairs={{0,4},{1,5},{2,6},{3,7},{4,0},{5,1},{6,2},{7,3},{16,20},{17,21},{1... | collective-permute-start | bytes 73736 | tf_op jit(solution)/shard_map/ppermute | solution.py:33
  259.0 3.9 %collective-permute-start.14 = (f32[48,128]{1,0:T(8,128)S(1)}, f32[48,128]{1,0:T(8,128)S(1)}, u32[]{:S(2)}, u32[]{:S(2)}) collective-permute-start(f32[48,128]{1,0:T(8,128)S(1)} %bitcast_add_fusion.2), channel_id=1, source_target_pairs={{0,24},{1,25},{2,26},{3,27},{4,28},{5,29},{6,30},{7,31},{16,0},{17... | collective-permute-start | bytes 73736 | tf_op jit(solution)/shard_map/ppermute | solution.py:33
  260.8 3.9 %collective-permute-start.12 = (f32[48,128]{1,0:T(8,128)S(1)}, f32[48,128]{1,0:T(8,128)S(1)}, u32[]{:S(2)}, u32[]{:S(2)}) collective-permute-start(f32[48,128]{1,0:T(8,128)S(1)} %bitcast_add_fusion.2), channel_id=1, source_target_pairs={{0,16},{1,17},{2,18},{3,19},{4,20},{5,21},{6,22},{7,23},{16,8},{17... | collective-permute-start | bytes 73736 | tf_op jit(solution)/shard_map/ppermute | solution.py:33
  260.8 4.2 %collective-permute-start.13 = (f32[48,128]{1,0:T(8,128)S(1)}, f32[48,128]{1,0:T(8,128)S(1)}, u32[]{:S(2)}, u32[]{:S(2)}) collective-permute-start(f32[48,128]{1,0:T(8,128)S(1)} %bitcast_add_fusion.2), channel_id=1, source_target_pairs={{0,8},{1,9},{2,10},{3,11},{4,12},{5,13},{6,14},{7,15},{16,24},{17,... | collective-permute-start | bytes 73736 | tf_op jit(solution)/shard_map/ppermute | solution.py:33
  265.0 4.3 %collective-permute-start.17 = (f32[48,128]{1,0:T(8,128)S(1)}, f32[48,128]{1,0:T(8,128)S(1)}, u32[]{:S(2)}, u32[]{:S(2)}) collective-permute-start(f32[48,128]{1,0:T(8,128)S(1)} %add_add_fusion.1), channel_id=1, source_target_pairs={{0,96},{1,97},{2,98},{3,99},{4,100},{5,101},{6,102},{7,103},{16,11... | collective-permute-start | bytes 73736 | tf_op jit(solution)/shard_map/ppermute | solution.py:33
  268.0 3.9 %collective-permute-start.15 = (f32[48,128]{1,0:T(8,128)S(1)}, f32[48,128]{1,0:T(8,128)S(1)}, u32[]{:S(2)}, u32[]{:S(2)}) collective-permute-start(f32[48,128]{1,0:T(8,128)S(1)} %add_add_fusion.1), channel_id=1, source_target_pairs={{0,32},{1,33},{2,34},{3,35},{4,36},{5,37},{6,38},{7,39},{16,48},{1... | collective-permute-start | bytes 73736 | tf_op jit(solution)/shard_map/ppermute | solution.py:33
  268.0 4.2 %collective-permute-start.16 = (f32[48,128]{1,0:T(8,128)S(1)}, f32[48,128]{1,0:T(8,128)S(1)}, u32[]{:S(2)}, u32[]{:S(2)}) collective-permute-start(f32[48,128]{1,0:T(8,128)S(1)} %add_add_fusion.1), channel_id=1, source_target_pairs={{0,64},{1,65},{2,66},{3,67},{4,68},{5,69},{6,70},{7,71},{16,80},{1... | collective-permute-start | bytes 73736 | tf_op jit(solution)/shard_map/ppermute | solution.py:33
  272.2 4.3 %collective-permute-start.20 = (f32[48,128]{1,0:T(8,128)S(1)}, f32[48,128]{1,0:T(8,128)S(1)}, u32[]{:S(2)}, u32[]{:S(2)}) collective-permute-start(f32[48,128]{1,0:T(8,128)S(1)} %add_add_fusion), channel_id=1, source_target_pairs={{0,2},{1,3},{2,4},{3,5},{4,6},{5,7},{6,0},{7,1},{16,18},{17,19},{1... | collective-permute-start | bytes 73736 | tf_op jit(solution)/shard_map/ppermute | solution.py:33
  272.2 4.3 %collective-permute-start.19 = (f32[48,128]{1,0:T(8,128)S(1)}, f32[48,128]{1,0:T(8,128)S(1)}, u32[]{:S(2)}, u32[]{:S(2)}) collective-permute-start(f32[48,128]{1,0:T(8,128)S(1)} %add_add_fusion), channel_id=1, source_target_pairs={{0,4},{1,5},{2,6},{3,7},{4,0},{5,1},{6,2},{7,3},{16,20},{17,21},{1... | collective-permute-start | bytes 73736 | tf_op jit(solution)/shard_map/ppermute | solution.py:33
  274.7 2.7 collective-permute-start.18
  278.0 7.2 %collective-permute-start.21 = (f32[192,128]{0,1:T(8,128)S(1)}, f32[192,128]{0,1:T(8,128)S(1)}, u32[]{:S(2)}, u32[]{:S(2)}) collective-permute-start(f32[192,128]{0,1:T(8,128)S(1)} %pad_maximum_fusion.1), channel_id=1, source_target_pairs={{0,1},{1,0},{2,3},{3,2},{4,5},{5,4},{6,7},{7,6},{16,17},{17,16},{1... | collective-permute-start | bytes 294920 | tf_op jit(solution)/shard_map/ppermute | solution.py:33

commit v2 on v0

v2 whole, which is shorter than its diff:
```python
import jax
import jax.numpy as jnp
from jax import lax
from jax.experimental import pallas as pl
from jax.experimental.pallas import tpu as pltpu
from jax.sharding import PartitionSpec as P

BLOCK = 128
BASIS = 256
BLOCKS_DEV = 16
PER_PEER = 8
TILE_DEV = 128
ROWS_DEV = 2048
N_ROW = 8
N_COL = 16
ITEMS = 262144
BOTH = ("row", "col")
CUTS = (688, 1376)
PARTS = 10
PANEL = 16
PIECE = 48
CHUNKS = 16
OUT_CHUNKS = 8


def device(z, y, x, core):
    z, y, x = z % 4, y % 4, x % 4
    return (z * 2 + y % 2) * N_COL + (y // 2 * 4 + x) * 2 + core


def shifted(value, dz=0, dy=0, dx=0, dcore=0):
    pairs = [
        (device(z, y, x, c), device(z + dz, y + dy, x + dx, (c + dcore) % 2))
        for z in range(4)
        for y in range(4)
        for x in range(4)
        for c in range(2)
    ]
    return lax.ppermute(value, BOTH, pairs)


def row_shifted(value, dz, flip):
    pairs = [(z * 2 + y, (z + dz) % 4 * 2 + (y ^ flip)) for z in range(4) for y in range(2)]
    return lax.ppermute(value, "row", pairs)


def together(*values):
    return lax.optimization_barrier(values)


def gather_column(own, place):
    below = row_shifted(own, 1, 0)
    above = row_shifted(own, -1, 0)
    beside = row_shifted(own, 0, 1)
    below, above, beside, place = together(below, above, beside, place)
    across = row_shifted(above, -1, 0)
    beside_above = row_shifted(above, 0, 1)
    beside_below = row_shifted(beside, 1, 0)
    place = lax.all_to_all(place.reshape(N_COL, PER_PEER), "col", 0, 0, tiled=True).reshape(-1)
    across, beside_above, beside_below, place = together(across, beside_above, beside_below, place)
    first, second = CUTS
    last = (
        row_shifted(beside_below[:first], 1, 0),
        row_shifted(beside_above[first:second], -1, 0),
        row_shifted(across[second:], 0, 1),
    )
    return (own, above, across, below, beside, beside_above, *last, beside_below), place


def split(value):
    high = value.astype(jnp.bfloat16)
    rest = value - high.astype(jnp.float32)
    middle = rest.astype(jnp.bfloat16)
    low = (rest - middle.astype(jnp.float32)).astype(jnp.bfloat16)
    return high, middle, low


def product_kernel(src, tiles_hbm, *refs):
    parts = refs[:PARTS]
    out_hbm, tiles, column, out, tile_sems, part_sems, out_sems = refs[PARTS:]
    loads = []
    start = 0
    for i, part in enumerate(parts):
        rows = part.shape[0]
        loads.append(pltpu.make_async_copy(part, column.at[pl.ds(start, rows)], part_sems.at[i]))
        start += rows
    share = TILE_DEV // CHUNKS
    tile_loads = []
    for g in range(CHUNKS):
        here = pl.ds(g * share, share)
        tile_loads.append(pltpu.make_async_copy(tiles_hbm.at[here], tiles.at[here], tile_sems.at[g]))
    for load in loads + tile_loads:
        load.start()
    for load in loads:
        load.wait()
    stores = []
    for g in range(CHUNKS):
        tile_loads[g].wait()

        @pl.loop(g * share, (g + 1) * share, unroll=8)
        def _(t):
            source = column[pl.ds(pl.multiple_of(src[t] * BLOCK, BLOCK), BLOCK), :]
            product = jnp.dot(tiles[t], source, preferred_element_type=jnp.float32)
            out[pl.ds(pl.multiple_of(t * BLOCK, BLOCK), BLOCK), :] = product.astype(jnp.bfloat16)

        here = pl.ds(g * share * BLOCK, share * BLOCK)
        store = pltpu.make_async_copy(out.at[here], out_hbm.at[here], out_sems.at[g])
        store.start()
        stores.append(store)
    for store in stores:
        store.wait()


def make_products(src, tiles, parts):
    return pl.pallas_call(
        product_kernel,
        out_shape=jax.ShapeDtypeStruct((TILE_DEV * BLOCK, BASIS), jnp.bfloat16),
        in_specs=[pl.BlockSpec(memory_space=pltpu.SMEM)]
        + [pl.BlockSpec(memory_space=pltpu.HBM)] * (1 + PARTS),
        out_specs=pl.BlockSpec(memory_space=pltpu.HBM),
        scratch_shapes=[
            pltpu.VMEM((TILE_DEV, BLOCK, BLOCK), jnp.bfloat16),
            pltpu.VMEM((N_ROW * ROWS_DEV, BASIS), jnp.bfloat16),
            pltpu.VMEM((TILE_DEV * BLOCK, BASIS), jnp.bfloat16),
            pltpu.SemaphoreType.DMA((CHUNKS,)),
            pltpu.SemaphoreType.DMA((PARTS,)),
            pltpu.SemaphoreType.DMA((CHUNKS,)),
        ],
        compiler_params=pltpu.CompilerParams(vmem_limit_bytes=48 * 1024 * 1024),
        name="products",
    )(src, tiles, *parts)


def sum_kernel(place, me, products_hbm, summed_hbm, gram, products, summed, packed, in_sems, out_sem):
    share = TILE_DEV // CHUNKS
    loads = []
    for g in range(CHUNKS):
        here = pl.ds(g * share * BLOCK, share * BLOCK)
        loads.append(pltpu.make_async_copy(products_hbm.at[here], products.at[here], in_sems.at[g]))
    for load in loads:
        load.start()
    summed[...] = jnp.zeros_like(summed)
    for g in range(CHUNKS):
        loads[g].wait()

        @pl.loop(g * share, (g + 1) * share, unroll=4)
        def _(t):
            rows = pl.ds(pl.multiple_of(place[t] * BLOCK, BLOCK), BLOCK)
            product = products[pl.ds(pl.multiple_of(t * BLOCK, BLOCK), BLOCK), :]
            summed[rows, :] += product.astype(jnp.float32)

    store = pltpu.make_async_copy(summed, summed_hbm, out_sem)
    store.start()

    def contract(a, b):
        return lax.dot_general(
            a, b, (((0,), (0,)), ((), ())), preferred_element_type=jnp.float32
        )

    high, middle, low = split(summed[...])
    mixed = contract(high, middle) + contract(high, low)
    total = contract(high, high) + contract(middle, middle) + mixed + mixed.T
    packed[:BLOCK, :] = total[:BLOCK, :BLOCK]
    packed[BLOCK : 2 * BLOCK, :] = total[:BLOCK, BLOCK:]
    packed[2 * BLOCK :, :] = total[BLOCK:, BLOCK:]
    for i, order in enumerate(piece_order(me)):
        gram[order] = packed[i * PIECE : (i + 1) * PIECE, :]
    store.wait()


def sum_and_gram(place, me, products):
    return pl.pallas_call(
        sum_kernel,
        out_shape=(
            jax.ShapeDtypeStruct((ROWS_DEV, BASIS), jnp.float32),
            jax.ShapeDtypeStruct((8, PIECE, BLOCK), jnp.float32),
        ),
        in_specs=[pl.BlockSpec(memory_space=pltpu.SMEM)] * 2
        + [pl.BlockSpec(memory_space=pltpu.HBM)],
        out_specs=(pl.BlockSpec(memory_space=pltpu.HBM), pl.BlockSpec(memory_space=pltpu.VMEM)),
        scratch_shapes=[
            pltpu.VMEM((TILE_DEV * BLOCK, BASIS), jnp.bfloat16),
            pltpu.VMEM((ROWS_DEV, BASIS), jnp.float32),
            pltpu.VMEM((3 * BLOCK, BLOCK), jnp.float32),
            pltpu.SemaphoreType.DMA((CHUNKS,)),
            pltpu.SemaphoreType.DMA,
        ],
        compiler_params=pltpu.CompilerParams(vmem_limit_bytes=48 * 1024 * 1024),
        name="sum_and_gram",
    )(place, me, products)


def reduce_everywhere(gram):
    part = gram[:4] + shifted(gram[4:], dcore=1)
    part = part[0] + sum(shifted(part[d], dx=d) for d in (1, 2, 3))
    part = part + sum(shifted(part, dy=d) for d in (1, 2, 3))
    part = part + sum(shifted(part, dz=d) for d in (1, 2, 3))
    mine = jnp.stack([part] + [shifted(part, dx=-d) for d in (1, 2, 3)])
    return mine, shifted(mine, dcore=1)


def piece_order(me):
    return [((i // 4) ^ me[0]) * 4 + ((i % 4 - me[1]) & 3) for i in range(8)]


def finish_kernel(me, mine, other, summed_hbm, ortho_hbm, factor, gram, work, summed, ortho, in_sem, out_sems):
    load = pltpu.make_async_copy(summed_hbm, summed, in_sem)
    load.start()
    for i, order in enumerate(piece_order(me)):
        here = pl.ds(i * PIECE, PIECE)

        @pl.when(order < 4)
        def _():
            gram[here, :] = mine[order & 3]

        @pl.when(order >= 4)
        def _():
            gram[here, :] = other[order & 3]

    row_id = lax.broadcasted_iota(jnp.int32, (BASIS, BASIS), 0)
    col_id = lax.broadcasted_iota(jnp.int32, (BASIS, BASIS), 1)
    work[:BLOCK, :BLOCK] = gram[:BLOCK, :] * (1.0 / ITEMS)
    work[:BLOCK, BLOCK:BASIS] = gram[BLOCK : 2 * BLOCK, :] * (1.0 / ITEMS)
    work[BLOCK:, :BLOCK] = jnp.zeros((BLOCK, BLOCK), jnp.float32)
    work[BLOCK:, BLOCK:BASIS] = gram[2 * BLOCK :, :] * (1.0 / ITEMS)
    work[:, BASIS:] = jnp.where(row_id == col_id, 1.0, 0.0)
    panel_row = lax.broadcasted_iota(jnp.int32, (PANEL, BLOCK), 0)
    for k in range(0, BASIS, PANEL):
        base = k // BLOCK * BLOCK
        window = pl.ds(base, 3 * BLOCK)
        panel = work[k : k + PANEL, window]
        strips = [panel[:, j * BLOCK : (j + 1) * BLOCK] for j in range(3)]
        columns = [
            jnp.broadcast_to(strips[0][:, k + i - base : k + i - base + 1], (PANEL, BLOCK))
            for i in range(PANEL)
        ]
        for i in range(PANEL):
            scale = lax.rsqrt(columns[i][i : i + 1, :])
            column = columns[i] * scale
            below = jnp.where(panel_row > i, column, 0.0)
            for j in range(3):
                pivot_row = strips[j][i : i + 1, :] * scale
                strips[j] = jnp.where(panel_row == i, pivot_row, strips[j] - below * pivot_row)
            for j in range(i + 1, PANEL):
                columns[j] = columns[j] - column * column[j : j + 1, :]
        panel = jnp.concatenate(strips, axis=1)
        work[k : k + PANEL, window] = panel
        after = k + PANEL
        if after < BASIS:
            high, middle, low = split(panel)
            left = jnp.concatenate([high, high, middle, middle, high, low], axis=0)
            right = jnp.concatenate([high, middle, high, middle, low, high], axis=0)
            update = lax.dot_general(
                left[:, : BASIS - base],
                right,
                (((0,), (0,)), ((), ())),
                preferred_element_type=jnp.float32,
            )
            work[after:, window] = work[after:, window] - update[after - base :, :]
    lower = row_id >= col_id
    factor[...] = jnp.where(lower, work[:, :BASIS].T, 0.0)
    inverse = jnp.where(lower, work[:, BASIS:], 0.0)
    load.wait()
    rows = ROWS_DEV // OUT_CHUNKS
    stores = []
    for i in range(OUT_CHUNKS):
        part = pl.ds(i * rows, rows)
        ortho[part, :] = lax.dot_general(
            summed[part, :],
            inverse,
            (((1,), (1,)), ((), ())),
            precision=lax.Precision.HIGHEST,
            preferred_element_type=jnp.float32,
        )
        store = pltpu.make_async_copy(ortho.at[part, :], ortho_hbm.at[part, :], out_sems.at[i])
        store.start()
        stores.append(store)
    for store in stores:
        store.wait()


def finish(me, mine, other, summed):
    return pl.pallas_call(
        finish_kernel,
        out_shape=(
            jax.ShapeDtypeStruct((ROWS_DEV, BASIS), jnp.float32),
            jax.ShapeDtypeStruct((BASIS, BASIS), jnp.float32),
        ),
        in_specs=[
            pl.BlockSpec(memory_space=pltpu.SMEM),
            pl.BlockSpec(memory_space=pltpu.VMEM),
            pl.BlockSpec(memory_space=pltpu.VMEM),
            pl.BlockSpec(memory_space=pl.ANY),
        ],
        out_specs=(pl.BlockSpec(memory_space=pl.ANY), pl.BlockSpec(memory_space=pltpu.VMEM)),
        scratch_shapes=[
            pltpu.VMEM((3 * BLOCK, BLOCK), jnp.float32),
            pltpu.VMEM((BASIS, 2 * BASIS), jnp.float32),
            pltpu.VMEM((ROWS_DEV, BASIS), jnp.float32),
            pltpu.VMEM((ROWS_DEV, BASIS), jnp.float32),
            pltpu.SemaphoreType.DMA,
            pltpu.SemaphoreType.DMA((OUT_CHUNKS,)),
        ],
        compiler_params=pltpu.CompilerParams(vmem_limit_bytes=40 * 1024 * 1024),
        name="finish",
    )(me, mine, other, summed)


def local(tiles, tile_src, tile_out, basis0):
    row = lax.axis_index("row").astype(jnp.int32)
    col = lax.axis_index("col").astype(jnp.int32)
    me = jnp.stack([col & 1, (col >> 1) & 3])
    src = tile_src[0, 0]
    group = src >> 4
    distance = (((group >> 1) - (row >> 1)) & 3) + 4 * ((group + row) & 1)
    src = distance * BLOCKS_DEV + (src & 15)

    parts, place = gather_column(basis0, tile_out[0, 0] & 15)
    products = make_products(src, tiles[0, 0], parts)
    products, place, me = together(products, place, me)
    products = lax.all_to_all(
        products.reshape(N_COL, PER_PEER * BLOCK, BASIS), "col", 0, 0, tiled=True
    )
    summed, gram = sum_and_gram(place, me, products.reshape(-1, BASIS))
    return finish(me, *reduce_everywhere(gram), summed)


def solution(mesh):
    in_specs = (
        P("row", "col", None, None, None),
        P("row", "col", None),
        P("row", "col", None),
        P(("row", "col"), None),
    )
    out_specs = (P(("row", "col"), None), P())
    return jax.shard_map(local, mesh=mesh, in_specs=in_specs, out_specs=out_specs, check_vma=False)
```

time: 735 us -> 238 us (0.32)
  waiting for transfers between devices: 561 us -> 45.6 us
  blocking collectives: 0 us -> 126 us
  other arithmetic: 59.3 us -> 2.11 us
  local copies, waits for them, and re-layouts: 60.7 us -> 6.14 us
  matrix products: 37.8 us -> 0 us
  starting transfers between devices: 0.3 us -> 29.6 us
  Pallas kernels: 0 us -> 27 us
  between operations: 15.1 us -> 0.91 us
    reduce_scatter x1 -> x0, waiting for transfers between devices: 246 us -> none  [local(): lax.psum_scatter(placed.reshape(ROWS_DEV * lax.axis_size('col'), BASIS),...]
    all_gather x1 -> x0, waiting for transfers between devices: 170 us -> none  [local(): lax.all_gather(basis0, 'row', axis=0, tiled=True).reshape(-1, BLOCK, BASIS)]
    psum x1 -> x0, waiting for transfers between devices: 144 us -> none  [local(): gram_total = lax.psum(local_gram, ('row', 'col')) / item_count]
    all_to_all x0 -> x2, blocking collectives: none -> 126 us  [the longest x1 103 us: local(): lax.all_to_all(products.reshape(N_COL, PER_PEER * BLOCK, BASIS), 'col', 0...]
    another operation x10 -> x2, other arithmetic: 54.7 us -> 0.08 us  [the longest x1 0.07 us: local(): me = jnp.stack([col & 1, col >> 1 & 3])]
    ppermute x0 -> x23, waiting for transfers between devices: none -> 45.6 us  [the longest x9 30.8 us: row_shifted(): return lax.ppermute(value, 'row', pairs)]
    dot_general x3 -> x0, matrix products: 33.3 us -> none  [the longest x1 15 us: local(): jnp.einsum('pqb,pqik->pbik', picker, products, preferred_element_type=jnp...]
    dot_general x1 -> x0, local copies, waits for them, and re-layouts: 31.7 us -> none  [local(): jnp.einsum('pqb,pqik->pbik', picker, products, preferred_element_type=jnp...]
  transfers between devices with their start and end apart: 3 -> 23, of which waited for: 3 -> 15; matrix products, arithmetic and copies ran while one was open for 0% -> 1% of each run, Pallas kernels for 0% -> 0%
where the time goes in v2:
time: 238 us; the launch traced here: 237 us
  blocking collectives  126 us (53%)
  waiting for transfers between devices  45.6 us (19%)
  starting transfers between devices  29.6 us (12%)
  Pallas kernels  27 us (11%)
  local copies, waits for them, and re-layouts  6.14 us (3%)
    all_to_all x1, blocking collectives, local(): lax.all_to_all(products.reshape(N_COL, PER_PEER * BLOCK, BASIS), 'col', 0...  103 us
    ppermute x9, waiting for transfers between devices, row_shifted(): return lax.ppermute(value, 'row', pairs)  30.8 us
    all_to_all x1, blocking collectives, gather_column(): lax.all_to_all(place.reshape(N_COL, PER_PEER), 'col', 0, 0, tiled=True)  23.3 us
    ppermute x14, starting transfers between devices, shifted(): return lax.ppermute(value, BOTH, pairs)  16.8 us
    ppermute x14, waiting for transfers between devices, shifted(): return lax.ppermute(value, BOTH, pairs)  14.8 us
    ppermute x9, starting transfers between devices, row_shifted(): return lax.ppermute(value, 'row', pairs)  12.9 us
    pallas_call x1, Pallas kernels, finish(): pl.pallas_call(finish_kernel, out_shape=(jax.ShapeDtypeStruct((ROWS_DEV,...  11.3 us
    pallas_call x1, Pallas kernels, make_products(): pl.pallas_call(product_kernel, out_shape=jax.ShapeDtypeStruct((TILE_DEV *...  9.93 us
  transfers between devices with their start and end apart: 23, of which 15 were waited for; matrix products, arithmetic and copies ran while one was open for 1% of the time, Pallas kernels for 0%

profile of v2, /device:TPU:1, one launch (start us, length us, event | category | flops | bytes accessed | tf_op | source)
XLA Modules:
  0.0 237.4 jit_solution(17219605935534131531)
XLA Ops:
  0.6 4.7 %collective-permute-start.1 = (bf16[2048,256]{1,0:T(8,128)(2,1)}, bf16[2048,256]{1,0:T(8,128)(2,1)S(1)}, u32[]{:S(2)}, u32[]{:S(2)}) collective-permute-start(bf16[2048,256]{1,0:T(8,128)(2,1)} %refs_0_.1), channel_id=1, source_target_pairs={{0,96},{16,112},{32,0},{48,16},{64,32},{80,48},{96,64},{112,80},{1... | collective-permute-start | bytes 3145736 | tf_op jit(solution)/shard_map/ppermute | solution.py:44
  5.3 1.3 collective-permute-start.2
  7.2 20.2 %collective-permute-done.1.refs_1_ = bf16[2048,256]{1,0:T(8,128)(2,1)S(1)} collective-permute-done((bf16[2048,256]{1,0:T(8,128)(2,1)}, bf16[2048,256]{1,0:T(8,128)(2,1)S(1)}, u32[]{:S(2)}, u32[]{:S(2)}) %collective-permute-start.1) | collective-permute-done | bytes 1048608 | tf_op jit(solution)/shard_map/ppermute | solution.py:44
  27.4 3.0 %collective-permute-done.refs_3_ = bf16[2048,256]{1,0:T(8,128)(2,1)S(1)} collective-permute-done((bf16[2048,256]{1,0:T(8,128)(2,1)}, bf16[2048,256]{1,0:T(8,128)(2,1)S(1)}, u32[]{:S(2)}, u32[]{:S(2)}) %collective-permute-start) | collective-permute-done | bytes 1048608 | tf_op jit(solution)/shard_map/ppermute | solution.py:44
  30.4 1.3 collective-permute-start.4
  31.7 2.7 %collective-permute-start.3 = (bf16[2048,256]{1,0:T(8,128)(2,1)S(1)}, bf16[2048,256]{1,0:T(8,128)(2,1)S(1)}, u32[]{:S(2)}, u32[]{:S(2)}) collective-permute-start(bf16[2048,256]{1,0:T(8,128)(2,1)S(1)} %collective-permute-done.1.refs_1_), channel_id=1, source_target_pairs={{0,96},{16,112},{32,0},{48,16},{64,32},{80,48},{96,64},{112,80},{1... | collective-permute-start | bytes 3145736 | tf_op jit(solution)/shard_map/ppermute | solution.py:44
  34.5 23.3 %all_to_all.14 = s32[16,1,8]{2,1,0:T(1,128)S(1)} all-to-all(s32[16,1,8]{2,1,0:T(1,128)S(1)} %bitcast.28), channel_id=1, replica_groups=mesh['row'=8,'col'=16] {'col'}, dimensions={0} | all-to-all | bytes 1024 | tf_op jit(solution)/shard_map/all_to_all | solution.py:59
  59.1 1.7 slice.28
  60.9 1.7 slice.27
  62.6 2.7 %collective-permute-start.7 = (bf16[688,256]{1,0:T(8,128)(2,1)}, bf16[688,256]{1,0:T(8,128)(2,1)}, u32[]{:S(2)}, u32[]{:S(2)}) collective-permute-start(bf16[688,256]{1,0:T(8,128)(2,1)} %slice.28), channel_id=1, source_target_pairs={{0,96},{16,112},{32,0},{48,16},{64,32},{80,48},{96,64},{112,80},{1... | collective-permute-start | bytes 1056776 | tf_op jit(solution)/shard_map/ppermute | solution.py:44
  67.0 7.6 %collective-permute-done.8.refs_8_ = bf16[672,256]{1,0:T(8,128)(2,1)} collective-permute-done((bf16[672,256]{1,0:T(8,128)(2,1)}, bf16[672,256]{1,0:T(8,128)(2,1)}, u32[]{:S(2)}, u32[]{:S(2)}) %collective-permute-start.8) | collective-permute-done | bytes 344096 | tf_op jit(solution)/shard_map/ppermute | solution.py:44
  74.7 1.2 copy-done
  75.9 9.9 %products.1 = bf16[16384,256]{1,0:T(8,128)(2,1)} custom-call(s32[128]{0:T(128)S(1)} %add_bitcast_fusion.src, bf16[128,128,128]{2,1,0:T(8,128)(2,1)} %bitcast.26, bf16[2048,256]{1,0:T(8,128)(2,1)S(1)} %copy-done, bf16[2048,256]{1,0:T(8,128)(2,1)S(1)} %collective-permute-done.1.refs_1_, bf16[2048,256]{1,0:T(8,128)(2,1)S(1)} %collective-permute-done.3.refs_2_, ...), custom_call_target="tpu_custom_call" | custom-call | tf_op jit(solution)/shard_map/products/pallas_call | solution.py:115
  85.8 102.7 %all_to_all.15 = bf16[16,1024,256]{2,1,0:T(8,128)(2,1)} all-to-all(bf16[16,1024,256]{2,1,0:T(8,128)(2,1)} %bitcast.24), channel_id=1, replica_groups=mesh['row'=8,'col'=16] {'col'}, dimensions={0} | all-to-all | bytes 16777216 | tf_op jit(solution)/shard_map/all_to_all | solution.py:321
  188.5 5.7 %sum_and_gram.1 = (f32[2048,256]{1,0:T(8,128)S(1)}, f32[8,48,128]{2,1,0:T(8,128)S(1)}) custom-call(s32[128]{0:T(128)S(1)} %reshape.36.place, s32[2]{0:T(128)S(1)} %pad_add_fusion.me, bf16[16384,256]{1,0:T(8,128)(2,1)} %bitcast.25), custom_call_target="tpu_custom_call" | custom-call | tf_op jit(solution)/shard_map/sum_and_gram/pallas_call | solution.py:172
  194.2 1.2 collective-permute-start.9
  195.4 0.9 collective-permute-done.9
  196.7 0.9 collective-permute-start.12
  198.2 2.5 %collective-permute-done.11 = f32[48,128]{1,0:T(8,128)S(1)} collective-permute-done((f32[48,128]{1,0:T(8,128)S(1)}, f32[48,128]{1,0:T(8,128)S(1)}, u32[]{:S(2)}, u32[]{:S(2)}) %collective-permute-start.11) | collective-permute-done | bytes 24608 | tf_op jit(solution)/shard_map/ppermute | solution.py:39
  200.6 1.1 collective-permute-done.10
  201.8 0.9 collective-permute-start.15
  202.6 1.2 collective-permute-start.14
  204.7 2.1 collective-permute-done.14
  206.8 0.9 collective-permute-done.13
  207.7 1.4 collective-permute-start.18
  209.8 0.8 collective-permute-done.18
  210.7 2.7 %collective-permute-done.17 = f32[48,128]{1,0:T(8,128)S(1)} collective-permute-done((f32[48,128]{1,0:T(8,128)S(1)}, f32[48,128]{1,0:T(8,128)S(1)}, u32[]{:S(2)}, u32[]{:S(2)}) %collective-permute-start.17) | collective-permute-done | bytes 24608 | tf_op jit(solution)/shard_map/ppermute | solution.py:39
  213.4 2.1 collective-permute-start.20
  216.1 1.5 collective-permute-done.21
  218.2 6.7 %collective-permute-start.22 = (f32[4,48,128]{2,1,0:T(8,128)S(1)}, f32[4,48,128]{2,1,0:T(8,128)S(1)}, u32[]{:S(2)}, u32[]{:S(2)}) collective-permute-start(f32[4,48,128]{2,1,0:T(8,128)S(1)} %pad_maximum_fusion.mine), channel_id=1, source_target_pairs={{0,1},{1,0},{2,3},{3,2},{4,5},{5,4},{6,7},{7,6},{16,17},{17,16},{1... | collective-permute-start | bytes 294920 | tf_op jit(solution)/shard_map/ppermute | solution.py:39
  224.9 0.9 collective-permute-done.22.other
  225.9 11.3 %finish.1 = (f32[2048,256]{1,0:T(8,128)}, f32[256,256]{1,0:T(8,128)}) custom-call(s32[2]{0:T(128)S(1)} %pad_add_fusion.me, f32[4,48,128]{2,1,0:T(8,128)S(1)} %pad_maximum_fusion.mine, f32[4,48,128]{2,1,0:T(8,128)S(1)} %collective-permute-done.22.other, f32[2048,256]{1,0:T(8,128)S(1)} %get-tuple-element.27.summed_hbm), custom_call_target="tpu_custom_call" | custom-call | tf_op jit(solution)/shard_map/finish/pallas_call | solution.py:283
  (38 shorter events, 7.5 us)
Async XLA Ops:
  0.6 26.8 %collective-permute-start.1 = (bf16[2048,256]{1,0:T(8,128)(2,1)}, bf16[2048,256]{1,0:T(8,128)(2,1)S(1)}, u32[]{:S(2)}, u32[]{:S(2)}) collective-permute-start(bf16[2048,256]{1,0:T(8,128)(2,1)} %refs_0_.1), channel_id=1, source_target_pairs={{0,96},{16,112},{32,0},{48,16},{64,32},{80,48},{96,64},{112,80},{1... | collective-permute-start | bytes 3145736 | tf_op jit(solution)/shard_map/ppermute | solution.py:44
  5.3 25.1 %collective-permute-start = (bf16[2048,256]{1,0:T(8,128)(2,1)}, bf16[2048,256]{1,0:T(8,128)(2,1)S(1)}, u32[]{:S(2)}, u32[]{:S(2)}) collective-permute-start(bf16[2048,256]{1,0:T(8,128)(2,1)} %refs_0_.1), channel_id=1, source_target_pairs={{0,32},{16,48},{32,64},{48,80},{64,96},{80,112},{96,0},{112,16},{1... | collective-permute-start | bytes 3145736 | tf_op jit(solution)/shard_map/ppermute | solution.py:44
  5.3 25.1 %collective-permute-start.2 = (bf16[2048,256]{1,0:T(8,128)(2,1)}, bf16[2048,256]{1,0:T(8,128)(2,1)}, u32[]{:S(2)}, u32[]{:S(2)}) collective-permute-start(bf16[2048,256]{1,0:T(8,128)(2,1)} %refs_0_.1), channel_id=1, source_target_pairs={{0,16},{16,0},{32,48},{48,32},{64,80},{80,64},{96,112},{112,96},{1... | collective-permute-start | bytes 3145736 | tf_op jit(solution)/shard_map/ppermute | solution.py:44
  30.4 28.7 %collective-permute-start.5 = (bf16[2048,256]{1,0:T(8,128)(2,1)}, bf16[2048,256]{1,0:T(8,128)(2,1)}, u32[]{:S(2)}, u32[]{:S(2)}) collective-permute-start(bf16[2048,256]{1,0:T(8,128)(2,1)} %collective-permute-done.2.refs_4_), channel_id=1, source_target_pairs={{0,32},{16,48},{32,64},{48,80},{64,96},{80,112},{96,0},{112,16},{1... | collective-permute-start | bytes 3145736 | tf_op jit(solution)/shard_map/ppermute | solution.py:44
  30.4 28.7 %collective-permute-start.4 = (bf16[2048,256]{1,0:T(8,128)(2,1)S(1)}, bf16[2048,256]{1,0:T(8,128)(2,1)}, u32[]{:S(2)}, u32[]{:S(2)}) collective-permute-start(bf16[2048,256]{1,0:T(8,128)(2,1)S(1)} %collective-permute-done.1.refs_1_), channel_id=1, source_target_pairs={{0,16},{16,0},{32,48},{48,32},{64,80},{80,64},{96,112},{112,96},{1... | collective-permute-start | bytes 3145736 | tf_op jit(solution)/shard_map/ppermute | solution.py:44
  31.7 27.4 %collective-permute-start.3 = (bf16[2048,256]{1,0:T(8,128)(2,1)S(1)}, bf16[2048,256]{1,0:T(8,128)(2,1)S(1)}, u32[]{:S(2)}, u32[]{:S(2)}) collective-permute-start(bf16[2048,256]{1,0:T(8,128)(2,1)S(1)} %collective-permute-done.1.refs_1_), channel_id=1, source_target_pairs={{0,96},{16,112},{32,0},{48,16},{64,32},{80,48},{96,64},{112,80},{1... | collective-permute-start | bytes 3145736 | tf_op jit(solution)/shard_map/ppermute | solution.py:44
  62.6 12.1 %collective-permute-start.6 = (bf16[688,256]{1,0:T(8,128)(2,1)}, bf16[688,256]{1,0:T(8,128)(2,1)S(1)}, u32[]{:S(2)}, u32[]{:S(2)}) collective-permute-start(bf16[688,256]{1,0:T(8,128)(2,1)} %slice.27), channel_id=1, source_target_pairs={{0,32},{16,48},{32,64},{48,80},{64,96},{80,112},{96,0},{112,16},{1... | collective-permute-start | bytes 1056776 | tf_op jit(solution)/shard_map/ppermute | solution.py:44
  62.6 12.1 %collective-permute-start.7 = (bf16[688,256]{1,0:T(8,128)(2,1)}, bf16[688,256]{1,0:T(8,128)(2,1)}, u32[]{:S(2)}, u32[]{:S(2)}) collective-permute-start(bf16[688,256]{1,0:T(8,128)(2,1)} %slice.28), channel_id=1, source_target_pairs={{0,96},{16,112},{32,0},{48,16},{64,32},{80,48},{96,64},{112,80},{1... | collective-permute-start | bytes 1056776 | tf_op jit(solution)/shard_map/ppermute | solution.py:44
  66.0 8.6 %collective-permute-start.8 = (bf16[672,256]{1,0:T(8,128)(2,1)}, bf16[672,256]{1,0:T(8,128)(2,1)}, u32[]{:S(2)}, u32[]{:S(2)}) collective-permute-start(bf16[672,256]{1,0:T(8,128)(2,1)} %slice.29), channel_id=1, source_target_pairs={{0,16},{16,0},{32,48},{48,32},{64,80},{80,64},{96,112},{112,96},{1... | collective-permute-start | bytes 1032200 | tf_op jit(solution)/shard_map/ppermute | solution.py:44
  74.7 1.2 copy-start
  194.2 2.1 collective-permute-start.9
  196.4 4.3 %collective-permute-start.11 = (f32[48,128]{1,0:T(8,128)S(1)}, f32[48,128]{1,0:T(8,128)S(1)}, u32[]{:S(2)}, u32[]{:S(2)}) collective-permute-start(f32[48,128]{1,0:T(8,128)S(1)} %get-tuple-element.28), channel_id=1, source_target_pairs={{0,4},{1,5},{2,6},{3,7},{4,0},{5,1},{6,2},{7,3},{16,20},{17,21},{1... | collective-permute-start | bytes 73736 | tf_op jit(solution)/shard_map/ppermute | solution.py:39
  196.7 3.9 %collective-permute-start.12 = (f32[48,128]{1,0:T(8,128)S(1)}, f32[48,128]{1,0:T(8,128)S(1)}, u32[]{:S(2)}, u32[]{:S(2)}) collective-permute-start(f32[48,128]{1,0:T(8,128)S(1)} %get-tuple-element.29), channel_id=1, source_target_pairs={{0,6},{1,7},{2,0},{3,1},{4,2},{5,3},{6,4},{7,5},{16,22},{17,23},{1... | collective-permute-start | bytes 73736 | tf_op jit(solution)/shard_map/ppermute | solution.py:39
  197.6 4.1 %collective-permute-start.10 = (f32[48,128]{1,0:T(8,128)S(1)}, f32[48,128]{1,0:T(8,128)S(1)}, u32[]{:S(2)}, u32[]{:S(2)}) collective-permute-start(f32[48,128]{1,0:T(8,128)S(1)} %get-tuple-element.30), channel_id=1, source_target_pairs={{0,2},{1,3},{2,4},{3,5},{4,6},{5,7},{6,0},{7,1},{16,18},{17,19},{1... | collective-permute-start | bytes 73736 | tf_op jit(solution)/shard_map/ppermute | solution.py:39
  201.8 2.9 %collective-permute-start.15 = (f32[48,128]{1,0:T(8,128)S(1)}, f32[48,128]{1,0:T(8,128)S(1)}, u32[]{:S(2)}, u32[]{:S(2)}) collective-permute-start(f32[48,128]{1,0:T(8,128)S(1)} %fusion), channel_id=1, source_target_pairs={{0,24},{1,25},{2,26},{3,27},{4,28},{5,29},{6,30},{7,31},{16,0},{17... | collective-permute-start | bytes 73736 | tf_op jit(solution)/shard_map/ppermute | solution.py:39
  202.6 4.2 %collective-permute-start.14 = (f32[48,128]{1,0:T(8,128)S(1)}, f32[48,128]{1,0:T(8,128)S(1)}, u32[]{:S(2)}, u32[]{:S(2)}) collective-permute-start(f32[48,128]{1,0:T(8,128)S(1)} %fusion), channel_id=1, source_target_pairs={{0,8},{1,9},{2,10},{3,11},{4,12},{5,13},{6,14},{7,15},{16,24},{17,... | collective-permute-start | bytes 73736 | tf_op jit(solution)/shard_map/ppermute | solution.py:39
  203.8 3.9 %collective-permute-start.13 = (f32[48,128]{1,0:T(8,128)S(1)}, f32[48,128]{1,0:T(8,128)S(1)}, u32[]{:S(2)}, u32[]{:S(2)}) collective-permute-start(f32[48,128]{1,0:T(8,128)S(1)} %fusion), channel_id=1, source_target_pairs={{0,16},{1,17},{2,18},{3,19},{4,20},{5,21},{6,22},{7,23},{16,8},{17... | collective-permute-start | bytes 73736 | tf_op jit(solution)/shard_map/ppermute | solution.py:39
  207.7 2.9 %collective-permute-start.18 = (f32[48,128]{1,0:T(8,128)S(1)}, f32[48,128]{1,0:T(8,128)S(1)}, u32[]{:S(2)}, u32[]{:S(2)}) collective-permute-start(f32[48,128]{1,0:T(8,128)S(1)} %add_add_fusion.1), channel_id=1, source_target_pairs={{0,96},{1,97},{2,98},{3,99},{4,100},{5,101},{6,102},{7,103},{16,11... | collective-permute-start | bytes 73736 | tf_op jit(solution)/shard_map/ppermute | solution.py:39
  209.1 4.2 %collective-permute-start.17 = (f32[48,128]{1,0:T(8,128)S(1)}, f32[48,128]{1,0:T(8,128)S(1)}, u32[]{:S(2)}, u32[]{:S(2)}) collective-permute-start(f32[48,128]{1,0:T(8,128)S(1)} %add_add_fusion.1), channel_id=1, source_target_pairs={{0,64},{1,65},{2,66},{3,67},{4,68},{5,69},{6,70},{7,71},{16,80},{1... | collective-permute-start | bytes 73736 | tf_op jit(solution)/shard_map/ppermute | solution.py:39
  209.1 4.2 %collective-permute-start.16 = (f32[48,128]{1,0:T(8,128)S(1)}, f32[48,128]{1,0:T(8,128)S(1)}, u32[]{:S(2)}, u32[]{:S(2)}) collective-permute-start(f32[48,128]{1,0:T(8,128)S(1)} %add_add_fusion.1), channel_id=1, source_target_pairs={{0,32},{1,33},{2,34},{3,35},{4,36},{5,37},{6,38},{7,39},{16,48},{1... | collective-permute-start | bytes 73736 | tf_op jit(solution)/shard_map/ppermute | solution.py:39
  213.3 4.3 %collective-permute-start.21 = (f32[48,128]{1,0:T(8,128)S(1)}, f32[48,128]{1,0:T(8,128)S(1)}, u32[]{:S(2)}, u32[]{:S(2)}) collective-permute-start(f32[48,128]{1,0:T(8,128)S(1)} %add_add_fusion), channel_id=1, source_target_pairs={{0,2},{1,3},{2,4},{3,5},{4,6},{5,7},{6,0},{7,1},{16,18},{17,19},{1... | collective-permute-start | bytes 73736 | tf_op jit(solution)/shard_map/ppermute | solution.py:39
  213.4 4.3 %collective-permute-start.20 = (f32[48,128]{1,0:T(8,128)S(1)}, f32[48,128]{1,0:T(8,128)S(1)}, u32[]{:S(2)}, u32[]{:S(2)}) collective-permute-start(f32[48,128]{1,0:T(8,128)S(1)} %add_add_fusion), channel_id=1, source_target_pairs={{0,4},{1,5},{2,6},{3,7},{4,0},{5,1},{6,2},{7,3},{16,20},{17,21},{1... | collective-permute-start | bytes 73736 | tf_op jit(solution)/shard_map/ppermute | solution.py:39
  215.5 2.7 %collective-permute-start.19 = (f32[48,128]{1,0:T(8,128)S(1)}, f32[48,128]{1,0:T(8,128)S(1)}, u32[]{:S(2)}, u32[]{:S(2)}) collective-permute-start(f32[48,128]{1,0:T(8,128)S(1)} %add_add_fusion), channel_id=1, source_target_pairs={{0,6},{1,7},{2,0},{3,1},{4,2},{5,3},{6,4},{7,5},{16,22},{17,23},{1... | collective-permute-start | bytes 73736 | tf_op jit(solution)/shard_map/ppermute | solution.py:39
  218.2 7.6 %collective-permute-start.22 = (f32[4,48,128]{2,1,0:T(8,128)S(1)}, f32[4,48,128]{2,1,0:T(8,128)S(1)}, u32[]{:S(2)}, u32[]{:S(2)}) collective-permute-start(f32[4,48,128]{2,1,0:T(8,128)S(1)} %pad_maximum_fusion.mine), channel_id=1, source_target_pairs={{0,1},{1,0},{2,3},{3,2},{4,5},{5,4},{6,7},{7,6},{16,17},{17,16},{1... | collective-permute-start | bytes 294920 | tf_op jit(solution)/shard_map/ppermute | solution.py:39

commit v3 on v2

--- a/solution.py
+++ b/solution.py
@@ -15,9 +15,8 @@
 N_COL = 16
 ITEMS = 262144
 BOTH = ("row", "col")
-CUTS = (688, 1376)
-PARTS = 10
-PANEL = 16
+PARTS = 14
+PANEL = 32
 PIECE = 48
 CHUNKS = 16
 OUT_CHUNKS = 8
@@ -49,22 +48,31 @@
 
 
 def gather_column(own, place):
+    half = ROWS_DEV // 2
     below = row_shifted(own, 1, 0)
-    above = row_shifted(own, -1, 0)
-    beside = row_shifted(own, 0, 1)
-    below, above, beside, place = together(below, above, beside, place)
-    across = row_shifted(above, -1, 0)
-    beside_above = row_shifted(above, 0, 1)
-    beside_below = row_shifted(beside, 1, 0)
-    place = lax.all_to_all(place.reshape(N_COL, PER_PEER), "col", 0, 0, tiled=True).reshape(-1)
-    across, beside_above, beside_below, place = together(across, beside_above, beside_below, place)
-    first, second = CUTS
-    last = (
-        row_shifted(beside_below[:first], 1, 0),
-        row_shifted(beside_above[first:second], -1, 0),
-        row_shifted(across[second:], 0, 1),
+    above_a = row_shifted(own[:half], -1, 0)
+    beside_a = row_shifted(own[:half], 0, 1)
+    above_b = row_shifted(own[half:], -1, 0)
+    beside_b = row_shifted(own[half:], 0, 1)
+    beside_below_a = row_shifted(beside_a, 1, 0)
+    beside_below_b = row_shifted(beside_b, 1, 0)
+    across_a = row_shifted(above_a, -1, 0)
+    across_b = row_shifted(above_b, -1, 0)
+    below, above_a, above_b = together(below, above_a, above_b)
+    beside_above_b = row_shifted(above_b, 0, 1)
+    beside_above_a = row_shifted(above_a, 0, 1)
+    beside_across_a = row_shifted(beside_below_a, 1, 0)
+    beside_across_b = row_shifted(beside_above_b, -1, 0)
+    across_a, across_b, beside_above_a, beside_below_b, place = together(
+        across_a, across_b, beside_above_a, beside_below_b, place
     )
-    return (own, above, across, below, beside, beside_above, *last, beside_below), place
+    place = lax.all_to_all(place.reshape(N_COL, 1, PER_PEER), "col", 0, 0, tiled=True)
+    parts = (
+        own, above_a, above_b, across_a, across_b, below, beside_a, beside_b,
+        beside_above_a, beside_above_b, beside_across_a, beside_across_b,
+        beside_below_a, beside_below_b,
+    )
+    return parts, place
 
 
 def split(value):
@@ -126,7 +134,7 @@
             pltpu.SemaphoreType.DMA((PARTS,)),
             pltpu.SemaphoreType.DMA((CHUNKS,)),
         ],
-        compiler_params=pltpu.CompilerParams(vmem_limit_bytes=48 * 1024 * 1024),
+        compiler_params=pltpu.CompilerParams(vmem_limit_bytes=56 * 1024 * 1024),
         name="products",
     )(src, tiles, *parts)
 
@@ -145,7 +153,7 @@
 
         @pl.loop(g * share, (g + 1) * share, unroll=4)
         def _(t):
-            rows = pl.ds(pl.multiple_of(place[t] * BLOCK, BLOCK), BLOCK)
+            rows = pl.ds(pl.multiple_of(place[t >> 3, 0, t & 7] * BLOCK, BLOCK), BLOCK)
             product = products[pl.ds(pl.multiple_of(t * BLOCK, BLOCK), BLOCK), :]
             summed[rows, :] += product.astype(jnp.float32)
 
@@ -260,16 +268,18 @@
     lower = row_id >= col_id
     factor[...] = jnp.where(lower, work[:, :BASIS].T, 0.0)
     inverse = jnp.where(lower, work[:, BASIS:], 0.0)
+    high, middle, _ = split(inverse)
+    right = jnp.concatenate([high, middle, high], axis=1)
     load.wait()
     rows = ROWS_DEV // OUT_CHUNKS
     stores = []
     for i in range(OUT_CHUNKS):
         part = pl.ds(i * rows, rows)
+        high, middle, _ = split(summed[part, :])
         ortho[part, :] = lax.dot_general(
-            summed[part, :],
-            inverse,
+            jnp.concatenate([high, high, middle], axis=1),
+            right,
             (((1,), (1,)), ((), ())),
-            precision=lax.Precision.HIGHEST,
             preferred_element_type=jnp.float32,
         )
         store = pltpu.make_async_copy(ortho.at[part, :], ortho_hbm.at[part, :], out_sems.at[i])

time: 238 us -> 232 us (0.975)
  blocking collectives: 126 us -> 103 us
  starting transfers between devices: 29.6 us -> 48.1 us
  local copies, waits for them, and re-layouts: 6.14 us -> 3.58 us
    all_to_all x1 -> x0, blocking collectives: 23.3 us -> none  [gather_column(): lax.all_to_all(place.reshape(N_COL, PER_PEER), 'col', 0, 0, tiled=True)]
    all_to_all x0 -> x1, starting transfers between devices: none -> 10.1 us  [gather_column(): lax.all_to_all(place.reshape(N_COL, 1, PER_PEER), 'col', 0, 0, tiled=True)]
    ppermute x9 -> x13, starting transfers between devices: 12.9 us -> 19.2 us  [row_shifted(): return lax.ppermute(value, 'row', pairs)]
    slice x3 -> x1, local copies, waits for them, and re-layouts: 4.22 us -> 1.27 us  [gather_column(): above_b = row_shifted(own[half:], -1, 0)]
    ppermute x9 -> x13, waiting for transfers between devices: 30.8 us -> 32.5 us  [row_shifted(): return lax.ppermute(value, 'row', pairs)]
  transfers between devices with their start and end apart: 23 -> 28, of which waited for: 15 -> 16; matrix products, arithmetic and copies ran while one was open for 1% -> 2% of each run, Pallas kernels for 0% -> 5%
where the time goes in v3:
time: 232 us
  blocking collectives  103 us (44%)
  starting transfers between devices  48.1 us (21%)
  waiting for transfers between devices  47.1 us (20%)
  Pallas kernels  26.7 us (12%)
  local copies, waits for them, and re-layouts  3.58 us (2%)
    all_to_all x1, blocking collectives, local(): lax.all_to_all(products.reshape(N_COL, PER_PEER * BLOCK, BASIS), 'col', 0...  103 us
    ppermute x13, waiting for transfers between devices, row_shifted(): return lax.ppermute(value, 'row', pairs)  32.5 us
    ppermute x13, starting transfers between devices, row_shifted(): return lax.ppermute(value, 'row', pairs)  19.2 us
    ppermute x14, starting transfers between devices, shifted(): return lax.ppermute(value, BOTH, pairs)  18.8 us
    ppermute x14, waiting for transfers between devices, shifted(): return lax.ppermute(value, BOTH, pairs)  14.6 us
    pallas_call x1, Pallas kernels, make_products(): pl.pallas_call(product_kernel, out_shape=jax.ShapeDtypeStruct((TILE_DEV *...  11 us
    all_to_all x1, starting transfers between devices, gather_column(): lax.all_to_all(place.reshape(N_COL, 1, PER_PEER), 'col', 0, 0, tiled=True)  10.1 us
    pallas_call x1, Pallas kernels, finish(): pl.pallas_call(finish_kernel, out_shape=(jax.ShapeDtypeStruct((ROWS_DEV,...  9.88 us
  transfers between devices with their start and end apart: 28, of which 16 were waited for; matrix products, arithmetic and copies ran while one was open for 2% of the time, Pallas kernels for 5%

profile of v3, /device:TPU:1, one launch (start us, length us, event | category | flops | bytes accessed | tf_op | source)
XLA Modules:
  0.0 231.7 jit_solution(11466353417093059618)
XLA Ops:
  0.6 2.5 %collective-permute-start = (bf16[2048,256]{1,0:T(8,128)(2,1)}, bf16[2048,256]{1,0:T(8,128)(2,1)S(1)}, u32[]{:S(2)}, u32[]{:S(2)}) collective-permute-start(bf16[2048,256]{1,0:T(8,128)(2,1)} %refs_0_.1), channel_id=1, source_target_pairs={{0,32},{16,48},{32,64},{48,80},{64,96},{80,112},{96,0},{112,16},{1... | collective-permute-start | bytes 3145736 | tf_op jit(solution)/shard_map/ppermute | solution.py:43
  3.2 1.3 fusion.1
  4.4 1.4 collective-permute-start.6
  6.0 2.1 collective-permute-start.2
  8.1 1.4 collective-permute-start.1
  9.6 7.4 %collective-permute-done.6.refs_7_ = bf16[1024,256]{1,0:T(8,128)(2,1)S(1)} collective-permute-done((bf16[1024,256]{1,0:T(8,128)(2,1)S(1)}, bf16[1024,256]{1,0:T(8,128)(2,1)S(1)}, u32[]{:S(2)}, u32[]{:S(2)}) %collective-permute-start.6) | collective-permute-done | bytes 524320 | tf_op jit(solution)/shard_map/ppermute | solution.py:43
  17.0 1.6 collective-permute-start.7
  18.6 9.6 %collective-permute-done.8.refs_6_ = bf16[1024,256]{1,0:T(8,128)(2,1)S(1)} collective-permute-done((bf16[1024,256]{1,0:T(8,128)(2,1)S(1)}, bf16[1024,256]{1,0:T(8,128)(2,1)S(1)}, u32[]{:S(2)}, u32[]{:S(2)}) %collective-permute-start.8) | collective-permute-done | bytes 524320 | tf_op jit(solution)/shard_map/ppermute | solution.py:43
  28.2 1.7 collective-permute-start.10
  30.0 1.4 collective-permute-start.9
  31.4 2.7 %collective-permute-start.4 = (bf16[1024,256]{1,0:T(8,128)(2,1)S(1)}, bf16[1024,256]{1,0:T(8,128)(2,1)S(1)}, u32[]{:S(2)}, u32[]{:S(2)}) collective-permute-start(bf16[1024,256]{1,0:T(8,128)(2,1)S(1)} %collective-permute-done.2.refs_2_), channel_id=1, source_target_pairs={{0,96},{16,112},{32,0},{48,16},{64,32},{80,48},{96,64},{112,80},{1... | collective-permute-start | bytes 1572872 | tf_op jit(solution)/shard_map/ppermute | solution.py:43
  34.2 5.5 %collective-permute-done.7.refs_13_ = bf16[1024,256]{1,0:T(8,128)(2,1)} collective-permute-done((bf16[1024,256]{1,0:T(8,128)(2,1)S(1)}, bf16[1024,256]{1,0:T(8,128)(2,1)}, u32[]{:S(2)}, u32[]{:S(2)}) %collective-permute-start.7) | collective-permute-done | bytes 524320 | tf_op jit(solution)/shard_map/ppermute | solution.py:43
  39.7 1.3 collective-permute-start.5
  41.0 9.9 %collective-permute-done.10.refs_12_ = bf16[1024,256]{1,0:T(8,128)(2,1)} collective-permute-done((bf16[1024,256]{1,0:T(8,128)(2,1)S(1)}, bf16[1024,256]{1,0:T(8,128)(2,1)}, u32[]{:S(2)}, u32[]{:S(2)}) %collective-permute-start.10) | collective-permute-done | bytes 524320 | tf_op jit(solution)/shard_map/ppermute | solution.py:43
  51.0 2.7 %collective-permute-start.12 = (bf16[1024,256]{1,0:T(8,128)(2,1)}, bf16[1024,256]{1,0:T(8,128)(2,1)}, u32[]{:S(2)}, u32[]{:S(2)}) collective-permute-start(bf16[1024,256]{1,0:T(8,128)(2,1)} %collective-permute-done.9.refs_9_), channel_id=1, source_target_pairs={{0,96},{16,112},{32,0},{48,16},{64,32},{80,48},{96,64},{112,80},{1... | collective-permute-start | bytes 1572872 | tf_op jit(solution)/shard_map/ppermute | solution.py:43
  54.4 1.3 add_bitcast_fusion.src
  57.9 10.1 %all-to-all-start = ((s32[16,1,8]{2,1,0:T(1,128)}), s32[16,1,8]{2,1,0:T(1,128)S(1)}, u32[]{:S(2)}, u32[]{:S(2)}) async-start(s32[16,1,8]{2,1,0:T(1,128)} %bitcast.3), calls=%async_computation | async-start | bytes 16384 | tf_op jit(solution)/shard_map/all_to_all | solution.py:69
  68.1 11.0 %products.1 = bf16[16384,256]{1,0:T(8,128)(2,1)} custom-call(s32[128]{0:T(128)} %add_bitcast_fusion.src, bf16[128,128,128]{2,1,0:T(8,128)(2,1)} %bitcast.26, bf16[2048,256]{1,0:T(8,128)(2,1)} %refs_0_.1, bf16[1024,256]{1,0:T(8,128)(2,1)} %copy-done.4, bf16[1024,256]{1,0:T(8,128)(2,1)} %copy-done.3, bf16[1024,256]{1,0:T(8,128)(2,1)} %copy-done.6, ...), custom_call_target="tpu_custom_call" | custom-call | tf_op jit(solution)/shard_map/products/pallas_call | solution.py:123
  79.1 103.2 %all_to_all.10 = bf16[16,1024,256]{2,1,0:T(8,128)(2,1)} all-to-all(bf16[16,1024,256]{2,1,0:T(8,128)(2,1)} %bitcast.24), channel_id=1, replica_groups=mesh['row'=8,'col'=16] {'col'}, dimensions={0} | all-to-all | bytes 16777216 | tf_op jit(solution)/shard_map/all_to_all | solution.py:331
  182.3 5.8 %sum_and_gram.1 = (f32[2048,256]{1,0:T(8,128)S(1)}, f32[8,48,128]{2,1,0:T(8,128)S(1)}) custom-call(s32[16,1,8]{2,1,0:T(1,128)S(1)} %all-to-all-done.place, s32[2]{0:T(128)S(1)} %pad_add_fusion.me, bf16[16384,256]{1,0:T(8,128)(2,1)} %bitcast.25), custom_call_target="tpu_custom_call" | custom-call | tf_op jit(solution)/shard_map/sum_and_gram/pallas_call | solution.py:180
  188.2 1.3 collective-permute-start.13
  190.8 0.9 collective-permute-start.16
  192.3 2.5 %collective-permute-done.15 = f32[48,128]{1,0:T(8,128)S(1)} collective-permute-done((f32[48,128]{1,0:T(8,128)S(1)}, f32[48,128]{1,0:T(8,128)S(1)}, u32[]{:S(2)}, u32[]{:S(2)}) %collective-permute-start.15) | collective-permute-done | bytes 24608 | tf_op jit(solution)/shard_map/ppermute | solution.py:38
  194.7 1.1 collective-permute-done.14
  196.4 1.2 collective-permute-start.18
  198.6 1.9 collective-permute-done.18
  201.5 3.5 %collective-permute-start.22 = (f32[48,128]{1,0:T(8,128)S(1)}, f32[48,128]{1,0:T(8,128)S(1)}, u32[]{:S(2)}, u32[]{:S(2)}) collective-permute-start(f32[48,128]{1,0:T(8,128)S(1)} %add_add_fusion.1), channel_id=1, source_target_pairs={{0,96},{1,97},{2,98},{3,99},{4,100},{5,101},{6,102},{7,103},{16,11... | collective-permute-start | bytes 73736 | tf_op jit(solution)/shard_map/ppermute | solution.py:38
  205.9 3.2 %collective-permute-done.21 = f32[48,128]{1,0:T(8,128)S(1)} collective-permute-done((f32[48,128]{1,0:T(8,128)S(1)}, f32[48,128]{1,0:T(8,128)S(1)}, u32[]{:S(2)}, u32[]{:S(2)}) %collective-permute-start.21) | collective-permute-done | bytes 24608 | tf_op jit(solution)/shard_map/ppermute | solution.py:38
  209.2 2.1 collective-permute-start.24
  211.9 1.5 collective-permute-done.25
  214.0 6.7 %collective-permute-start.26 = (f32[4,48,128]{2,1,0:T(8,128)S(1)}, f32[4,48,128]{2,1,0:T(8,128)S(1)}, u32[]{:S(2)}, u32[]{:S(2)}) collective-permute-start(f32[4,48,128]{2,1,0:T(8,128)S(1)} %pad_maximum_fusion.mine), channel_id=1, source_target_pairs={{0,1},{1,0},{2,3},{3,2},{4,5},{5,4},{6,7},{7,6},{16,17},{17,16},{1... | collective-permute-start | bytes 294920 | tf_op jit(solution)/shard_map/ppermute | solution.py:38
  221.7 9.9 %finish.1 = (f32[2048,256]{1,0:T(8,128)}, f32[256,256]{1,0:T(8,128)}) custom-call(s32[2]{0:T(128)S(1)} %pad_add_fusion.me, f32[4,48,128]{2,1,0:T(8,128)S(1)} %pad_maximum_fusion.mine, f32[4,48,128]{2,1,0:T(8,128)S(1)} %collective-permute-done.26.other, f32[2048,256]{1,0:T(8,128)S(1)} %get-tuple-element.27.summed_hbm), custom_call_target="tpu_custom_call" | custom-call | tf_op jit(solution)/shard_map/finish/pallas_call | solution.py:293
  (54 shorter events, 10.7 us)
Async XLA Ops:
  0.6 29.4 %collective-permute-start = (bf16[2048,256]{1,0:T(8,128)(2,1)}, bf16[2048,256]{1,0:T(8,128)(2,1)S(1)}, u32[]{:S(2)}, u32[]{:S(2)}) collective-permute-start(bf16[2048,256]{1,0:T(8,128)(2,1)} %refs_0_.1), channel_id=1, source_target_pairs={{0,32},{16,48},{32,64},{48,80},{64,96},{80,112},{96,0},{112,16},{1... | collective-permute-start | bytes 3145736 | tf_op jit(solution)/shard_map/ppermute | solution.py:43
  4.4 12.6 %collective-permute-start.6 = (bf16[1024,256]{1,0:T(8,128)(2,1)S(1)}, bf16[1024,256]{1,0:T(8,128)(2,1)S(1)}, u32[]{:S(2)}, u32[]{:S(2)}) collective-permute-start(bf16[1024,256]{1,0:T(8,128)(2,1)S(1)} %get-tuple-element.28), channel_id=1, source_target_pairs={{0,16},{16,0},{32,48},{48,32},{64,80},{80,64},{96,112},{112,96},{1... | collective-permute-start | bytes 1572872 | tf_op jit(solution)/shard_map/ppermute | solution.py:43
  5.8 22.4 %collective-permute-start.8 = (bf16[1024,256]{1,0:T(8,128)(2,1)S(1)}, bf16[1024,256]{1,0:T(8,128)(2,1)S(1)}, u32[]{:S(2)}, u32[]{:S(2)}) collective-permute-start(bf16[1024,256]{1,0:T(8,128)(2,1)S(1)} %get-tuple-element.29), channel_id=1, source_target_pairs={{0,16},{16,0},{32,48},{48,32},{64,80},{80,64},{96,112},{112,96},{1... | collective-permute-start | bytes 1572872 | tf_op jit(solution)/shard_map/ppermute | solution.py:43
  6.0 24.0 %collective-permute-start.2 = (bf16[1024,256]{1,0:T(8,128)(2,1)S(1)}, bf16[1024,256]{1,0:T(8,128)(2,1)S(1)}, u32[]{:S(2)}, u32[]{:S(2)}) collective-permute-start(bf16[1024,256]{1,0:T(8,128)(2,1)S(1)} %get-tuple-element.28), channel_id=1, source_target_pairs={{0,96},{16,112},{32,0},{48,16},{64,32},{80,48},{96,64},{112,80},{1... | collective-permute-start | bytes 1572872 | tf_op jit(solution)/shard_map/ppermute | solution.py:43
  8.1 21.9 %collective-permute-start.1 = (bf16[1024,256]{1,0:T(8,128)(2,1)S(1)}, bf16[1024,256]{1,0:T(8,128)(2,1)S(1)}, u32[]{:S(2)}, u32[]{:S(2)}) collective-permute-start(bf16[1024,256]{1,0:T(8,128)(2,1)S(1)} %get-tuple-element.29), channel_id=1, source_target_pairs={{0,96},{16,112},{32,0},{48,16},{64,32},{80,48},{96,64},{112,80},{1... | collective-permute-start | bytes 1572872 | tf_op jit(solution)/shard_map/ppermute | solution.py:43
  17.0 51.0 %copy-start.1 = (bf16[1024,256]{1,0:T(8,128)(2,1)}, bf16[1024,256]{1,0:T(8,128)(2,1)S(1)}, u32[]{:S(2)}) copy-start(bf16[1024,256]{1,0:T(8,128)(2,1)S(1)} %collective-permute-done.6.refs_7_) | copy-start | bytes 1572868
  17.0 22.7 %collective-permute-start.7 = (bf16[1024,256]{1,0:T(8,128)(2,1)S(1)}, bf16[1024,256]{1,0:T(8,128)(2,1)}, u32[]{:S(2)}, u32[]{:S(2)}) collective-permute-start(bf16[1024,256]{1,0:T(8,128)(2,1)S(1)} %collective-permute-done.6.refs_7_), channel_id=1, source_target_pairs={{0,32},{16,48},{32,64},{48,80},{64,96},{80,112},{96,0},{112,16},{1... | collective-permute-start | bytes 1572872 | tf_op jit(solution)/shard_map/ppermute | solution.py:43
  28.2 39.8 %copy-start.2 = (bf16[1024,256]{1,0:T(8,128)(2,1)}, bf16[1024,256]{1,0:T(8,128)(2,1)S(1)}, u32[]{:S(2)}) copy-start(bf16[1024,256]{1,0:T(8,128)(2,1)S(1)} %collective-permute-done.8.refs_6_) | copy-start | bytes 1572868
  28.2 22.7 %collective-permute-start.10 = (bf16[1024,256]{1,0:T(8,128)(2,1)S(1)}, bf16[1024,256]{1,0:T(8,128)(2,1)}, u32[]{:S(2)}, u32[]{:S(2)}) collective-permute-start(bf16[1024,256]{1,0:T(8,128)(2,1)S(1)} %collective-permute-done.8.refs_6_), channel_id=1, source_target_pairs={{0,32},{16,48},{32,64},{48,80},{64,96},{80,112},{96,0},{112,16},{1... | collective-permute-start | bytes 1572872 | tf_op jit(solution)/shard_map/ppermute | solution.py:43
  30.0 38.1 %copy-start.3 = (bf16[1024,256]{1,0:T(8,128)(2,1)}, bf16[1024,256]{1,0:T(8,128)(2,1)S(1)}, u32[]{:S(2)}) copy-start(bf16[1024,256]{1,0:T(8,128)(2,1)S(1)} %collective-permute-done.2.refs_2_) | copy-start | bytes 1572868
  30.0 38.1 %copy-start.4 = (bf16[1024,256]{1,0:T(8,128)(2,1)}, bf16[1024,256]{1,0:T(8,128)(2,1)S(1)}, u32[]{:S(2)}) copy-start(bf16[1024,256]{1,0:T(8,128)(2,1)S(1)} %collective-permute-done.1.refs_1_) | copy-start | bytes 1572868
  30.0 21.0 %collective-permute-start.9 = (bf16[1024,256]{1,0:T(8,128)(2,1)S(1)}, bf16[1024,256]{1,0:T(8,128)(2,1)}, u32[]{:S(2)}, u32[]{:S(2)}) collective-permute-start(bf16[1024,256]{1,0:T(8,128)(2,1)S(1)} %collective-permute-done.2.refs_2_), channel_id=1, source_target_pairs={{0,16},{16,0},{32,48},{48,32},{64,80},{80,64},{96,112},{112,96},{1... | collective-permute-start | bytes 1572872 | tf_op jit(solution)/shard_map/ppermute | solution.py:43
  31.4 24.2 %collective-permute-start.4 = (bf16[1024,256]{1,0:T(8,128)(2,1)S(1)}, bf16[1024,256]{1,0:T(8,128)(2,1)S(1)}, u32[]{:S(2)}, u32[]{:S(2)}) collective-permute-start(bf16[1024,256]{1,0:T(8,128)(2,1)S(1)} %collective-permute-done.2.refs_2_), channel_id=1, source_target_pairs={{0,96},{16,112},{32,0},{48,16},{64,32},{80,48},{96,64},{112,80},{1... | collective-permute-start | bytes 1572872 | tf_op jit(solution)/shard_map/ppermute | solution.py:43
  34.1 21.5 %collective-permute-start.3 = (bf16[1024,256]{1,0:T(8,128)(2,1)S(1)}, bf16[1024,256]{1,0:T(8,128)(2,1)S(1)}, u32[]{:S(2)}, u32[]{:S(2)}) collective-permute-start(bf16[1024,256]{1,0:T(8,128)(2,1)S(1)} %collective-permute-done.1.refs_1_), channel_id=1, source_target_pairs={{0,96},{16,112},{32,0},{48,16},{64,32},{80,48},{96,64},{112,80},{1... | collective-permute-start | bytes 1572872 | tf_op jit(solution)/shard_map/ppermute | solution.py:43
  39.7 17.5 %collective-permute-start.5 = (bf16[1024,256]{1,0:T(8,128)(2,1)S(1)}, bf16[1024,256]{1,0:T(8,128)(2,1)}, u32[]{:S(2)}, u32[]{:S(2)}) collective-permute-start(bf16[1024,256]{1,0:T(8,128)(2,1)S(1)} %collective-permute-done.1.refs_1_), channel_id=1, source_target_pairs={{0,16},{16,0},{32,48},{48,32},{64,80},{80,64},{96,112},{112,96},{1... | collective-permute-start | bytes 1572872 | tf_op jit(solution)/shard_map/ppermute | solution.py:43
  51.0 17.0 %collective-permute-start.11 = (bf16[1024,256]{1,0:T(8,128)(2,1)}, bf16[1024,256]{1,0:T(8,128)(2,1)}, u32[]{:S(2)}, u32[]{:S(2)}) collective-permute-start(bf16[1024,256]{1,0:T(8,128)(2,1)} %collective-permute-done.10.refs_12_), channel_id=1, source_target_pairs={{0,32},{16,48},{32,64},{48,80},{64,96},{80,112},{96,0},{112,16},{1... | collective-permute-start | bytes 1572872 | tf_op jit(solution)/shard_map/ppermute | solution.py:43
  51.0 17.0 %collective-permute-start.12 = (bf16[1024,256]{1,0:T(8,128)(2,1)}, bf16[1024,256]{1,0:T(8,128)(2,1)}, u32[]{:S(2)}, u32[]{:S(2)}) collective-permute-start(bf16[1024,256]{1,0:T(8,128)(2,1)} %collective-permute-done.9.refs_9_), channel_id=1, source_target_pairs={{0,96},{16,112},{32,0},{48,16},{64,32},{80,48},{96,64},{112,80},{1... | collective-permute-start | bytes 1572872 | tf_op jit(solution)/shard_map/ppermute | solution.py:43
  57.9 21.2 %all-to-all-start = ((s32[16,1,8]{2,1,0:T(1,128)}), s32[16,1,8]{2,1,0:T(1,128)S(1)}, u32[]{:S(2)}, u32[]{:S(2)}) async-start(s32[16,1,8]{2,1,0:T(1,128)} %bitcast.3), calls=%async_computation | async-start | bytes 16384 | tf_op jit(solution)/shard_map/all_to_all | solution.py:69
  188.2 2.3 collective-permute-start.13
  190.5 4.3 %collective-permute-start.15 = (f32[48,128]{1,0:T(8,128)S(1)}, f32[48,128]{1,0:T(8,128)S(1)}, u32[]{:S(2)}, u32[]{:S(2)}) collective-permute-start(f32[48,128]{1,0:T(8,128)S(1)} %get-tuple-element.30), channel_id=1, source_target_pairs={{0,4},{1,5},{2,6},{3,7},{4,0},{5,1},{6,2},{7,3},{16,20},{17,21},{1... | collective-permute-start | bytes 73736 | tf_op jit(solution)/shard_map/ppermute | solution.py:38
  190.8 3.9 %collective-permute-start.16 = (f32[48,128]{1,0:T(8,128)S(1)}, f32[48,128]{1,0:T(8,128)S(1)}, u32[]{:S(2)}, u32[]{:S(2)}) collective-permute-start(f32[48,128]{1,0:T(8,128)S(1)} %get-tuple-element.31), channel_id=1, source_target_pairs={{0,6},{1,7},{2,0},{3,1},{4,2},{5,3},{6,4},{7,5},{16,22},{17,23},{1... | collective-permute-start | bytes 73736 | tf_op jit(solution)/shard_map/ppermute | solution.py:38
  191.7 4.1 %collective-permute-start.14 = (f32[48,128]{1,0:T(8,128)S(1)}, f32[48,128]{1,0:T(8,128)S(1)}, u32[]{:S(2)}, u32[]{:S(2)}) collective-permute-start(f32[48,128]{1,0:T(8,128)S(1)} %get-tuple-element.32), channel_id=1, source_target_pairs={{0,2},{1,3},{2,4},{3,5},{4,6},{5,7},{6,0},{7,1},{16,18},{17,19},{1... | collective-permute-start | bytes 73736 | tf_op jit(solution)/shard_map/ppermute | solution.py:38
  195.9 2.7 %collective-permute-start.19 = (f32[48,128]{1,0:T(8,128)S(1)}, f32[48,128]{1,0:T(8,128)S(1)}, u32[]{:S(2)}, u32[]{:S(2)}) collective-permute-start(f32[48,128]{1,0:T(8,128)S(1)} %fusion), channel_id=1, source_target_pairs={{0,24},{1,25},{2,26},{3,27},{4,28},{5,29},{6,30},{7,31},{16,0},{17... | collective-permute-start | bytes 73736 | tf_op jit(solution)/shard_map/ppermute | solution.py:38
  196.4 4.2 %collective-permute-start.18 = (f32[48,128]{1,0:T(8,128)S(1)}, f32[48,128]{1,0:T(8,128)S(1)}, u32[]{:S(2)}, u32[]{:S(2)}) collective-permute-start(f32[48,128]{1,0:T(8,128)S(1)} %fusion), channel_id=1, source_target_pairs={{0,8},{1,9},{2,10},{3,11},{4,12},{5,13},{6,14},{7,15},{16,24},{17,... | collective-permute-start | bytes 73736 | tf_op jit(solution)/shard_map/ppermute | solution.py:38
  197.6 3.9 %collective-permute-start.17 = (f32[48,128]{1,0:T(8,128)S(1)}, f32[48,128]{1,0:T(8,128)S(1)}, u32[]{:S(2)}, u32[]{:S(2)}) collective-permute-start(f32[48,128]{1,0:T(8,128)S(1)} %fusion), channel_id=1, source_target_pairs={{0,16},{1,17},{2,18},{3,19},{4,20},{5,21},{6,22},{7,23},{16,8},{17... | collective-permute-start | bytes 73736 | tf_op jit(solution)/shard_map/ppermute | solution.py:38
  201.5 4.4 %collective-permute-start.22 = (f32[48,128]{1,0:T(8,128)S(1)}, f32[48,128]{1,0:T(8,128)S(1)}, u32[]{:S(2)}, u32[]{:S(2)}) collective-permute-start(f32[48,128]{1,0:T(8,128)S(1)} %add_add_fusion.1), channel_id=1, source_target_pairs={{0,96},{1,97},{2,98},{3,99},{4,100},{5,101},{6,102},{7,103},{16,11... | collective-permute-start | bytes 73736 | tf_op jit(solution)/shard_map/ppermute | solution.py:38
  205.0 4.2 %collective-permute-start.21 = (f32[48,128]{1,0:T(8,128)S(1)}, f32[48,128]{1,0:T(8,128)S(1)}, u32[]{:S(2)}, u32[]{:S(2)}) collective-permute-start(f32[48,128]{1,0:T(8,128)S(1)} %add_add_fusion.1), channel_id=1, source_target_pairs={{0,64},{1,65},{2,66},{3,67},{4,68},{5,69},{6,70},{7,71},{16,80},{1... | collective-permute-start | bytes 73736 | tf_op jit(solution)/shard_map/ppermute | solution.py:38
  205.0 4.2 %collective-permute-start.20 = (f32[48,128]{1,0:T(8,128)S(1)}, f32[48,128]{1,0:T(8,128)S(1)}, u32[]{:S(2)}, u32[]{:S(2)}) collective-permute-start(f32[48,128]{1,0:T(8,128)S(1)} %add_add_fusion.1), channel_id=1, source_target_pairs={{0,32},{1,33},{2,34},{3,35},{4,36},{5,37},{6,38},{7,39},{16,48},{1... | collective-permute-start | bytes 73736 | tf_op jit(solution)/shard_map/ppermute | solution.py:38
  209.2 4.3 %collective-permute-start.25 = (f32[48,128]{1,0:T(8,128)S(1)}, f32[48,128]{1,0:T(8,128)S(1)}, u32[]{:S(2)}, u32[]{:S(2)}) collective-permute-start(f32[48,128]{1,0:T(8,128)S(1)} %add_add_fusion), channel_id=1, source_target_pairs={{0,2},{1,3},{2,4},{3,5},{4,6},{5,7},{6,0},{7,1},{16,18},{17,19},{1... | collective-permute-start | bytes 73736 | tf_op jit(solution)/shard_map/ppermute | solution.py:38
  209.2 4.3 %collective-permute-start.24 = (f32[48,128]{1,0:T(8,128)S(1)}, f32[48,128]{1,0:T(8,128)S(1)}, u32[]{:S(2)}, u32[]{:S(2)}) collective-permute-start(f32[48,128]{1,0:T(8,128)S(1)} %add_add_fusion), channel_id=1, source_target_pairs={{0,4},{1,5},{2,6},{3,7},{4,0},{5,1},{6,2},{7,3},{16,20},{17,21},{1... | collective-permute-start | bytes 73736 | tf_op jit(solution)/shard_map/ppermute | solution.py:38
  211.3 2.7 %collective-permute-start.23 = (f32[48,128]{1,0:T(8,128)S(1)}, f32[48,128]{1,0:T(8,128)S(1)}, u32[]{:S(2)}, u32[]{:S(2)}) collective-permute-start(f32[48,128]{1,0:T(8,128)S(1)} %add_add_fusion), channel_id=1, source_target_pairs={{0,6},{1,7},{2,0},{3,1},{4,2},{5,3},{6,4},{7,5},{16,22},{17,23},{1... | collective-permute-start | bytes 73736 | tf_op jit(solution)/shard_map/ppermute | solution.py:38
  214.0 7.6 %collective-permute-start.26 = (f32[4,48,128]{2,1,0:T(8,128)S(1)}, f32[4,48,128]{2,1,0:T(8,128)S(1)}, u32[]{:S(2)}, u32[]{:S(2)}) collective-permute-start(f32[4,48,128]{2,1,0:T(8,128)S(1)} %pad_maximum_fusion.mine), channel_id=1, source_target_pairs={{0,1},{1,0},{2,3},{3,2},{4,5},{5,4},{6,7},{7,6},{16,17},{17,16},{1... | collective-permute-start | bytes 294920 | tf_op jit(solution)/shard_map/ppermute | solution.py:38
  (3 other events, 39.6 us)

commit v4 on v3

--- a/solution.py
+++ b/solution.py
@@ -16,6 +16,7 @@
 ITEMS = 262144
 BOTH = ("row", "col")
 PARTS = 14
+LATE = (10, 11, 13, 12, 9, 8, 3, 4, 0)
 PANEL = 32
 PIECE = 48
 CHUNKS = 16
@@ -61,10 +62,10 @@
     below, above_a, above_b = together(below, above_a, above_b)
     beside_above_b = row_shifted(above_b, 0, 1)
     beside_above_a = row_shifted(above_a, 0, 1)
-    beside_across_a = row_shifted(beside_below_a, 1, 0)
-    beside_across_b = row_shifted(beside_above_b, -1, 0)
-    across_a, across_b, beside_above_a, beside_below_b, place = together(
-        across_a, across_b, beside_above_a, beside_below_b, place
+    beside_across_b = row_shifted(beside_below_b, 1, 0)
+    beside_across_a = row_shifted(beside_above_a, -1, 0)
+    across_a, across_b, beside_above_b, beside_below_a, place = together(
+        across_a, across_b, beside_above_b, beside_below_a, place
     )
     place = lax.all_to_all(place.reshape(N_COL, 1, PER_PEER), "col", 0, 0, tiled=True)
     parts = (
@@ -83,27 +84,24 @@
     return high, middle, low
 
 
-def product_kernel(src, tiles_hbm, *refs):
+def product_kernel(src, tiles, *refs):
     parts = refs[:PARTS]
-    out_hbm, tiles, column, out, tile_sems, part_sems, out_sems = refs[PARTS:]
-    loads = []
-    start = 0
-    for i, part in enumerate(parts):
-        rows = part.shape[0]
-        loads.append(pltpu.make_async_copy(part, column.at[pl.ds(start, rows)], part_sems.at[i]))
-        start += rows
-    share = TILE_DEV // CHUNKS
-    tile_loads = []
-    for g in range(CHUNKS):
-        here = pl.ds(g * share, share)
-        tile_loads.append(pltpu.make_async_copy(tiles_hbm.at[here], tiles.at[here], tile_sems.at[g]))
-    for load in loads + tile_loads:
+    out_hbm, column, out, part_sems, out_sems = refs[PARTS:]
+    starts = [sum(part.shape[0] for part in parts[:i]) for i in range(PARTS)]
+    places = [column.at[pl.ds(starts[i], parts[i].shape[0])] for i in range(PARTS)]
+    loads = [
+        pltpu.make_async_copy(parts[i], places[i], part_sems.at[k]) for k, i in enumerate(LATE)
+    ]
+    for load in loads:
         load.start()
+    for i in range(PARTS):
+        if i not in LATE:
+            places[i][...] = parts[i][...]
     for load in loads:
         load.wait()
+    share = TILE_DEV // CHUNKS
     stores = []
     for g in range(CHUNKS):
-        tile_loads[g].wait()
 
         @pl.loop(g * share, (g + 1) * share, unroll=8)
         def _(t):
@@ -123,39 +121,31 @@
     return pl.pallas_call(
         product_kernel,
         out_shape=jax.ShapeDtypeStruct((TILE_DEV * BLOCK, BASIS), jnp.bfloat16),
-        in_specs=[pl.BlockSpec(memory_space=pltpu.SMEM)]
-        + [pl.BlockSpec(memory_space=pltpu.HBM)] * (1 + PARTS),
+        in_specs=[pl.BlockSpec(memory_space=pltpu.SMEM), pl.BlockSpec(memory_space=pltpu.VMEM)]
+        + [
+            pl.BlockSpec(memory_space=pltpu.HBM if i in LATE else pltpu.VMEM)
+            for i in range(PARTS)
+        ],
         out_specs=pl.BlockSpec(memory_space=pltpu.HBM),
         scratch_shapes=[
-            pltpu.VMEM((TILE_DEV, BLOCK, BLOCK), jnp.bfloat16),
             pltpu.VMEM((N_ROW * ROWS_DEV, BASIS), jnp.bfloat16),
             pltpu.VMEM((TILE_DEV * BLOCK, BASIS), jnp.bfloat16),
+            pltpu.SemaphoreType.DMA((len(LATE),)),
             pltpu.SemaphoreType.DMA((CHUNKS,)),
-            pltpu.SemaphoreType.DMA((PARTS,)),
-            pltpu.SemaphoreType.DMA((CHUNKS,)),
-        ],
-        compiler_params=pltpu.CompilerParams(vmem_limit_bytes=56 * 1024 * 1024),
+        ],
+        compiler_params=pltpu.CompilerParams(vmem_limit_bytes=53 * 1024 * 1024),
         name="products",
     )(src, tiles, *parts)
 
 
-def sum_kernel(place, me, products_hbm, summed_hbm, gram, products, summed, packed, in_sems, out_sem):
-    share = TILE_DEV // CHUNKS
-    loads = []
-    for g in range(CHUNKS):
-        here = pl.ds(g * share * BLOCK, share * BLOCK)
-        loads.append(pltpu.make_async_copy(products_hbm.at[here], products.at[here], in_sems.at[g]))
-    for load in loads:
-        load.start()
+def sum_kernel(place, me, products, summed_hbm, gram, summed, packed, out_sem):
     summed[...] = jnp.zeros_like(summed)
-    for g in range(CHUNKS):
-        loads[g].wait()
-
-        @pl.loop(g * share, (g + 1) * share, unroll=4)
-        def _(t):
-            rows = pl.ds(pl.multiple_of(place[t >> 3, 0, t & 7] * BLOCK, BLOCK), BLOCK)
-            product = products[pl.ds(pl.multiple_of(t * BLOCK, BLOCK), BLOCK), :]
-            summed[rows, :] += product.astype(jnp.float32)
+
+    @pl.loop(0, TILE_DEV, unroll=8)
+    def _(t):
+        rows = pl.ds(pl.multiple_of(place[t >> 3, 0, t & 7] * BLOCK, BLOCK), BLOCK)
+        product = products[pl.ds(pl.multiple_of(t * BLOCK, BLOCK), BLOCK), :]
+        summed[rows, :] += product.astype(jnp.float32)
 
     store = pltpu.make_async_copy(summed, summed_hbm, out_sem)
     store.start()
@@ -184,16 +174,14 @@
             jax.ShapeDtypeStruct((8, PIECE, BLOCK), jnp.float32),
         ),
         in_specs=[pl.BlockSpec(memory_space=pltpu.SMEM)] * 2
-        + [pl.BlockSpec(memory_space=pltpu.HBM)],
+        + [pl.BlockSpec(memory_space=pltpu.VMEM)],
         out_specs=(pl.BlockSpec(memory_space=pltpu.HBM), pl.BlockSpec(memory_space=pltpu.VMEM)),
         scratch_shapes=[
-            pltpu.VMEM((TILE_DEV * BLOCK, BASIS), jnp.bfloat16),
             pltpu.VMEM((ROWS_DEV, BASIS), jnp.float32),
             pltpu.VMEM((3 * BLOCK, BLOCK), jnp.float32),
-            pltpu.SemaphoreType.DMA((CHUNKS,)),
             pltpu.SemaphoreType.DMA,
         ],
-        compiler_params=pltpu.CompilerParams(vmem_limit_bytes=48 * 1024 * 1024),
+        compiler_params=pltpu.CompilerParams(vmem_limit_bytes=32 * 1024 * 1024),
         name="sum_and_gram",
     )(place, me, products)
 

time: 232 us -> 226 us (0.974)
  waiting for transfers between devices: 47.1 us -> 43.3 us
  Pallas kernels: 26.7 us -> 23.2 us
    ppermute x13, waiting for transfers between devices: 32.5 us -> 28.8 us  [row_shifted(): return lax.ppermute(value, 'row', pairs)]
  transfers between devices with their start and end apart: 28 -> 28, of which waited for: 16 -> 19; matrix products, arithmetic and copies ran while one was open for 2% -> 2% of each run, Pallas kernels for 5% -> 4%
where the time goes in v4:
time: 226 us; the launch traced here: 225 us
  blocking collectives  104 us (46%)
  starting transfers between devices  49 us (22%)
  waiting for transfers between devices  43.3 us (19%)
  Pallas kernels  23.2 us (10%)
  local copies, waits for them, and re-layouts  3.56 us (2%)
    all_to_all x1, blocking collectives, local(): lax.all_to_all(products.reshape(N_COL, PER_PEER * BLOCK, BASIS), 'col', 0...  104 us
    ppermute x13, waiting for transfers between devices, row_shifted(): return lax.ppermute(value, 'row', pairs)  28.8 us
    ppermute x13, starting transfers between devices, row_shifted(): return lax.ppermute(value, 'row', pairs)  20.2 us
    ppermute x14, starting transfers between devices, shifted(): return lax.ppermute(value, BOTH, pairs)  18.9 us
    ppermute x14, waiting for transfers between devices, shifted(): return lax.ppermute(value, BOTH, pairs)  14.5 us
    all_to_all x1, starting transfers between devices, gather_column(): lax.all_to_all(place.reshape(N_COL, 1, PER_PEER), 'col', 0, 0, tiled=True)  9.93 us
    pallas_call x1, Pallas kernels, finish(): pl.pallas_call(finish_kernel, out_shape=(jax.ShapeDtypeStruct((ROWS_DEV,...  9.87 us
    pallas_call x1, Pallas kernels, make_products(): pl.pallas_call(product_kernel, out_shape=jax.ShapeDtypeStruct((TILE_DEV *...  9.2 us
  transfers between devices with their start and end apart: 28, of which 19 were waited for; matrix products, arithmetic and copies ran while one was open for 2% of the time, Pallas kernels for 4%

profile of v4, /device:TPU:1, one launch (start us, length us, event | category | flops | bytes accessed | tf_op | source)
XLA Modules:
  0.0 225.3 jit_solution(7016817767946802699)
XLA Ops:
  0.6 2.5 %collective-permute-start = (bf16[2048,256]{1,0:T(8,128)(2,1)}, bf16[2048,256]{1,0:T(8,128)(2,1)S(1)}, u32[]{:S(2)}, u32[]{:S(2)}) collective-permute-start(bf16[2048,256]{1,0:T(8,128)(2,1)} %refs_0_.1), channel_id=1, source_target_pairs={{0,32},{16,48},{32,64},{48,80},{64,96},{80,112},{96,0},{112,16},{1... | collective-permute-start | bytes 3145736 | tf_op jit(solution)/shard_map/ppermute | solution.py:44
  3.2 2.1 fusion.1
  5.2 1.3 collective-permute-start.8
  6.5 2.1 collective-permute-start.2
  8.7 1.4 collective-permute-start.1
  10.3 7.4 %collective-permute-done.8.refs_7_ = bf16[1024,256]{1,0:T(8,128)(2,1)S(1)} collective-permute-done((bf16[1024,256]{1,0:T(8,128)(2,1)S(1)}, bf16[1024,256]{1,0:T(8,128)(2,1)S(1)}, u32[]{:S(2)}, u32[]{:S(2)}) %collective-permute-start.8) | collective-permute-done | bytes 524320 | tf_op jit(solution)/shard_map/ppermute | solution.py:44
  17.7 1.6 collective-permute-start.11
  19.3 3.0 %collective-permute-start.4 = (bf16[1024,256]{1,0:T(8,128)(2,1)S(1)}, bf16[1024,256]{1,0:T(8,128)(2,1)}, u32[]{:S(2)}, u32[]{:S(2)}) collective-permute-start(bf16[1024,256]{1,0:T(8,128)(2,1)S(1)} %collective-permute-done.2.refs_2_), channel_id=1, source_target_pairs={{0,96},{16,112},{32,0},{48,16},{64,32},{80,48},{96,64},{112,80},{1... | collective-permute-start | bytes 1572872 | tf_op jit(solution)/shard_map/ppermute | solution.py:44
  22.3 8.0 %collective-permute-done.1.refs_1_ = bf16[1024,256]{1,0:T(8,128)(2,1)S(1)} collective-permute-done((bf16[1024,256]{1,0:T(8,128)(2,1)}, bf16[1024,256]{1,0:T(8,128)(2,1)S(1)}, u32[]{:S(2)}, u32[]{:S(2)}) %collective-permute-start.1) | collective-permute-done | bytes 524320 | tf_op jit(solution)/shard_map/ppermute | solution.py:44
  30.5 3.3 %collective-permute-start.3 = (bf16[1024,256]{1,0:T(8,128)(2,1)S(1)}, bf16[1024,256]{1,0:T(8,128)(2,1)S(1)}, u32[]{:S(2)}, u32[]{:S(2)}) collective-permute-start(bf16[1024,256]{1,0:T(8,128)(2,1)S(1)} %collective-permute-done.1.refs_1_), channel_id=1, source_target_pairs={{0,96},{16,112},{32,0},{48,16},{64,32},{80,48},{96,64},{112,80},{1... | collective-permute-start | bytes 1572872 | tf_op jit(solution)/shard_map/ppermute | solution.py:44
  33.8 6.0 %collective-permute-done.11.refs_13_ = bf16[1024,256]{1,0:T(8,128)(2,1)} collective-permute-done((bf16[1024,256]{1,0:T(8,128)(2,1)S(1)}, bf16[1024,256]{1,0:T(8,128)(2,1)}, u32[]{:S(2)}, u32[]{:S(2)}) %collective-permute-start.11) | collective-permute-done | bytes 524320 | tf_op jit(solution)/shard_map/ppermute | solution.py:44
  39.7 1.3 collective-permute-start.5
  41.6 1.3 collective-permute-start.12
  42.9 2.0 collective-permute-start.10
  46.3 3.7 %collective-permute-done.7.refs_12_ = bf16[1024,256]{1,0:T(8,128)(2,1)S(1)} collective-permute-done((bf16[1024,256]{1,0:T(8,128)(2,1)S(1)}, bf16[1024,256]{1,0:T(8,128)(2,1)S(1)}, u32[]{:S(2)}, u32[]{:S(2)}) %collective-permute-start.7) | collective-permute-done | bytes 524320 | tf_op jit(solution)/shard_map/ppermute | solution.py:44
  50.0 2.8 %collective-permute-done.3.refs_3_ = bf16[1024,256]{1,0:T(8,128)(2,1)S(1)} collective-permute-done((bf16[1024,256]{1,0:T(8,128)(2,1)S(1)}, bf16[1024,256]{1,0:T(8,128)(2,1)S(1)}, u32[]{:S(2)}, u32[]{:S(2)}) %collective-permute-start.3) | collective-permute-done | bytes 524320 | tf_op jit(solution)/shard_map/ppermute | solution.py:44
  54.5 9.9 %all-to-all-start = ((s32[16,1,8]{2,1,0:T(1,128)}), s32[16,1,8]{2,1,0:T(1,128)S(1)}, u32[]{:S(2)}, u32[]{:S(2)}) async-start(s32[16,1,8]{2,1,0:T(1,128)} %bitcast.3), calls=%async_computation | async-start | bytes 16384 | tf_op jit(solution)/shard_map/all_to_all | solution.py:70
  64.5 9.2 %products.1 = bf16[16384,256]{1,0:T(8,128)(2,1)} custom-call(s32[128]{0:T(128)S(1)} %add_bitcast_fusion.src, bf16[128,128,128]{2,1,0:T(8,128)(2,1)} %bitcast.26, bf16[2048,256]{1,0:T(8,128)(2,1)} %refs_0_.1, bf16[1024,256]{1,0:T(8,128)(2,1)S(1)} %collective-permute-done.1.refs_1_, bf16[1024,256]{1,0:T(8,128)(2,1)} %copy-done.2, bf16[1024,256]{1,0:T(8,128)(2,1)} %copy-done.4, ...), custom_call_target="tpu_custom_call" | custom-call | tf_op jit(solution)/shard_map/products/pallas_call | solution.py:121
  73.7 103.9 %all_to_all.10 = bf16[16,1024,256]{2,1,0:T(8,128)(2,1)S(1)} all-to-all(bf16[16,1024,256]{2,1,0:T(8,128)(2,1)} %bitcast.25), channel_id=1, replica_groups=mesh['row'=8,'col'=16] {'col'}, dimensions={0} | all-to-all | bytes 16777216 | tf_op jit(solution)/shard_map/all_to_all | solution.py:319
  177.6 4.1 %sum_and_gram.1 = (f32[2048,256]{1,0:T(8,128)S(1)}, f32[8,48,128]{2,1,0:T(8,128)S(1)}) custom-call(s32[16,1,8]{2,1,0:T(1,128)S(1)} %all-to-all-done.place, s32[2]{0:T(128)S(1)} %pad_add_fusion.me, bf16[16384,256]{1,0:T(8,128)(2,1)S(1)} %bitcast.24), custom_call_target="tpu_custom_call" | custom-call | tf_op jit(solution)/shard_map/sum_and_gram/pallas_call | solution.py:170
  181.7 1.2 collective-permute-start.13
  184.2 1.0 collective-permute-start.16
  185.7 2.5 %collective-permute-done.15 = f32[48,128]{1,0:T(8,128)S(1)} collective-permute-done((f32[48,128]{1,0:T(8,128)S(1)}, f32[48,128]{1,0:T(8,128)S(1)}, u32[]{:S(2)}, u32[]{:S(2)}) %collective-permute-start.15) | collective-permute-done | bytes 24608 | tf_op jit(solution)/shard_map/ppermute | solution.py:39
  188.1 1.1 collective-permute-done.14
  189.8 1.2 collective-permute-start.18
  192.0 1.9 collective-permute-done.18
  194.9 3.4 %collective-permute-start.22 = (f32[48,128]{1,0:T(8,128)S(1)}, f32[48,128]{1,0:T(8,128)S(1)}, u32[]{:S(2)}, u32[]{:S(2)}) collective-permute-start(f32[48,128]{1,0:T(8,128)S(1)} %add_add_fusion.1), channel_id=1, source_target_pairs={{0,96},{1,97},{2,98},{3,99},{4,100},{5,101},{6,102},{7,103},{16,11... | collective-permute-start | bytes 73736 | tf_op jit(solution)/shard_map/ppermute | solution.py:39
  199.2 3.3 %collective-permute-done.21 = f32[48,128]{1,0:T(8,128)S(1)} collective-permute-done((f32[48,128]{1,0:T(8,128)S(1)}, f32[48,128]{1,0:T(8,128)S(1)}, u32[]{:S(2)}, u32[]{:S(2)}) %collective-permute-start.21) | collective-permute-done | bytes 24608 | tf_op jit(solution)/shard_map/ppermute | solution.py:39
  202.6 2.1 collective-permute-start.24
  205.3 1.5 collective-permute-done.25
  207.4 6.9 %collective-permute-start.26 = (f32[4,48,128]{2,1,0:T(8,128)S(1)}, f32[4,48,128]{2,1,0:T(8,128)S(1)}, u32[]{:S(2)}, u32[]{:S(2)}) collective-permute-start(f32[4,48,128]{2,1,0:T(8,128)S(1)} %pad_maximum_fusion.mine), channel_id=1, source_target_pairs={{0,1},{1,0},{2,3},{3,2},{4,5},{5,4},{6,7},{7,6},{16,17},{17,16},{1... | collective-permute-start | bytes 294920 | tf_op jit(solution)/shard_map/ppermute | solution.py:39
  215.3 9.9 %finish.1 = (f32[2048,256]{1,0:T(8,128)}, f32[256,256]{1,0:T(8,128)}) custom-call(s32[2]{0:T(128)S(1)} %pad_add_fusion.me, f32[4,48,128]{2,1,0:T(8,128)S(1)} %pad_maximum_fusion.mine, f32[4,48,128]{2,1,0:T(8,128)S(1)} %collective-permute-done.26.other, f32[2048,256]{1,0:T(8,128)S(1)} %get-tuple-element.27.summed_hbm), custom_call_target="tpu_custom_call" | custom-call | tf_op jit(solution)/shard_map/finish/pallas_call | solution.py:281
  (52 shorter events, 11.4 us)
Async XLA Ops:
  0.6 29.8 %collective-permute-start = (bf16[2048,256]{1,0:T(8,128)(2,1)}, bf16[2048,256]{1,0:T(8,128)(2,1)S(1)}, u32[]{:S(2)}, u32[]{:S(2)}) collective-permute-start(bf16[2048,256]{1,0:T(8,128)(2,1)} %refs_0_.1), channel_id=1, source_target_pairs={{0,32},{16,48},{32,64},{48,80},{64,96},{80,112},{96,0},{112,16},{1... | collective-permute-start | bytes 3145736 | tf_op jit(solution)/shard_map/ppermute | solution.py:44
  5.2 12.5 %collective-permute-start.8 = (bf16[1024,256]{1,0:T(8,128)(2,1)S(1)}, bf16[1024,256]{1,0:T(8,128)(2,1)S(1)}, u32[]{:S(2)}, u32[]{:S(2)}) collective-permute-start(bf16[1024,256]{1,0:T(8,128)(2,1)S(1)} %get-tuple-element.28), channel_id=1, source_target_pairs={{0,16},{16,0},{32,48},{48,32},{64,80},{80,64},{96,112},{112,96},{1... | collective-permute-start | bytes 1572872 | tf_op jit(solution)/shard_map/ppermute | solution.py:44
  6.5 12.8 %collective-permute-start.2 = (bf16[1024,256]{1,0:T(8,128)(2,1)S(1)}, bf16[1024,256]{1,0:T(8,128)(2,1)S(1)}, u32[]{:S(2)}, u32[]{:S(2)}) collective-permute-start(bf16[1024,256]{1,0:T(8,128)(2,1)S(1)} %get-tuple-element.28), channel_id=1, source_target_pairs={{0,96},{16,112},{32,0},{48,16},{64,32},{80,48},{96,64},{112,80},{1... | collective-permute-start | bytes 1572872 | tf_op jit(solution)/shard_map/ppermute | solution.py:44
  8.7 21.7 %collective-permute-start.1 = (bf16[1024,256]{1,0:T(8,128)(2,1)}, bf16[1024,256]{1,0:T(8,128)(2,1)S(1)}, u32[]{:S(2)}, u32[]{:S(2)}) collective-permute-start(bf16[1024,256]{1,0:T(8,128)(2,1)} %get-tuple-element.29), channel_id=1, source_target_pairs={{0,96},{16,112},{32,0},{48,16},{64,32},{80,48},{96,64},{112,80},{1... | collective-permute-start | bytes 1572872 | tf_op jit(solution)/shard_map/ppermute | solution.py:44
  10.1 23.6 %collective-permute-start.6 = (bf16[1024,256]{1,0:T(8,128)(2,1)}, bf16[1024,256]{1,0:T(8,128)(2,1)S(1)}, u32[]{:S(2)}, u32[]{:S(2)}) collective-permute-start(bf16[1024,256]{1,0:T(8,128)(2,1)} %get-tuple-element.29), channel_id=1, source_target_pairs={{0,16},{16,0},{32,48},{48,32},{64,80},{80,64},{96,112},{112,96},{1... | collective-permute-start | bytes 1572872 | tf_op jit(solution)/shard_map/ppermute | solution.py:44
  17.7 46.8 %copy-start.1 = (bf16[1024,256]{1,0:T(8,128)(2,1)}, bf16[1024,256]{1,0:T(8,128)(2,1)S(1)}, u32[]{:S(2)}) copy-start(bf16[1024,256]{1,0:T(8,128)(2,1)S(1)} %collective-permute-done.8.refs_7_) | copy-start | bytes 1572868
  17.7 22.0 %collective-permute-start.11 = (bf16[1024,256]{1,0:T(8,128)(2,1)S(1)}, bf16[1024,256]{1,0:T(8,128)(2,1)}, u32[]{:S(2)}, u32[]{:S(2)}) collective-permute-start(bf16[1024,256]{1,0:T(8,128)(2,1)S(1)} %collective-permute-done.8.refs_7_), channel_id=1, source_target_pairs={{0,32},{16,48},{32,64},{48,80},{64,96},{80,112},{96,0},{112,16},{1... | collective-permute-start | bytes 1572872 | tf_op jit(solution)/shard_map/ppermute | solution.py:44
  19.3 45.1 %copy-start.2 = (bf16[1024,256]{1,0:T(8,128)(2,1)}, bf16[1024,256]{1,0:T(8,128)(2,1)S(1)}, u32[]{:S(2)}) copy-start(bf16[1024,256]{1,0:T(8,128)(2,1)S(1)} %collective-permute-done.2.refs_2_) | copy-start | bytes 1572868
  19.3 22.3 %collective-permute-start.4 = (bf16[1024,256]{1,0:T(8,128)(2,1)S(1)}, bf16[1024,256]{1,0:T(8,128)(2,1)}, u32[]{:S(2)}, u32[]{:S(2)}) collective-permute-start(bf16[1024,256]{1,0:T(8,128)(2,1)S(1)} %collective-permute-done.2.refs_2_), channel_id=1, source_target_pairs={{0,96},{16,112},{32,0},{48,16},{64,32},{80,48},{96,64},{112,80},{1... | collective-permute-start | bytes 1572872 | tf_op jit(solution)/shard_map/ppermute | solution.py:44
  30.4 34.1 %copy-start = (bf16[2048,256]{1,0:T(8,128)(2,1)}, bf16[2048,256]{1,0:T(8,128)(2,1)S(1)}, u32[]{:S(2)}) copy-start(bf16[2048,256]{1,0:T(8,128)(2,1)S(1)} %collective-permute-done.refs_5_) | copy-start | bytes 3145732
  30.4 12.5 %collective-permute-start.9 = (bf16[1024,256]{1,0:T(8,128)(2,1)S(1)}, bf16[1024,256]{1,0:T(8,128)(2,1)}, u32[]{:S(2)}, u32[]{:S(2)}) collective-permute-start(bf16[1024,256]{1,0:T(8,128)(2,1)S(1)} %collective-permute-done.1.refs_1_), channel_id=1, source_target_pairs={{0,16},{16,0},{32,48},{48,32},{64,80},{80,64},{96,112},{112,96},{1... | collective-permute-start | bytes 1572872 | tf_op jit(solution)/shard_map/ppermute | solution.py:44
  30.5 22.4 %collective-permute-start.3 = (bf16[1024,256]{1,0:T(8,128)(2,1)S(1)}, bf16[1024,256]{1,0:T(8,128)(2,1)S(1)}, u32[]{:S(2)}, u32[]{:S(2)}) collective-permute-start(bf16[1024,256]{1,0:T(8,128)(2,1)S(1)} %collective-permute-done.1.refs_1_), channel_id=1, source_target_pairs={{0,96},{16,112},{32,0},{48,16},{64,32},{80,48},{96,64},{112,80},{1... | collective-permute-start | bytes 1572872 | tf_op jit(solution)/shard_map/ppermute | solution.py:44
  33.8 30.7 %copy-start.3 = (bf16[1024,256]{1,0:T(8,128)(2,1)}, bf16[1024,256]{1,0:T(8,128)(2,1)S(1)}, u32[]{:S(2)}) copy-start(bf16[1024,256]{1,0:T(8,128)(2,1)S(1)} %collective-permute-done.6.refs_6_) | copy-start | bytes 1572868
  33.8 16.3 %collective-permute-start.7 = (bf16[1024,256]{1,0:T(8,128)(2,1)S(1)}, bf16[1024,256]{1,0:T(8,128)(2,1)S(1)}, u32[]{:S(2)}, u32[]{:S(2)}) collective-permute-start(bf16[1024,256]{1,0:T(8,128)(2,1)S(1)} %collective-permute-done.6.refs_6_), channel_id=1, source_target_pairs={{0,32},{16,48},{32,64},{48,80},{64,96},{80,112},{96,0},{112,16},{1... | collective-permute-start | bytes 1572872 | tf_op jit(solution)/shard_map/ppermute | solution.py:44
  39.7 14.1 %collective-permute-start.5 = (bf16[1024,256]{1,0:T(8,128)(2,1)S(1)}, bf16[1024,256]{1,0:T(8,128)(2,1)}, u32[]{:S(2)}, u32[]{:S(2)}) collective-permute-start(bf16[1024,256]{1,0:T(8,128)(2,1)S(1)} %collective-permute-done.2.refs_2_), channel_id=1, source_target_pairs={{0,16},{16,0},{32,48},{48,32},{64,80},{80,64},{96,112},{112,96},{1... | collective-permute-start | bytes 1572872 | tf_op jit(solution)/shard_map/ppermute | solution.py:44
  41.6 22.8 %collective-permute-start.12 = (bf16[1024,256]{1,0:T(8,128)(2,1)}, bf16[1024,256]{1,0:T(8,128)(2,1)}, u32[]{:S(2)}, u32[]{:S(2)}) collective-permute-start(bf16[1024,256]{1,0:T(8,128)(2,1)} %collective-permute-done.11.refs_13_), channel_id=1, source_target_pairs={{0,32},{16,48},{32,64},{48,80},{64,96},{80,112},{96,0},{112,16},{1... | collective-permute-start | bytes 1572872 | tf_op jit(solution)/shard_map/ppermute | solution.py:44
  42.9 21.5 %collective-permute-start.10 = (bf16[1024,256]{1,0:T(8,128)(2,1)}, bf16[1024,256]{1,0:T(8,128)(2,1)}, u32[]{:S(2)}, u32[]{:S(2)}) collective-permute-start(bf16[1024,256]{1,0:T(8,128)(2,1)} %collective-permute-done.9.refs_8_), channel_id=1, source_target_pairs={{0,96},{16,112},{32,0},{48,16},{64,32},{80,48},{96,64},{112,80},{1... | collective-permute-start | bytes 1572872 | tf_op jit(solution)/shard_map/ppermute | solution.py:44
  54.5 19.2 %all-to-all-start = ((s32[16,1,8]{2,1,0:T(1,128)}), s32[16,1,8]{2,1,0:T(1,128)S(1)}, u32[]{:S(2)}, u32[]{:S(2)}) async-start(s32[16,1,8]{2,1,0:T(1,128)} %bitcast.3), calls=%async_computation | async-start | bytes 16384 | tf_op jit(solution)/shard_map/all_to_all | solution.py:70
  181.7 2.1 collective-permute-start.13
  183.9 4.3 %collective-permute-start.15 = (f32[48,128]{1,0:T(8,128)S(1)}, f32[48,128]{1,0:T(8,128)S(1)}, u32[]{:S(2)}, u32[]{:S(2)}) collective-permute-start(f32[48,128]{1,0:T(8,128)S(1)} %get-tuple-element.30), channel_id=1, source_target_pairs={{0,4},{1,5},{2,6},{3,7},{4,0},{5,1},{6,2},{7,3},{16,20},{17,21},{1... | collective-permute-start | bytes 73736 | tf_op jit(solution)/shard_map/ppermute | solution.py:39
  184.2 3.9 %collective-permute-start.16 = (f32[48,128]{1,0:T(8,128)S(1)}, f32[48,128]{1,0:T(8,128)S(1)}, u32[]{:S(2)}, u32[]{:S(2)}) collective-permute-start(f32[48,128]{1,0:T(8,128)S(1)} %get-tuple-element.31), channel_id=1, source_target_pairs={{0,6},{1,7},{2,0},{3,1},{4,2},{5,3},{6,4},{7,5},{16,22},{17,23},{1... | collective-permute-start | bytes 73736 | tf_op jit(solution)/shard_map/ppermute | solution.py:39
  185.1 4.1 %collective-permute-start.14 = (f32[48,128]{1,0:T(8,128)S(1)}, f32[48,128]{1,0:T(8,128)S(1)}, u32[]{:S(2)}, u32[]{:S(2)}) collective-permute-start(f32[48,128]{1,0:T(8,128)S(1)} %get-tuple-element.32), channel_id=1, source_target_pairs={{0,2},{1,3},{2,4},{3,5},{4,6},{5,7},{6,0},{7,1},{16,18},{17,19},{1... | collective-permute-start | bytes 73736 | tf_op jit(solution)/shard_map/ppermute | solution.py:39
  189.2 2.7 %collective-permute-start.19 = (f32[48,128]{1,0:T(8,128)S(1)}, f32[48,128]{1,0:T(8,128)S(1)}, u32[]{:S(2)}, u32[]{:S(2)}) collective-permute-start(f32[48,128]{1,0:T(8,128)S(1)} %fusion), channel_id=1, source_target_pairs={{0,24},{1,25},{2,26},{3,27},{4,28},{5,29},{6,30},{7,31},{16,0},{17... | collective-permute-start | bytes 73736 | tf_op jit(solution)/shard_map/ppermute | solution.py:39
  189.8 4.2 %collective-permute-start.18 = (f32[48,128]{1,0:T(8,128)S(1)}, f32[48,128]{1,0:T(8,128)S(1)}, u32[]{:S(2)}, u32[]{:S(2)}) collective-permute-start(f32[48,128]{1,0:T(8,128)S(1)} %fusion), channel_id=1, source_target_pairs={{0,8},{1,9},{2,10},{3,11},{4,12},{5,13},{6,14},{7,15},{16,24},{17,... | collective-permute-start | bytes 73736 | tf_op jit(solution)/shard_map/ppermute | solution.py:39
  191.0 3.9 %collective-permute-start.17 = (f32[48,128]{1,0:T(8,128)S(1)}, f32[48,128]{1,0:T(8,128)S(1)}, u32[]{:S(2)}, u32[]{:S(2)}) collective-permute-start(f32[48,128]{1,0:T(8,128)S(1)} %fusion), channel_id=1, source_target_pairs={{0,16},{1,17},{2,18},{3,19},{4,20},{5,21},{6,22},{7,23},{16,8},{17... | collective-permute-start | bytes 73736 | tf_op jit(solution)/shard_map/ppermute | solution.py:39
  194.9 4.4 %collective-permute-start.22 = (f32[48,128]{1,0:T(8,128)S(1)}, f32[48,128]{1,0:T(8,128)S(1)}, u32[]{:S(2)}, u32[]{:S(2)}) collective-permute-start(f32[48,128]{1,0:T(8,128)S(1)} %add_add_fusion.1), channel_id=1, source_target_pairs={{0,96},{1,97},{2,98},{3,99},{4,100},{5,101},{6,102},{7,103},{16,11... | collective-permute-start | bytes 73736 | tf_op jit(solution)/shard_map/ppermute | solution.py:39
  198.3 4.2 %collective-permute-start.21 = (f32[48,128]{1,0:T(8,128)S(1)}, f32[48,128]{1,0:T(8,128)S(1)}, u32[]{:S(2)}, u32[]{:S(2)}) collective-permute-start(f32[48,128]{1,0:T(8,128)S(1)} %add_add_fusion.1), channel_id=1, source_target_pairs={{0,64},{1,65},{2,66},{3,67},{4,68},{5,69},{6,70},{7,71},{16,80},{1... | collective-permute-start | bytes 73736 | tf_op jit(solution)/shard_map/ppermute | solution.py:39
  198.4 4.2 %collective-permute-start.20 = (f32[48,128]{1,0:T(8,128)S(1)}, f32[48,128]{1,0:T(8,128)S(1)}, u32[]{:S(2)}, u32[]{:S(2)}) collective-permute-start(f32[48,128]{1,0:T(8,128)S(1)} %add_add_fusion.1), channel_id=1, source_target_pairs={{0,32},{1,33},{2,34},{3,35},{4,36},{5,37},{6,38},{7,39},{16,48},{1... | collective-permute-start | bytes 73736 | tf_op jit(solution)/shard_map/ppermute | solution.py:39
  202.5 4.3 %collective-permute-start.25 = (f32[48,128]{1,0:T(8,128)S(1)}, f32[48,128]{1,0:T(8,128)S(1)}, u32[]{:S(2)}, u32[]{:S(2)}) collective-permute-start(f32[48,128]{1,0:T(8,128)S(1)} %add_add_fusion), channel_id=1, source_target_pairs={{0,2},{1,3},{2,4},{3,5},{4,6},{5,7},{6,0},{7,1},{16,18},{17,19},{1... | collective-permute-start | bytes 73736 | tf_op jit(solution)/shard_map/ppermute | solution.py:39
  202.6 4.3 %collective-permute-start.24 = (f32[48,128]{1,0:T(8,128)S(1)}, f32[48,128]{1,0:T(8,128)S(1)}, u32[]{:S(2)}, u32[]{:S(2)}) collective-permute-start(f32[48,128]{1,0:T(8,128)S(1)} %add_add_fusion), channel_id=1, source_target_pairs={{0,4},{1,5},{2,6},{3,7},{4,0},{5,1},{6,2},{7,3},{16,20},{17,21},{1... | collective-permute-start | bytes 73736 | tf_op jit(solution)/shard_map/ppermute | solution.py:39
  204.7 2.7 %collective-permute-start.23 = (f32[48,128]{1,0:T(8,128)S(1)}, f32[48,128]{1,0:T(8,128)S(1)}, u32[]{:S(2)}, u32[]{:S(2)}) collective-permute-start(f32[48,128]{1,0:T(8,128)S(1)} %add_add_fusion), channel_id=1, source_target_pairs={{0,6},{1,7},{2,0},{3,1},{4,2},{5,3},{6,4},{7,5},{16,22},{17,23},{1... | collective-permute-start | bytes 73736 | tf_op jit(solution)/shard_map/ppermute | solution.py:39
  207.4 7.9 %collective-permute-start.26 = (f32[4,48,128]{2,1,0:T(8,128)S(1)}, f32[4,48,128]{2,1,0:T(8,128)S(1)}, u32[]{:S(2)}, u32[]{:S(2)}) collective-permute-start(f32[4,48,128]{2,1,0:T(8,128)S(1)} %pad_maximum_fusion.mine), channel_id=1, source_target_pairs={{0,1},{1,0},{2,3},{3,2},{4,5},{5,4},{6,7},{7,6},{16,17},{17,16},{1... | collective-permute-start | bytes 294920 | tf_op jit(solution)/shard_map/ppermute | solution.py:39
  (2 other events, 3.6 us)

commit v5 on v4

--- a/solution.py
+++ b/solution.py
@@ -16,10 +16,11 @@
 ITEMS = 262144
 BOTH = ("row", "col")
 PARTS = 14
-LATE = (10, 11, 13, 12, 9, 8, 3, 4, 0)
+LATE = (10, 11, 13, 8, 4, 0)
 PANEL = 32
+SUB = 16
 PIECE = 48
-CHUNKS = 16
+CHUNKS = 8
 OUT_CHUNKS = 8
 
 
@@ -103,7 +104,7 @@
     stores = []
     for g in range(CHUNKS):
 
-        @pl.loop(g * share, (g + 1) * share, unroll=8)
+        @pl.loop(g * share, (g + 1) * share, unroll=share)
         def _(t):
             source = column[pl.ds(pl.multiple_of(src[t] * BLOCK, BLOCK), BLOCK), :]
             product = jnp.dot(tiles[t], source, preferred_element_type=jnp.float32)
@@ -133,7 +134,7 @@
             pltpu.SemaphoreType.DMA((len(LATE),)),
             pltpu.SemaphoreType.DMA((CHUNKS,)),
         ],
-        compiler_params=pltpu.CompilerParams(vmem_limit_bytes=53 * 1024 * 1024),
+        compiler_params=pltpu.CompilerParams(vmem_limit_bytes=51 * 1024 * 1024),
         name="products",
     )(src, tiles, *parts)
 
@@ -220,26 +221,41 @@
     work[BLOCK:, :BLOCK] = jnp.zeros((BLOCK, BLOCK), jnp.float32)
     work[BLOCK:, BLOCK:BASIS] = gram[2 * BLOCK :, :] * (1.0 / ITEMS)
     work[:, BASIS:] = jnp.where(row_id == col_id, 1.0, 0.0)
-    panel_row = lax.broadcasted_iota(jnp.int32, (PANEL, BLOCK), 0)
+    sub_row = lax.broadcasted_iota(jnp.int32, (8, BLOCK), 0)
+    groups = PANEL // 8
+    lower = row_id >= col_id
     for k in range(0, BASIS, PANEL):
         base = k // BLOCK * BLOCK
         window = pl.ds(base, 3 * BLOCK)
-        panel = work[k : k + PANEL, window]
-        strips = [panel[:, j * BLOCK : (j + 1) * BLOCK] for j in range(3)]
-        columns = [
-            jnp.broadcast_to(strips[0][:, k + i - base : k + i - base + 1], (PANEL, BLOCK))
-            for i in range(PANEL)
+        strips = [
+            [work[k + 8 * g : k + 8 * g + 8, pl.ds(base + BLOCK * j, BLOCK)] for j in range(3)]
+            for g in range(groups)
         ]
-        for i in range(PANEL):
-            scale = lax.rsqrt(columns[i][i : i + 1, :])
-            column = columns[i] * scale
-            below = jnp.where(panel_row > i, column, 0.0)
-            for j in range(3):
-                pivot_row = strips[j][i : i + 1, :] * scale
-                strips[j] = jnp.where(panel_row == i, pivot_row, strips[j] - below * pivot_row)
-            for j in range(i + 1, PANEL):
-                columns[j] = columns[j] - column * column[j : j + 1, :]
-        panel = jnp.concatenate(strips, axis=1)
+        for begin in range(0, PANEL, SUB):
+            columns = {
+                (i, g): jnp.broadcast_to(
+                    strips[g][0][:, k + i - base : k + i - base + 1], (8, BLOCK)
+                )
+                for i in range(begin, begin + SUB)
+                for g in range(begin // 8, groups)
+            }
+            for i in range(begin, begin + SUB):
+                own, at = i // 8, i % 8
+                scale = lax.rsqrt(columns[i, own][at : at + 1, :])
+                column = {g: columns[i, g] * scale for g in range(own, groups)}
+                for q in range(i + 1, begin + SUB):
+                    near = column[q // 8][q % 8 : q % 8 + 1, :]
+                    for g in range(own, groups):
+                        columns[q, g] = columns[q, g] - column[g] * near
+                below = jnp.where(sub_row > at, column[own], 0.0)
+                for j in range(3):
+                    pivot_row = strips[own][j][at : at + 1, :] * scale
+                    strips[own][j] = jnp.where(
+                        sub_row == at, pivot_row, strips[own][j] - below * pivot_row
+                    )
+                    for g in range(own + 1, groups):
+                        strips[g][j] = strips[g][j] - column[g] * pivot_row
+        panel = jnp.concatenate([jnp.concatenate(strip, axis=1) for strip in strips], axis=0)
         work[k : k + PANEL, window] = panel
         after = k + PANEL
         if after < BASIS:
@@ -253,7 +269,6 @@
                 preferred_element_type=jnp.float32,
             )
             work[after:, window] = work[after:, window] - update[after - base :, :]
-    lower = row_id >= col_id
     factor[...] = jnp.where(lower, work[:, :BASIS].T, 0.0)
     inverse = jnp.where(lower, work[:, BASIS:], 0.0)
     high, middle, _ = split(inverse)

time: 226 us -> 224 us (level)
  transfers between devices with their start and end apart: 28 -> 28, of which waited for: 19 -> 20; matrix products, arithmetic and copies ran while one was open for 2% -> 2% of each run, Pallas kernels for 4% -> 4%
where the time goes in v5:
time: 224 us
  blocking collectives  104 us (46%)
  starting transfers between devices  47.9 us (21%)
  waiting for transfers between devices  44.7 us (20%)
  Pallas kernels  22.2 us (10%)
  local copies, waits for them, and re-layouts  2.77 us (1%)
    all_to_all x1, blocking collectives, local(): lax.all_to_all(products.reshape(N_COL, PER_PEER * BLOCK, BASIS), 'col', 0...  104 us
    ppermute x13, waiting for transfers between devices, row_shifted(): return lax.ppermute(value, 'row', pairs)  30.2 us
    ppermute x13, starting transfers between devices, row_shifted(): return lax.ppermute(value, 'row', pairs)  20 us
    ppermute x14, starting transfers between devices, shifted(): return lax.ppermute(value, BOTH, pairs)  18.8 us
    ppermute x14, waiting for transfers between devices, shifted(): return lax.ppermute(value, BOTH, pairs)  14.5 us
    pallas_call x1, Pallas kernels, finish(): pl.pallas_call(finish_kernel, out_shape=(jax.ShapeDtypeStruct((ROWS_DEV,...  9.5 us
    all_to_all x1, starting transfers between devices, gather_column(): lax.all_to_all(place.reshape(N_COL, 1, PER_PEER), 'col', 0, 0, tiled=True)  9.15 us
    pallas_call x1, Pallas kernels, make_products(): pl.pallas_call(product_kernel, out_shape=jax.ShapeDtypeStruct((TILE_DEV *...  8.6 us
  transfers between devices with their start and end apart: 28, of which 20 were waited for; matrix products, arithmetic and copies ran while one was open for 2% of the time, Pallas kernels for 4%

profile of v5, /device:TPU:1, one launch (start us, length us, event | category | flops | bytes accessed | tf_op | source)
XLA Modules:
  0.0 224.1 jit_solution(1143344481995911036)
XLA Ops:
  0.6 2.5 %collective-permute-start = (bf16[2048,256]{1,0:T(8,128)(2,1)}, bf16[2048,256]{1,0:T(8,128)(2,1)}, u32[]{:S(2)}, u32[]{:S(2)}) collective-permute-start(bf16[2048,256]{1,0:T(8,128)(2,1)} %refs_0_.1), channel_id=1, source_target_pairs={{0,32},{16,48},{32,64},{48,80},{64,96},{80,112},{96,0},{112,16},{1... | collective-permute-start | bytes 3145736 | tf_op jit(solution)/shard_map/ppermute | solution.py:45
  3.2 2.1 fusion.1
  5.2 1.3 collective-permute-start.8
  6.5 2.1 collective-permute-start.2
  8.7 1.4 collective-permute-start.1
  10.3 7.5 %collective-permute-done.8.refs_7_ = bf16[1024,256]{1,0:T(8,128)(2,1)S(1)} collective-permute-done((bf16[1024,256]{1,0:T(8,128)(2,1)S(1)}, bf16[1024,256]{1,0:T(8,128)(2,1)S(1)}, u32[]{:S(2)}, u32[]{:S(2)}) %collective-permute-start.8) | collective-permute-done | bytes 524320 | tf_op jit(solution)/shard_map/ppermute | solution.py:45
  17.8 1.6 collective-permute-start.11
  19.4 2.9 %collective-permute-start.4 = (bf16[1024,256]{1,0:T(8,128)(2,1)S(1)}, bf16[1024,256]{1,0:T(8,128)(2,1)S(1)}, u32[]{:S(2)}, u32[]{:S(2)}) collective-permute-start(bf16[1024,256]{1,0:T(8,128)(2,1)S(1)} %collective-permute-done.2.refs_2_), channel_id=1, source_target_pairs={{0,96},{16,112},{32,0},{48,16},{64,32},{80,48},{96,64},{112,80},{1... | collective-permute-start | bytes 1572872 | tf_op jit(solution)/shard_map/ppermute | solution.py:45
  22.3 8.0 %collective-permute-done.1.refs_1_ = bf16[1024,256]{1,0:T(8,128)(2,1)S(1)} collective-permute-done((bf16[1024,256]{1,0:T(8,128)(2,1)}, bf16[1024,256]{1,0:T(8,128)(2,1)S(1)}, u32[]{:S(2)}, u32[]{:S(2)}) %collective-permute-start.1) | collective-permute-done | bytes 524320 | tf_op jit(solution)/shard_map/ppermute | solution.py:45
  30.6 3.2 %collective-permute-start.3 = (bf16[1024,256]{1,0:T(8,128)(2,1)S(1)}, bf16[1024,256]{1,0:T(8,128)(2,1)S(1)}, u32[]{:S(2)}, u32[]{:S(2)}) collective-permute-start(bf16[1024,256]{1,0:T(8,128)(2,1)S(1)} %collective-permute-done.1.refs_1_), channel_id=1, source_target_pairs={{0,96},{16,112},{32,0},{48,16},{64,32},{80,48},{96,64},{112,80},{1... | collective-permute-start | bytes 1572872 | tf_op jit(solution)/shard_map/ppermute | solution.py:45
  33.8 6.0 %collective-permute-done.11.refs_13_ = bf16[1024,256]{1,0:T(8,128)(2,1)} collective-permute-done((bf16[1024,256]{1,0:T(8,128)(2,1)S(1)}, bf16[1024,256]{1,0:T(8,128)(2,1)}, u32[]{:S(2)}, u32[]{:S(2)}) %collective-permute-start.11) | collective-permute-done | bytes 524320 | tf_op jit(solution)/shard_map/ppermute | solution.py:45
  39.7 1.3 collective-permute-start.5
  41.6 1.3 collective-permute-start.12
  42.9 1.9 collective-permute-start.10
  46.2 3.8 %collective-permute-done.7.refs_12_ = bf16[1024,256]{1,0:T(8,128)(2,1)S(1)} collective-permute-done((bf16[1024,256]{1,0:T(8,128)(2,1)S(1)}, bf16[1024,256]{1,0:T(8,128)(2,1)S(1)}, u32[]{:S(2)}, u32[]{:S(2)}) %collective-permute-start.7) | collective-permute-done | bytes 524320 | tf_op jit(solution)/shard_map/ppermute | solution.py:45
  50.0 2.8 %collective-permute-done.3.refs_3_ = bf16[1024,256]{1,0:T(8,128)(2,1)S(1)} collective-permute-done((bf16[1024,256]{1,0:T(8,128)(2,1)S(1)}, bf16[1024,256]{1,0:T(8,128)(2,1)S(1)}, u32[]{:S(2)}, u32[]{:S(2)}) %collective-permute-start.3) | collective-permute-done | bytes 524320 | tf_op jit(solution)/shard_map/ppermute | solution.py:45
  52.9 1.0 collective-permute-done.5.refs_9_
  54.5 9.1 %all-to-all-start = ((s32[16,1,8]{2,1,0:T(1,128)}), s32[16,1,8]{2,1,0:T(1,128)S(1)}, u32[]{:S(2)}, u32[]{:S(2)}) async-start(s32[16,1,8]{2,1,0:T(1,128)} %bitcast.3), calls=%async_computation | async-start | bytes 16384 | tf_op jit(solution)/shard_map/all_to_all | solution.py:71
  64.1 8.6 %products.1 = bf16[16384,256]{1,0:T(8,128)(2,1)} custom-call(s32[128]{0:T(128)S(1)} %add_bitcast_fusion.src, bf16[128,128,128]{2,1,0:T(8,128)(2,1)} %bitcast.26, bf16[2048,256]{1,0:T(8,128)(2,1)} %refs_0_.1, bf16[1024,256]{1,0:T(8,128)(2,1)S(1)} %collective-permute-done.1.refs_1_, bf16[1024,256]{1,0:T(8,128)(2,1)S(1)} %collective-permute-done.2.refs_2_, ...), custom_call_target="tpu_custom_call" | custom-call | tf_op jit(solution)/shard_map/products/pallas_call | solution.py:122
  72.7 104.3 %all_to_all.10 = bf16[16,1024,256]{2,1,0:T(8,128)(2,1)S(1)} all-to-all(bf16[16,1024,256]{2,1,0:T(8,128)(2,1)} %bitcast.25), channel_id=1, replica_groups=mesh['row'=8,'col'=16] {'col'}, dimensions={0} | all-to-all | bytes 16777216 | tf_op jit(solution)/shard_map/all_to_all | solution.py:334
  177.0 4.1 %sum_and_gram.1 = (f32[2048,256]{1,0:T(8,128)S(1)}, f32[8,48,128]{2,1,0:T(8,128)S(1)}) custom-call(s32[16,1,8]{2,1,0:T(1,128)S(1)} %all-to-all-done.place, s32[2]{0:T(128)S(1)} %pad_add_fusion.me, bf16[16384,256]{1,0:T(8,128)(2,1)S(1)} %bitcast.24), custom_call_target="tpu_custom_call" | custom-call | tf_op jit(solution)/shard_map/sum_and_gram/pallas_call | solution.py:171
  181.1 1.2 collective-permute-start.13
  185.0 2.5 %collective-permute-done.15 = f32[48,128]{1,0:T(8,128)S(1)} collective-permute-done((f32[48,128]{1,0:T(8,128)S(1)}, f32[48,128]{1,0:T(8,128)S(1)}, u32[]{:S(2)}, u32[]{:S(2)}) %collective-permute-start.15) | collective-permute-done | bytes 24608 | tf_op jit(solution)/shard_map/ppermute | solution.py:40
  187.5 1.1 collective-permute-done.14
  189.1 1.2 collective-permute-start.18
  191.4 1.9 collective-permute-done.18
  194.2 3.2 %collective-permute-start.22 = (f32[48,128]{1,0:T(8,128)S(1)}, f32[48,128]{1,0:T(8,128)S(1)}, u32[]{:S(2)}, u32[]{:S(2)}) collective-permute-start(f32[48,128]{1,0:T(8,128)S(1)} %add_add_fusion.1), channel_id=1, source_target_pairs={{0,96},{1,97},{2,98},{3,99},{4,100},{5,101},{6,102},{7,103},{16,11... | collective-permute-start | bytes 73736 | tf_op jit(solution)/shard_map/ppermute | solution.py:40
  198.4 3.3 %collective-permute-done.21 = f32[48,128]{1,0:T(8,128)S(1)} collective-permute-done((f32[48,128]{1,0:T(8,128)S(1)}, f32[48,128]{1,0:T(8,128)S(1)}, u32[]{:S(2)}, u32[]{:S(2)}) %collective-permute-start.21) | collective-permute-done | bytes 24608 | tf_op jit(solution)/shard_map/ppermute | solution.py:40
  201.8 2.1 collective-permute-start.24
  204.5 1.5 collective-permute-done.25
  206.6 6.9 %collective-permute-start.26 = (f32[4,48,128]{2,1,0:T(8,128)S(1)}, f32[4,48,128]{2,1,0:T(8,128)S(1)}, u32[]{:S(2)}, u32[]{:S(2)}) collective-permute-start(f32[4,48,128]{2,1,0:T(8,128)S(1)} %pad_maximum_fusion.mine), channel_id=1, source_target_pairs={{0,1},{1,0},{2,3},{3,2},{4,5},{5,4},{6,7},{7,6},{16,17},{17,16},{1... | collective-permute-start | bytes 294920 | tf_op jit(solution)/shard_map/ppermute | solution.py:40
  214.5 9.5 %finish.1 = (f32[2048,256]{1,0:T(8,128)}, f32[256,256]{1,0:T(8,128)}) custom-call(s32[2]{0:T(128)S(1)} %pad_add_fusion.me, f32[4,48,128]{2,1,0:T(8,128)S(1)} %pad_maximum_fusion.mine, f32[4,48,128]{2,1,0:T(8,128)S(1)} %collective-permute-done.26.other, f32[2048,256]{1,0:T(8,128)S(1)} %get-tuple-element.27.summed_hbm), custom_call_target="tpu_custom_call" | custom-call | tf_op jit(solution)/shard_map/finish/pallas_call | solution.py:296
  (44 shorter events, 11.9 us)
Async XLA Ops:
  0.6 29.8 %collective-permute-start = (bf16[2048,256]{1,0:T(8,128)(2,1)}, bf16[2048,256]{1,0:T(8,128)(2,1)}, u32[]{:S(2)}, u32[]{:S(2)}) collective-permute-start(bf16[2048,256]{1,0:T(8,128)(2,1)} %refs_0_.1), channel_id=1, source_target_pairs={{0,32},{16,48},{32,64},{48,80},{64,96},{80,112},{96,0},{112,16},{1... | collective-permute-start | bytes 3145736 | tf_op jit(solution)/shard_map/ppermute | solution.py:45
  5.2 12.6 %collective-permute-start.8 = (bf16[1024,256]{1,0:T(8,128)(2,1)S(1)}, bf16[1024,256]{1,0:T(8,128)(2,1)S(1)}, u32[]{:S(2)}, u32[]{:S(2)}) collective-permute-start(bf16[1024,256]{1,0:T(8,128)(2,1)S(1)} %get-tuple-element.28), channel_id=1, source_target_pairs={{0,16},{16,0},{32,48},{48,32},{64,80},{80,64},{96,112},{112,96},{1... | collective-permute-start | bytes 1572872 | tf_op jit(solution)/shard_map/ppermute | solution.py:45
  6.5 12.9 %collective-permute-start.2 = (bf16[1024,256]{1,0:T(8,128)(2,1)S(1)}, bf16[1024,256]{1,0:T(8,128)(2,1)S(1)}, u32[]{:S(2)}, u32[]{:S(2)}) collective-permute-start(bf16[1024,256]{1,0:T(8,128)(2,1)S(1)} %get-tuple-element.28), channel_id=1, source_target_pairs={{0,96},{16,112},{32,0},{48,16},{64,32},{80,48},{96,64},{112,80},{1... | collective-permute-start | bytes 1572872 | tf_op jit(solution)/shard_map/ppermute | solution.py:45
  8.7 21.7 %collective-permute-start.1 = (bf16[1024,256]{1,0:T(8,128)(2,1)}, bf16[1024,256]{1,0:T(8,128)(2,1)S(1)}, u32[]{:S(2)}, u32[]{:S(2)}) collective-permute-start(bf16[1024,256]{1,0:T(8,128)(2,1)} %get-tuple-element.29), channel_id=1, source_target_pairs={{0,96},{16,112},{32,0},{48,16},{64,32},{80,48},{96,64},{112,80},{1... | collective-permute-start | bytes 1572872 | tf_op jit(solution)/shard_map/ppermute | solution.py:45
  10.1 23.6 %collective-permute-start.6 = (bf16[1024,256]{1,0:T(8,128)(2,1)}, bf16[1024,256]{1,0:T(8,128)(2,1)S(1)}, u32[]{:S(2)}, u32[]{:S(2)}) collective-permute-start(bf16[1024,256]{1,0:T(8,128)(2,1)} %get-tuple-element.29), channel_id=1, source_target_pairs={{0,16},{16,0},{32,48},{48,32},{64,80},{80,64},{96,112},{112,96},{1... | collective-permute-start | bytes 1572872 | tf_op jit(solution)/shard_map/ppermute | solution.py:45
  17.8 46.3 %copy-start = (bf16[1024,256]{1,0:T(8,128)(2,1)}, bf16[1024,256]{1,0:T(8,128)(2,1)S(1)}, u32[]{:S(2)}) copy-start(bf16[1024,256]{1,0:T(8,128)(2,1)S(1)} %collective-permute-done.8.refs_7_) | copy-start | bytes 1572868
  17.8 21.9 %collective-permute-start.11 = (bf16[1024,256]{1,0:T(8,128)(2,1)S(1)}, bf16[1024,256]{1,0:T(8,128)(2,1)}, u32[]{:S(2)}, u32[]{:S(2)}) collective-permute-start(bf16[1024,256]{1,0:T(8,128)(2,1)S(1)} %collective-permute-done.8.refs_7_), channel_id=1, source_target_pairs={{0,32},{16,48},{32,64},{48,80},{64,96},{80,112},{96,0},{112,16},{1... | collective-permute-start | bytes 1572872 | tf_op jit(solution)/shard_map/ppermute | solution.py:45
  19.4 22.2 %collective-permute-start.4 = (bf16[1024,256]{1,0:T(8,128)(2,1)S(1)}, bf16[1024,256]{1,0:T(8,128)(2,1)S(1)}, u32[]{:S(2)}, u32[]{:S(2)}) collective-permute-start(bf16[1024,256]{1,0:T(8,128)(2,1)S(1)} %collective-permute-done.2.refs_2_), channel_id=1, source_target_pairs={{0,96},{16,112},{32,0},{48,16},{64,32},{80,48},{96,64},{112,80},{1... | collective-permute-start | bytes 1572872 | tf_op jit(solution)/shard_map/ppermute | solution.py:45
  30.4 12.5 %collective-permute-start.9 = (bf16[1024,256]{1,0:T(8,128)(2,1)S(1)}, bf16[1024,256]{1,0:T(8,128)(2,1)}, u32[]{:S(2)}, u32[]{:S(2)}) collective-permute-start(bf16[1024,256]{1,0:T(8,128)(2,1)S(1)} %collective-permute-done.1.refs_1_), channel_id=1, source_target_pairs={{0,16},{16,0},{32,48},{48,32},{64,80},{80,64},{96,112},{112,96},{1... | collective-permute-start | bytes 1572872 | tf_op jit(solution)/shard_map/ppermute | solution.py:45
  30.6 22.3 %collective-permute-start.3 = (bf16[1024,256]{1,0:T(8,128)(2,1)S(1)}, bf16[1024,256]{1,0:T(8,128)(2,1)S(1)}, u32[]{:S(2)}, u32[]{:S(2)}) collective-permute-start(bf16[1024,256]{1,0:T(8,128)(2,1)S(1)} %collective-permute-done.1.refs_1_), channel_id=1, source_target_pairs={{0,96},{16,112},{32,0},{48,16},{64,32},{80,48},{96,64},{112,80},{1... | collective-permute-start | bytes 1572872 | tf_op jit(solution)/shard_map/ppermute | solution.py:45
  33.8 16.3 %collective-permute-start.7 = (bf16[1024,256]{1,0:T(8,128)(2,1)S(1)}, bf16[1024,256]{1,0:T(8,128)(2,1)S(1)}, u32[]{:S(2)}, u32[]{:S(2)}) collective-permute-start(bf16[1024,256]{1,0:T(8,128)(2,1)S(1)} %collective-permute-done.6.refs_6_), channel_id=1, source_target_pairs={{0,32},{16,48},{32,64},{48,80},{64,96},{80,112},{96,0},{112,16},{1... | collective-permute-start | bytes 1572872 | tf_op jit(solution)/shard_map/ppermute | solution.py:45
  39.7 14.1 %collective-permute-start.5 = (bf16[1024,256]{1,0:T(8,128)(2,1)S(1)}, bf16[1024,256]{1,0:T(8,128)(2,1)}, u32[]{:S(2)}, u32[]{:S(2)}) collective-permute-start(bf16[1024,256]{1,0:T(8,128)(2,1)S(1)} %collective-permute-done.2.refs_2_), channel_id=1, source_target_pairs={{0,16},{16,0},{32,48},{48,32},{64,80},{80,64},{96,112},{112,96},{1... | collective-permute-start | bytes 1572872 | tf_op jit(solution)/shard_map/ppermute | solution.py:45
  41.6 22.0 %collective-permute-start.12 = (bf16[1024,256]{1,0:T(8,128)(2,1)}, bf16[1024,256]{1,0:T(8,128)(2,1)}, u32[]{:S(2)}, u32[]{:S(2)}) collective-permute-start(bf16[1024,256]{1,0:T(8,128)(2,1)} %collective-permute-done.11.refs_13_), channel_id=1, source_target_pairs={{0,32},{16,48},{32,64},{48,80},{64,96},{80,112},{96,0},{112,16},{1... | collective-permute-start | bytes 1572872 | tf_op jit(solution)/shard_map/ppermute | solution.py:45
  42.9 21.2 %collective-permute-start.10 = (bf16[1024,256]{1,0:T(8,128)(2,1)}, bf16[1024,256]{1,0:T(8,128)(2,1)}, u32[]{:S(2)}, u32[]{:S(2)}) collective-permute-start(bf16[1024,256]{1,0:T(8,128)(2,1)} %collective-permute-done.9.refs_8_), channel_id=1, source_target_pairs={{0,96},{16,112},{32,0},{48,16},{64,32},{80,48},{96,64},{112,80},{1... | collective-permute-start | bytes 1572872 | tf_op jit(solution)/shard_map/ppermute | solution.py:45
  50.0 2.8 %copy-start.1 = (bf16[1024,256]{1,0:T(8,128)(2,1)}, bf16[1024,256]{1,0:T(8,128)(2,1)S(1)}, u32[]{:S(2)}) copy-start(bf16[1024,256]{1,0:T(8,128)(2,1)S(1)} %collective-permute-done.7.refs_12_) | copy-start | bytes 1572868
  54.5 18.2 %all-to-all-start = ((s32[16,1,8]{2,1,0:T(1,128)}), s32[16,1,8]{2,1,0:T(1,128)S(1)}, u32[]{:S(2)}, u32[]{:S(2)}) async-start(s32[16,1,8]{2,1,0:T(1,128)} %bitcast.3), calls=%async_computation | async-start | bytes 16384 | tf_op jit(solution)/shard_map/all_to_all | solution.py:71
  181.1 2.1 collective-permute-start.13
  183.2 4.3 %collective-permute-start.15 = (f32[48,128]{1,0:T(8,128)S(1)}, f32[48,128]{1,0:T(8,128)S(1)}, u32[]{:S(2)}, u32[]{:S(2)}) collective-permute-start(f32[48,128]{1,0:T(8,128)S(1)} %get-tuple-element.30), channel_id=1, source_target_pairs={{0,4},{1,5},{2,6},{3,7},{4,0},{5,1},{6,2},{7,3},{16,20},{17,21},{1... | collective-permute-start | bytes 73736 | tf_op jit(solution)/shard_map/ppermute | solution.py:40
  183.6 3.9 %collective-permute-start.16 = (f32[48,128]{1,0:T(8,128)S(1)}, f32[48,128]{1,0:T(8,128)S(1)}, u32[]{:S(2)}, u32[]{:S(2)}) collective-permute-start(f32[48,128]{1,0:T(8,128)S(1)} %get-tuple-element.31), channel_id=1, source_target_pairs={{0,6},{1,7},{2,0},{3,1},{4,2},{5,3},{6,4},{7,5},{16,22},{17,23},{1... | collective-permute-start | bytes 73736 | tf_op jit(solution)/shard_map/ppermute | solution.py:40
  184.5 4.1 %collective-permute-start.14 = (f32[48,128]{1,0:T(8,128)S(1)}, f32[48,128]{1,0:T(8,128)S(1)}, u32[]{:S(2)}, u32[]{:S(2)}) collective-permute-start(f32[48,128]{1,0:T(8,128)S(1)} %get-tuple-element.32), channel_id=1, source_target_pairs={{0,2},{1,3},{2,4},{3,5},{4,6},{5,7},{6,0},{7,1},{16,18},{17,19},{1... | collective-permute-start | bytes 73736 | tf_op jit(solution)/shard_map/ppermute | solution.py:40
  188.6 2.7 %collective-permute-start.19 = (f32[48,128]{1,0:T(8,128)S(1)}, f32[48,128]{1,0:T(8,128)S(1)}, u32[]{:S(2)}, u32[]{:S(2)}) collective-permute-start(f32[48,128]{1,0:T(8,128)S(1)} %fusion), channel_id=1, source_target_pairs={{0,24},{1,25},{2,26},{3,27},{4,28},{5,29},{6,30},{7,31},{16,0},{17... | collective-permute-start | bytes 73736 | tf_op jit(solution)/shard_map/ppermute | solution.py:40
  189.1 4.2 %collective-permute-start.18 = (f32[48,128]{1,0:T(8,128)S(1)}, f32[48,128]{1,0:T(8,128)S(1)}, u32[]{:S(2)}, u32[]{:S(2)}) collective-permute-start(f32[48,128]{1,0:T(8,128)S(1)} %fusion), channel_id=1, source_target_pairs={{0,8},{1,9},{2,10},{3,11},{4,12},{5,13},{6,14},{7,15},{16,24},{17,... | collective-permute-start | bytes 73736 | tf_op jit(solution)/shard_map/ppermute | solution.py:40
  190.3 3.9 %collective-permute-start.17 = (f32[48,128]{1,0:T(8,128)S(1)}, f32[48,128]{1,0:T(8,128)S(1)}, u32[]{:S(2)}, u32[]{:S(2)}) collective-permute-start(f32[48,128]{1,0:T(8,128)S(1)} %fusion), channel_id=1, source_target_pairs={{0,16},{1,17},{2,18},{3,19},{4,20},{5,21},{6,22},{7,23},{16,8},{17... | collective-permute-start | bytes 73736 | tf_op jit(solution)/shard_map/ppermute | solution.py:40
  194.2 4.2 %collective-permute-start.22 = (f32[48,128]{1,0:T(8,128)S(1)}, f32[48,128]{1,0:T(8,128)S(1)}, u32[]{:S(2)}, u32[]{:S(2)}) collective-permute-start(f32[48,128]{1,0:T(8,128)S(1)} %add_add_fusion.1), channel_id=1, source_target_pairs={{0,96},{1,97},{2,98},{3,99},{4,100},{5,101},{6,102},{7,103},{16,11... | collective-permute-start | bytes 73736 | tf_op jit(solution)/shard_map/ppermute | solution.py:40
  197.5 4.2 %collective-permute-start.21 = (f32[48,128]{1,0:T(8,128)S(1)}, f32[48,128]{1,0:T(8,128)S(1)}, u32[]{:S(2)}, u32[]{:S(2)}) collective-permute-start(f32[48,128]{1,0:T(8,128)S(1)} %add_add_fusion.1), channel_id=1, source_target_pairs={{0,64},{1,65},{2,66},{3,67},{4,68},{5,69},{6,70},{7,71},{16,80},{1... | collective-permute-start | bytes 73736 | tf_op jit(solution)/shard_map/ppermute | solution.py:40
  197.6 4.2 %collective-permute-start.20 = (f32[48,128]{1,0:T(8,128)S(1)}, f32[48,128]{1,0:T(8,128)S(1)}, u32[]{:S(2)}, u32[]{:S(2)}) collective-permute-start(f32[48,128]{1,0:T(8,128)S(1)} %add_add_fusion.1), channel_id=1, source_target_pairs={{0,32},{1,33},{2,34},{3,35},{4,36},{5,37},{6,38},{7,39},{16,48},{1... | collective-permute-start | bytes 73736 | tf_op jit(solution)/shard_map/ppermute | solution.py:40
  201.7 4.3 %collective-permute-start.25 = (f32[48,128]{1,0:T(8,128)S(1)}, f32[48,128]{1,0:T(8,128)S(1)}, u32[]{:S(2)}, u32[]{:S(2)}) collective-permute-start(f32[48,128]{1,0:T(8,128)S(1)} %add_add_fusion), channel_id=1, source_target_pairs={{0,2},{1,3},{2,4},{3,5},{4,6},{5,7},{6,0},{7,1},{16,18},{17,19},{1... | collective-permute-start | bytes 73736 | tf_op jit(solution)/shard_map/ppermute | solution.py:40
  201.8 4.3 %collective-permute-start.24 = (f32[48,128]{1,0:T(8,128)S(1)}, f32[48,128]{1,0:T(8,128)S(1)}, u32[]{:S(2)}, u32[]{:S(2)}) collective-permute-start(f32[48,128]{1,0:T(8,128)S(1)} %add_add_fusion), channel_id=1, source_target_pairs={{0,4},{1,5},{2,6},{3,7},{4,0},{5,1},{6,2},{7,3},{16,20},{17,21},{1... | collective-permute-start | bytes 73736 | tf_op jit(solution)/shard_map/ppermute | solution.py:40
  203.9 2.7 %collective-permute-start.23 = (f32[48,128]{1,0:T(8,128)S(1)}, f32[48,128]{1,0:T(8,128)S(1)}, u32[]{:S(2)}, u32[]{:S(2)}) collective-permute-start(f32[48,128]{1,0:T(8,128)S(1)} %add_add_fusion), channel_id=1, source_target_pairs={{0,6},{1,7},{2,0},{3,1},{4,2},{5,3},{6,4},{7,5},{16,22},{17,23},{1... | collective-permute-start | bytes 73736 | tf_op jit(solution)/shard_map/ppermute | solution.py:40
  206.6 7.9 %collective-permute-start.26 = (f32[4,48,128]{2,1,0:T(8,128)S(1)}, f32[4,48,128]{2,1,0:T(8,128)S(1)}, u32[]{:S(2)}, u32[]{:S(2)}) collective-permute-start(f32[4,48,128]{2,1,0:T(8,128)S(1)} %pad_maximum_fusion.mine), channel_id=1, source_target_pairs={{0,1},{1,0},{2,3},{3,2},{4,5},{5,4},{6,7},{7,6},{16,17},{17,16},{1... | collective-permute-start | bytes 294920 | tf_op jit(solution)/shard_map/ppermute | solution.py:40

commit v6 on v5

--- a/solution.py
+++ b/solution.py
@@ -19,7 +19,7 @@
 LATE = (10, 11, 13, 8, 4, 0)
 PANEL = 32
 SUB = 16
-PIECE = 48
+PIECE = 192
 CHUNKS = 8
 OUT_CHUNKS = 8
 
@@ -162,8 +162,8 @@
     packed[:BLOCK, :] = total[:BLOCK, :BLOCK]
     packed[BLOCK : 2 * BLOCK, :] = total[:BLOCK, BLOCK:]
     packed[2 * BLOCK :, :] = total[BLOCK:, BLOCK:]
-    for i, order in enumerate(piece_order(me)):
-        gram[order] = packed[i * PIECE : (i + 1) * PIECE, :]
+    for i in range(2):
+        gram[i ^ me[0]] = packed[i * PIECE : (i + 1) * PIECE, :]
     store.wait()
 
 
@@ -172,7 +172,7 @@
         sum_kernel,
         out_shape=(
             jax.ShapeDtypeStruct((ROWS_DEV, BASIS), jnp.float32),
-            jax.ShapeDtypeStruct((8, PIECE, BLOCK), jnp.float32),
+            jax.ShapeDtypeStruct((2, PIECE, BLOCK), jnp.float32),
         ),
         in_specs=[pl.BlockSpec(memory_space=pltpu.SMEM)] * 2
         + [pl.BlockSpec(memory_space=pltpu.VMEM)],
@@ -188,32 +188,18 @@
 
 
 def reduce_everywhere(gram):
-    part = gram[:4] + shifted(gram[4:], dcore=1)
-    part = part[0] + sum(shifted(part[d], dx=d) for d in (1, 2, 3))
-    part = part + sum(shifted(part, dy=d) for d in (1, 2, 3))
-    part = part + sum(shifted(part, dz=d) for d in (1, 2, 3))
-    mine = jnp.stack([part] + [shifted(part, dx=-d) for d in (1, 2, 3)])
+    mine = gram[0] + shifted(gram[1], dcore=1)
+    mine = mine + sum(shifted(mine, dx=d) for d in (1, 2, 3))
+    mine = mine + sum(shifted(mine, dy=d) for d in (1, 2, 3))
+    mine = mine + sum(shifted(mine, dz=d) for d in (1, 2, 3))
     return mine, shifted(mine, dcore=1)
-
-
-def piece_order(me):
-    return [((i // 4) ^ me[0]) * 4 + ((i % 4 - me[1]) & 3) for i in range(8)]
 
 
 def finish_kernel(me, mine, other, summed_hbm, ortho_hbm, factor, gram, work, summed, ortho, in_sem, out_sems):
     load = pltpu.make_async_copy(summed_hbm, summed, in_sem)
     load.start()
-    for i, order in enumerate(piece_order(me)):
-        here = pl.ds(i * PIECE, PIECE)
-
-        @pl.when(order < 4)
-        def _():
-            gram[here, :] = mine[order & 3]
-
-        @pl.when(order >= 4)
-        def _():
-            gram[here, :] = other[order & 3]
-
+    gram[pl.ds(pl.multiple_of(me[0] * PIECE, 8), PIECE), :] = mine[...]
+    gram[pl.ds(pl.multiple_of((1 - me[0]) * PIECE, 8), PIECE), :] = other[...]
     row_id = lax.broadcasted_iota(jnp.int32, (BASIS, BASIS), 0)
     col_id = lax.broadcasted_iota(jnp.int32, (BASIS, BASIS), 1)
     work[:BLOCK, :BLOCK] = gram[:BLOCK, :] * (1.0 / ITEMS)

time: 224 us -> 223 us (level)
  starting transfers between devices: 47.9 us -> 40.5 us
  waiting for transfers between devices: 44.7 us -> 50.5 us
    ppermute x14 -> x11, starting transfers between devices: 18.8 us -> 11.4 us  [shifted(): return lax.ppermute(value, BOTH, pairs)]
    ppermute x14 -> x11, waiting for transfers between devices: 14.5 us -> 20.4 us  [shifted(): return lax.ppermute(value, BOTH, pairs)]
  transfers between devices with their start and end apart: 28 -> 25, of which waited for: 20 -> 19; matrix products, arithmetic and copies ran while one was open for 2% -> 2% of each run, Pallas kernels for 4% -> 4%
where the time goes in v6:
time: 223 us
  blocking collectives  104 us (47%)
  waiting for transfers between devices  50.5 us (23%)
  starting transfers between devices  40.5 us (18%)
  Pallas kernels  22.2 us (10%)
  local copies, waits for them, and re-layouts  2.76 us (1%)
    all_to_all x1, blocking collectives, local(): lax.all_to_all(products.reshape(N_COL, PER_PEER * BLOCK, BASIS), 'col', 0...  104 us
    ppermute x13, waiting for transfers between devices, row_shifted(): return lax.ppermute(value, 'row', pairs)  30.2 us
    ppermute x11, waiting for transfers between devices, shifted(): return lax.ppermute(value, BOTH, pairs)  20.4 us
    ppermute x13, starting transfers between devices, row_shifted(): return lax.ppermute(value, 'row', pairs)  20 us
    ppermute x11, starting transfers between devices, shifted(): return lax.ppermute(value, BOTH, pairs)  11.4 us
    pallas_call x1, Pallas kernels, finish(): pl.pallas_call(finish_kernel, out_shape=(jax.ShapeDtypeStruct((ROWS_DEV,...  9.5 us
    all_to_all x1, starting transfers between devices, gather_column(): lax.all_to_all(place.reshape(N_COL, 1, PER_PEER), 'col', 0, 0, tiled=True)  9.15 us
    pallas_call x1, Pallas kernels, make_products(): pl.pallas_call(product_kernel, out_shape=jax.ShapeDtypeStruct((TILE_DEV *...  8.6 us
  transfers between devices with their start and end apart: 25, of which 19 were waited for; matrix products, arithmetic and copies ran while one was open for 2% of the time, Pallas kernels for 4%

profile of v6, /device:TPU:1, one launch (start us, length us, event | category | flops | bytes accessed | tf_op | source)
XLA Modules:
  0.0 222.6 jit_solution(7930655622651402673)
XLA Ops:
  0.6 2.5 %collective-permute-start = (bf16[2048,256]{1,0:T(8,128)(2,1)}, bf16[2048,256]{1,0:T(8,128)(2,1)}, u32[]{:S(2)}, u32[]{:S(2)}) collective-permute-start(bf16[2048,256]{1,0:T(8,128)(2,1)} %refs_0_.1), channel_id=1, source_target_pairs={{0,32},{16,48},{32,64},{48,80},{64,96},{80,112},{96,0},{112,16},{1... | collective-permute-start | bytes 3145736 | tf_op jit(solution)/shard_map/ppermute | solution.py:45
  3.2 2.1 fusion
  5.2 1.3 collective-permute-start.8
  6.5 2.1 collective-permute-start.2
  8.7 1.4 collective-permute-start.1
  10.3 7.5 %collective-permute-done.8.refs_7_ = bf16[1024,256]{1,0:T(8,128)(2,1)S(1)} collective-permute-done((bf16[1024,256]{1,0:T(8,128)(2,1)S(1)}, bf16[1024,256]{1,0:T(8,128)(2,1)S(1)}, u32[]{:S(2)}, u32[]{:S(2)}) %collective-permute-start.8) | collective-permute-done | bytes 524320 | tf_op jit(solution)/shard_map/ppermute | solution.py:45
  17.8 1.6 collective-permute-start.11
  19.4 2.9 %collective-permute-start.4 = (bf16[1024,256]{1,0:T(8,128)(2,1)S(1)}, bf16[1024,256]{1,0:T(8,128)(2,1)S(1)}, u32[]{:S(2)}, u32[]{:S(2)}) collective-permute-start(bf16[1024,256]{1,0:T(8,128)(2,1)S(1)} %collective-permute-done.2.refs_2_), channel_id=1, source_target_pairs={{0,96},{16,112},{32,0},{48,16},{64,32},{80,48},{96,64},{112,80},{1... | collective-permute-start | bytes 1572872 | tf_op jit(solution)/shard_map/ppermute | solution.py:45
  22.3 8.0 %collective-permute-done.1.refs_1_ = bf16[1024,256]{1,0:T(8,128)(2,1)S(1)} collective-permute-done((bf16[1024,256]{1,0:T(8,128)(2,1)}, bf16[1024,256]{1,0:T(8,128)(2,1)S(1)}, u32[]{:S(2)}, u32[]{:S(2)}) %collective-permute-start.1) | collective-permute-done | bytes 524320 | tf_op jit(solution)/shard_map/ppermute | solution.py:45
  30.6 3.2 %collective-permute-start.3 = (bf16[1024,256]{1,0:T(8,128)(2,1)S(1)}, bf16[1024,256]{1,0:T(8,128)(2,1)S(1)}, u32[]{:S(2)}, u32[]{:S(2)}) collective-permute-start(bf16[1024,256]{1,0:T(8,128)(2,1)S(1)} %collective-permute-done.1.refs_1_), channel_id=1, source_target_pairs={{0,96},{16,112},{32,0},{48,16},{64,32},{80,48},{96,64},{112,80},{1... | collective-permute-start | bytes 1572872 | tf_op jit(solution)/shard_map/ppermute | solution.py:45
  33.8 6.0 %collective-permute-done.11.refs_13_ = bf16[1024,256]{1,0:T(8,128)(2,1)} collective-permute-done((bf16[1024,256]{1,0:T(8,128)(2,1)S(1)}, bf16[1024,256]{1,0:T(8,128)(2,1)}, u32[]{:S(2)}, u32[]{:S(2)}) %collective-permute-start.11) | collective-permute-done | bytes 524320 | tf_op jit(solution)/shard_map/ppermute | solution.py:45
  39.7 1.3 collective-permute-start.5
  41.6 1.3 collective-permute-start.12
  42.9 1.9 collective-permute-start.10
  46.2 3.8 %collective-permute-done.7.refs_12_ = bf16[1024,256]{1,0:T(8,128)(2,1)S(1)} collective-permute-done((bf16[1024,256]{1,0:T(8,128)(2,1)S(1)}, bf16[1024,256]{1,0:T(8,128)(2,1)S(1)}, u32[]{:S(2)}, u32[]{:S(2)}) %collective-permute-start.7) | collective-permute-done | bytes 524320 | tf_op jit(solution)/shard_map/ppermute | solution.py:45
  50.0 2.8 %collective-permute-done.3.refs_3_ = bf16[1024,256]{1,0:T(8,128)(2,1)S(1)} collective-permute-done((bf16[1024,256]{1,0:T(8,128)(2,1)S(1)}, bf16[1024,256]{1,0:T(8,128)(2,1)S(1)}, u32[]{:S(2)}, u32[]{:S(2)}) %collective-permute-start.3) | collective-permute-done | bytes 524320 | tf_op jit(solution)/shard_map/ppermute | solution.py:45
  54.5 9.1 %all-to-all-start = ((s32[16,1,8]{2,1,0:T(1,128)}), s32[16,1,8]{2,1,0:T(1,128)S(1)}, u32[]{:S(2)}, u32[]{:S(2)}) async-start(s32[16,1,8]{2,1,0:T(1,128)} %bitcast.3), calls=%async_computation | async-start | bytes 16384 | tf_op jit(solution)/shard_map/all_to_all | solution.py:71
  64.1 8.6 %products.1 = bf16[16384,256]{1,0:T(8,128)(2,1)} custom-call(s32[128]{0:T(128)S(1)} %add_bitcast_fusion.src, bf16[128,128,128]{2,1,0:T(8,128)(2,1)} %bitcast.16, bf16[2048,256]{1,0:T(8,128)(2,1)} %refs_0_.1, bf16[1024,256]{1,0:T(8,128)(2,1)S(1)} %collective-permute-done.1.refs_1_, bf16[1024,256]{1,0:T(8,128)(2,1)S(1)} %collective-permute-done.2.refs_2_, ...), custom_call_target="tpu_custom_call" | custom-call | tf_op jit(solution)/shard_map/products/pallas_call | solution.py:122
  72.7 104.3 %all_to_all.10 = bf16[16,1024,256]{2,1,0:T(8,128)(2,1)S(1)} all-to-all(bf16[16,1024,256]{2,1,0:T(8,128)(2,1)} %bitcast.15), channel_id=1, replica_groups=mesh['row'=8,'col'=16] {'col'}, dimensions={0} | all-to-all | bytes 16777216 | tf_op jit(solution)/shard_map/all_to_all | solution.py:320
  177.0 4.1 %sum_and_gram.1 = (f32[2048,256]{1,0:T(8,128)S(1)}, f32[2,192,128]{2,1,0:T(8,128)S(1)}) custom-call(s32[16,1,8]{2,1,0:T(1,128)S(1)} %all-to-all-done.place, s32[2]{0:T(128)S(1)} %pad_add_fusion.me, bf16[16384,256]{1,0:T(8,128)(2,1)S(1)} %bitcast.14), custom_call_target="tpu_custom_call" | custom-call | tf_op jit(solution)/shard_map/sum_and_gram/pallas_call | solution.py:171
  184.8 2.6 %collective-permute-done.16 = f32[192,128]{1,0:T(8,128)S(1)} collective-permute-done((f32[192,128]{1,0:T(8,128)S(1)}, f32[192,128]{1,0:T(8,128)S(1)}, u32[]{:S(2)}, u32[]{:S(2)}) %collective-permute-start.16) | collective-permute-done | bytes 98336 | tf_op jit(solution)/shard_map/ppermute | solution.py:40
  187.3 1.9 collective-permute-done.15
  189.2 2.9 %collective-permute-done.14 = f32[192,128]{1,0:T(8,128)S(1)} collective-permute-done((f32[192,128]{1,0:T(8,128)S(1)}, f32[192,128]{1,0:T(8,128)S(1)}, u32[]{:S(2)}, u32[]{:S(2)}) %collective-permute-start.14) | collective-permute-done | bytes 98336 | tf_op jit(solution)/shard_map/ppermute | solution.py:40
  192.2 1.6 collective-permute-start.18
  193.9 2.2 collective-permute-done.19
  196.1 1.6 collective-permute-done.18
  197.7 2.3 %collective-permute-done.17 = f32[192,128]{1,0:T(8,128)S(1)} collective-permute-done((f32[192,128]{1,0:T(8,128)S(1)}, f32[192,128]{1,0:T(8,128)S(1)}, u32[]{:S(2)}, u32[]{:S(2)}) %collective-permute-start.17) | collective-permute-done | bytes 98336 | tf_op jit(solution)/shard_map/ppermute | solution.py:40
  200.0 3.2 %collective-permute-start.22 = (f32[192,128]{1,0:T(8,128)S(1)}, f32[192,128]{1,0:T(8,128)S(1)}, u32[]{:S(2)}, u32[]{:S(2)}) collective-permute-start(f32[192,128]{1,0:T(8,128)S(1)} %add_add_fusion.1), channel_id=1, source_target_pairs={{0,96},{1,97},{2,98},{3,99},{4,100},{5,101},{6,102},{7,103},{16,11... | collective-permute-start | bytes 294920 | tf_op jit(solution)/shard_map/ppermute | solution.py:40
  204.1 1.9 collective-permute-done.22
  206.0 2.3 %collective-permute-done.21 = f32[192,128]{1,0:T(8,128)S(1)} collective-permute-done((f32[192,128]{1,0:T(8,128)S(1)}, f32[192,128]{1,0:T(8,128)S(1)}, u32[]{:S(2)}, u32[]{:S(2)}) %collective-permute-start.21) | collective-permute-done | bytes 98336 | tf_op jit(solution)/shard_map/ppermute | solution.py:40
  209.1 2.9 %collective-permute-start.23 = (f32[192,128]{1,0:T(8,128)S(1)}, f32[192,128]{1,0:T(8,128)S(1)}, u32[]{:S(2)}, u32[]{:S(2)}) collective-permute-start(f32[192,128]{1,0:T(8,128)S(1)} %add_add_fusion.mine), channel_id=1, source_target_pairs={{0,1},{1,0},{2,3},{3,2},{4,5},{5,4},{6,7},{7,6},{16,17},{17,16},{1... | collective-permute-start | bytes 294920 | tf_op jit(solution)/shard_map/ppermute | solution.py:40
  213.0 9.5 %finish.1 = (f32[2048,256]{1,0:T(8,128)}, f32[256,256]{1,0:T(8,128)}) custom-call(s32[2]{0:T(128)S(1)} %pad_add_fusion.me, f32[192,128]{1,0:T(8,128)S(1)} %add_add_fusion.mine, f32[192,128]{1,0:T(8,128)S(1)} %collective-permute-done.23.other, f32[2048,256]{1,0:T(8,128)S(1)} %get-tuple-element.27.summed_hbm), custom_call_target="tpu_custom_call" | custom-call | tf_op jit(solution)/shard_map/finish/pallas_call | solution.py:282
  (36 shorter events, 10.7 us)
Async XLA Ops:
  0.6 29.8 %collective-permute-start = (bf16[2048,256]{1,0:T(8,128)(2,1)}, bf16[2048,256]{1,0:T(8,128)(2,1)}, u32[]{:S(2)}, u32[]{:S(2)}) collective-permute-start(bf16[2048,256]{1,0:T(8,128)(2,1)} %refs_0_.1), channel_id=1, source_target_pairs={{0,32},{16,48},{32,64},{48,80},{64,96},{80,112},{96,0},{112,16},{1... | collective-permute-start | bytes 3145736 | tf_op jit(solution)/shard_map/ppermute | solution.py:45
  5.2 12.6 %collective-permute-start.8 = (bf16[1024,256]{1,0:T(8,128)(2,1)S(1)}, bf16[1024,256]{1,0:T(8,128)(2,1)S(1)}, u32[]{:S(2)}, u32[]{:S(2)}) collective-permute-start(bf16[1024,256]{1,0:T(8,128)(2,1)S(1)} %get-tuple-element.28), channel_id=1, source_target_pairs={{0,16},{16,0},{32,48},{48,32},{64,80},{80,64},{96,112},{112,96},{1... | collective-permute-start | bytes 1572872 | tf_op jit(solution)/shard_map/ppermute | solution.py:45
  6.5 12.9 %collective-permute-start.2 = (bf16[1024,256]{1,0:T(8,128)(2,1)S(1)}, bf16[1024,256]{1,0:T(8,128)(2,1)S(1)}, u32[]{:S(2)}, u32[]{:S(2)}) collective-permute-start(bf16[1024,256]{1,0:T(8,128)(2,1)S(1)} %get-tuple-element.28), channel_id=1, source_target_pairs={{0,96},{16,112},{32,0},{48,16},{64,32},{80,48},{96,64},{112,80},{1... | collective-permute-start | bytes 1572872 | tf_op jit(solution)/shard_map/ppermute | solution.py:45
  8.7 21.7 %collective-permute-start.1 = (bf16[1024,256]{1,0:T(8,128)(2,1)}, bf16[1024,256]{1,0:T(8,128)(2,1)S(1)}, u32[]{:S(2)}, u32[]{:S(2)}) collective-permute-start(bf16[1024,256]{1,0:T(8,128)(2,1)} %get-tuple-element.29), channel_id=1, source_target_pairs={{0,96},{16,112},{32,0},{48,16},{64,32},{80,48},{96,64},{112,80},{1... | collective-permute-start | bytes 1572872 | tf_op jit(solution)/shard_map/ppermute | solution.py:45
  10.1 23.6 %collective-permute-start.6 = (bf16[1024,256]{1,0:T(8,128)(2,1)}, bf16[1024,256]{1,0:T(8,128)(2,1)S(1)}, u32[]{:S(2)}, u32[]{:S(2)}) collective-permute-start(bf16[1024,256]{1,0:T(8,128)(2,1)} %get-tuple-element.29), channel_id=1, source_target_pairs={{0,16},{16,0},{32,48},{48,32},{64,80},{80,64},{96,112},{112,96},{1... | collective-permute-start | bytes 1572872 | tf_op jit(solution)/shard_map/ppermute | solution.py:45
  17.8 46.3 %copy-start = (bf16[1024,256]{1,0:T(8,128)(2,1)}, bf16[1024,256]{1,0:T(8,128)(2,1)S(1)}, u32[]{:S(2)}) copy-start(bf16[1024,256]{1,0:T(8,128)(2,1)S(1)} %collective-permute-done.8.refs_7_) | copy-start | bytes 1572868
  17.8 21.9 %collective-permute-start.11 = (bf16[1024,256]{1,0:T(8,128)(2,1)S(1)}, bf16[1024,256]{1,0:T(8,128)(2,1)}, u32[]{:S(2)}, u32[]{:S(2)}) collective-permute-start(bf16[1024,256]{1,0:T(8,128)(2,1)S(1)} %collective-permute-done.8.refs_7_), channel_id=1, source_target_pairs={{0,32},{16,48},{32,64},{48,80},{64,96},{80,112},{96,0},{112,16},{1... | collective-permute-start | bytes 1572872 | tf_op jit(solution)/shard_map/ppermute | solution.py:45
  19.4 22.2 %collective-permute-start.4 = (bf16[1024,256]{1,0:T(8,128)(2,1)S(1)}, bf16[1024,256]{1,0:T(8,128)(2,1)S(1)}, u32[]{:S(2)}, u32[]{:S(2)}) collective-permute-start(bf16[1024,256]{1,0:T(8,128)(2,1)S(1)} %collective-permute-done.2.refs_2_), channel_id=1, source_target_pairs={{0,96},{16,112},{32,0},{48,16},{64,32},{80,48},{96,64},{112,80},{1... | collective-permute-start | bytes 1572872 | tf_op jit(solution)/shard_map/ppermute | solution.py:45
  30.4 12.5 %collective-permute-start.9 = (bf16[1024,256]{1,0:T(8,128)(2,1)S(1)}, bf16[1024,256]{1,0:T(8,128)(2,1)}, u32[]{:S(2)}, u32[]{:S(2)}) collective-permute-start(bf16[1024,256]{1,0:T(8,128)(2,1)S(1)} %collective-permute-done.1.refs_1_), channel_id=1, source_target_pairs={{0,16},{16,0},{32,48},{48,32},{64,80},{80,64},{96,112},{112,96},{1... | collective-permute-start | bytes 1572872 | tf_op jit(solution)/shard_map/ppermute | solution.py:45
  30.6 22.3 %collective-permute-start.3 = (bf16[1024,256]{1,0:T(8,128)(2,1)S(1)}, bf16[1024,256]{1,0:T(8,128)(2,1)S(1)}, u32[]{:S(2)}, u32[]{:S(2)}) collective-permute-start(bf16[1024,256]{1,0:T(8,128)(2,1)S(1)} %collective-permute-done.1.refs_1_), channel_id=1, source_target_pairs={{0,96},{16,112},{32,0},{48,16},{64,32},{80,48},{96,64},{112,80},{1... | collective-permute-start | bytes 1572872 | tf_op jit(solution)/shard_map/ppermute | solution.py:45
  33.8 16.3 %collective-permute-start.7 = (bf16[1024,256]{1,0:T(8,128)(2,1)S(1)}, bf16[1024,256]{1,0:T(8,128)(2,1)S(1)}, u32[]{:S(2)}, u32[]{:S(2)}) collective-permute-start(bf16[1024,256]{1,0:T(8,128)(2,1)S(1)} %collective-permute-done.6.refs_6_), channel_id=1, source_target_pairs={{0,32},{16,48},{32,64},{48,80},{64,96},{80,112},{96,0},{112,16},{1... | collective-permute-start | bytes 1572872 | tf_op jit(solution)/shard_map/ppermute | solution.py:45
  39.7 14.1 %collective-permute-start.5 = (bf16[1024,256]{1,0:T(8,128)(2,1)S(1)}, bf16[1024,256]{1,0:T(8,128)(2,1)}, u32[]{:S(2)}, u32[]{:S(2)}) collective-permute-start(bf16[1024,256]{1,0:T(8,128)(2,1)S(1)} %collective-permute-done.2.refs_2_), channel_id=1, source_target_pairs={{0,16},{16,0},{32,48},{48,32},{64,80},{80,64},{96,112},{112,96},{1... | collective-permute-start | bytes 1572872 | tf_op jit(solution)/shard_map/ppermute | solution.py:45
  41.6 22.0 %collective-permute-start.12 = (bf16[1024,256]{1,0:T(8,128)(2,1)}, bf16[1024,256]{1,0:T(8,128)(2,1)}, u32[]{:S(2)}, u32[]{:S(2)}) collective-permute-start(bf16[1024,256]{1,0:T(8,128)(2,1)} %collective-permute-done.11.refs_13_), channel_id=1, source_target_pairs={{0,32},{16,48},{32,64},{48,80},{64,96},{80,112},{96,0},{112,16},{1... | collective-permute-start | bytes 1572872 | tf_op jit(solution)/shard_map/ppermute | solution.py:45
  42.9 21.2 %collective-permute-start.10 = (bf16[1024,256]{1,0:T(8,128)(2,1)}, bf16[1024,256]{1,0:T(8,128)(2,1)}, u32[]{:S(2)}, u32[]{:S(2)}) collective-permute-start(bf16[1024,256]{1,0:T(8,128)(2,1)} %collective-permute-done.9.refs_8_), channel_id=1, source_target_pairs={{0,96},{16,112},{32,0},{48,16},{64,32},{80,48},{96,64},{112,80},{1... | collective-permute-start | bytes 1572872 | tf_op jit(solution)/shard_map/ppermute | solution.py:45
  50.0 2.8 %copy-start.1 = (bf16[1024,256]{1,0:T(8,128)(2,1)}, bf16[1024,256]{1,0:T(8,128)(2,1)S(1)}, u32[]{:S(2)}) copy-start(bf16[1024,256]{1,0:T(8,128)(2,1)S(1)} %collective-permute-done.7.refs_12_) | copy-start | bytes 1572868
  54.5 18.2 %all-to-all-start = ((s32[16,1,8]{2,1,0:T(1,128)}), s32[16,1,8]{2,1,0:T(1,128)S(1)}, u32[]{:S(2)}, u32[]{:S(2)}) async-start(s32[16,1,8]{2,1,0:T(1,128)} %bitcast.3), calls=%async_computation | async-start | bytes 16384 | tf_op jit(solution)/shard_map/all_to_all | solution.py:71
  181.1 2.1 collective-permute-start.13
  183.2 4.1 %collective-permute-start.16 = (f32[192,128]{1,0:T(8,128)S(1)}, f32[192,128]{1,0:T(8,128)S(1)}, u32[]{:S(2)}, u32[]{:S(2)}) collective-permute-start(f32[192,128]{1,0:T(8,128)S(1)} %bitcast_add_fusion), channel_id=1, source_target_pairs={{0,6},{1,7},{2,0},{3,1},{4,2},{5,3},{6,4},{7,5},{16,22},{17,23},{1... | collective-permute-start | bytes 294920 | tf_op jit(solution)/shard_map/ppermute | solution.py:40
  183.8 5.4 %collective-permute-start.15 = (f32[192,128]{1,0:T(8,128)S(1)}, f32[192,128]{1,0:T(8,128)S(1)}, u32[]{:S(2)}, u32[]{:S(2)}) collective-permute-start(f32[192,128]{1,0:T(8,128)S(1)} %bitcast_add_fusion), channel_id=1, source_target_pairs={{0,4},{1,5},{2,6},{3,7},{4,0},{5,1},{6,2},{7,3},{16,20},{17,21},{1... | collective-permute-start | bytes 294920 | tf_op jit(solution)/shard_map/ppermute | solution.py:40
  183.9 8.2 %collective-permute-start.14 = (f32[192,128]{1,0:T(8,128)S(1)}, f32[192,128]{1,0:T(8,128)S(1)}, u32[]{:S(2)}, u32[]{:S(2)}) collective-permute-start(f32[192,128]{1,0:T(8,128)S(1)} %bitcast_add_fusion), channel_id=1, source_target_pairs={{0,2},{1,3},{2,4},{3,5},{4,6},{5,7},{6,0},{7,1},{16,18},{17,19},{1... | collective-permute-start | bytes 294920 | tf_op jit(solution)/shard_map/ppermute | solution.py:40
  192.1 3.9 %collective-permute-start.19 = (f32[192,128]{1,0:T(8,128)S(1)}, f32[192,128]{1,0:T(8,128)S(1)}, u32[]{:S(2)}, u32[]{:S(2)}) collective-permute-start(f32[192,128]{1,0:T(8,128)S(1)} %add_add_fusion.2), channel_id=1, source_target_pairs={{0,24},{1,25},{2,26},{3,27},{4,28},{5,29},{6,30},{7,31},{16,0},{17... | collective-permute-start | bytes 294920 | tf_op jit(solution)/shard_map/ppermute | solution.py:40
  192.2 5.5 %collective-permute-start.18 = (f32[192,128]{1,0:T(8,128)S(1)}, f32[192,128]{1,0:T(8,128)S(1)}, u32[]{:S(2)}, u32[]{:S(2)}) collective-permute-start(f32[192,128]{1,0:T(8,128)S(1)} %add_add_fusion.2), channel_id=1, source_target_pairs={{0,8},{1,9},{2,10},{3,11},{4,12},{5,13},{6,14},{7,15},{16,24},{17,... | collective-permute-start | bytes 294920 | tf_op jit(solution)/shard_map/ppermute | solution.py:40
  193.9 6.1 %collective-permute-start.17 = (f32[192,128]{1,0:T(8,128)S(1)}, f32[192,128]{1,0:T(8,128)S(1)}, u32[]{:S(2)}, u32[]{:S(2)}) collective-permute-start(f32[192,128]{1,0:T(8,128)S(1)} %add_add_fusion.2), channel_id=1, source_target_pairs={{0,16},{1,17},{2,18},{3,19},{4,20},{5,21},{6,22},{7,23},{16,8},{17... | collective-permute-start | bytes 294920 | tf_op jit(solution)/shard_map/ppermute | solution.py:40
  200.0 6.0 %collective-permute-start.22 = (f32[192,128]{1,0:T(8,128)S(1)}, f32[192,128]{1,0:T(8,128)S(1)}, u32[]{:S(2)}, u32[]{:S(2)}) collective-permute-start(f32[192,128]{1,0:T(8,128)S(1)} %add_add_fusion.1), channel_id=1, source_target_pairs={{0,96},{1,97},{2,98},{3,99},{4,100},{5,101},{6,102},{7,103},{16,11... | collective-permute-start | bytes 294920 | tf_op jit(solution)/shard_map/ppermute | solution.py:40
  203.3 5.1 %collective-permute-start.21 = (f32[192,128]{1,0:T(8,128)S(1)}, f32[192,128]{1,0:T(8,128)S(1)}, u32[]{:S(2)}, u32[]{:S(2)}) collective-permute-start(f32[192,128]{1,0:T(8,128)S(1)} %add_add_fusion.1), channel_id=1, source_target_pairs={{0,64},{1,65},{2,66},{3,67},{4,68},{5,69},{6,70},{7,71},{16,80},{1... | collective-permute-start | bytes 294920 | tf_op jit(solution)/shard_map/ppermute | solution.py:40
  203.3 5.7 %collective-permute-start.20 = (f32[192,128]{1,0:T(8,128)S(1)}, f32[192,128]{1,0:T(8,128)S(1)}, u32[]{:S(2)}, u32[]{:S(2)}) collective-permute-start(f32[192,128]{1,0:T(8,128)S(1)} %add_add_fusion.1), channel_id=1, source_target_pairs={{0,32},{1,33},{2,34},{3,35},{4,36},{5,37},{6,38},{7,39},{16,48},{1... | collective-permute-start | bytes 294920 | tf_op jit(solution)/shard_map/ppermute | solution.py:40
  209.1 3.9 %collective-permute-start.23 = (f32[192,128]{1,0:T(8,128)S(1)}, f32[192,128]{1,0:T(8,128)S(1)}, u32[]{:S(2)}, u32[]{:S(2)}) collective-permute-start(f32[192,128]{1,0:T(8,128)S(1)} %add_add_fusion.mine), channel_id=1, source_target_pairs={{0,1},{1,0},{2,3},{3,2},{4,5},{5,4},{6,7},{7,6},{16,17},{17,16},{1... | collective-permute-start | bytes 294920 | tf_op jit(solution)/shard_map/ppermute | solution.py:40
